TPU v7x, 32 devices: a whole 2x2x4 slice. The times are simulated.
32 devices in a mesh: grp: 1, row: 4 (over z), col: 4 (over y, x), layer: 2 (over core).
Axes of the slice: x: 2, y: 2, z: 4, core: 2. Of those that a mesh axis runs over, the one named last changes fastest.
Arguments:
- a_blocks: bfloat16 [4, 2, 4, 6, 128, 128], P(('grp', 'row'), 'layer', 'col'), may hold values from -6 to 6
- a_rows: int32 [4, 2, 4, 6], P(('grp', 'row'), 'layer', 'col'), may hold values from 0 to 15, all different within a row
- b_blocks: bfloat16 [4, 2, 128, 1024], P(('grp', 'col'), 'layer', None, 'row'), may hold values from -0.5 to 0.5
- b_occupied: int32 [4, 2, 8], P(('grp', 'col'), 'layer', 'row'), may hold values 0 or 1
- keep: int32 [64, 8], P(('grp', 'col'), 'row'), may hold values 0 or 1
- owner_rows: int32 [4, 2, 8], P(('grp', 'col')), may hold values from 0 to 7, each once within a row
Outputs:
- owned: bfloat16 [8, 8, 128, 1024], P(('grp', 'col', 'layer'), None, None, 'row')
Inputs may be any that keep to these rules, and one draw needn't show every extreme that they name: `a_rows`: the 6 numbers of one list are different. `owner_rows`: each list over the last dimension names every number once.
All inputs are finite; a program needn't handle non-finite values. No bound on the sum of `b_occupied` or of `keep` on one device may be relied on, other than what follows from the above.
Results may differ from a plain program's by a relative error of at most 0.001.
Values may be sent and summed in bfloat16 or wider, within the bound.
No kernel may reach another device: no remote copies, remote signals or barrier semaphores. Data moves between devices by JAX's collectives and lax.ppermute only.
A program may use at most 64 MiB of HBM per device.

v0:
```python
import jax
import jax.numpy as jnp
from jax import lax
from jax.sharding import PartitionSpec as P


def spread(row_ids, slot_values, slot_index):
    picker = (row_ids[:, None, :] == slot_index[None, :, None]).astype(slot_values.dtype)
    return jnp.einsum(
        "gms,gsab->gmab", picker, slot_values, preferred_element_type=slot_values.dtype
    )


def apply_dense(running, dense_part, panel_part):
    return running + jnp.einsum(
        "gmab,gbc->mac", dense_part, panel_part, preferred_element_type=jnp.float32
    )


def run_groups(running, piece_count, add_group):
    full_groups = piece_count // 2
    running = lax.fori_loop(0, full_groups, lambda t, carry: add_group(carry, t * 2, 2), running)
    return running


def make_slot_fold(panels, slot_index):

    def fold_slots(carry, piece, start):
        piece_values, piece_rows = piece
        piece_count = piece_values.shape[0]

        def add_group(inner, first_row, group_size):
            part_values = lax.dynamic_slice_in_dim(piece_values, first_row, group_size, 0)
            part_rows = lax.dynamic_slice_in_dim(piece_rows, first_row, group_size, 0)
            panel_part = lax.dynamic_slice_in_dim(panels, first_row, group_size, 0)
            updated = apply_dense(inner, spread(part_rows, part_values, slot_index), panel_part)
            return updated

        return run_groups(carry, piece_count, add_group)

    return fold_slots


def shards(a_blocks, a_rows, b_blocks, b_occupied, keep, owner_rows):
    block_size = b_blocks.shape[2]
    slab_width = b_blocks.shape[3]
    col_count = keep.shape[1]
    group_rows = keep.shape[0]
    slot_count = a_rows.shape[3]
    layer_count = lax.axis_size("layer")
    own_count = group_rows // layer_count
    slot_index = jnp.arange(group_rows, dtype=jnp.int32)
    local_rows = b_blocks.shape[0]
    occupied = b_occupied[:, 0].astype(b_blocks.dtype)
    shaped = (
        b_blocks.reshape(local_rows, block_size, col_count, block_size) * occupied[:, None, :, None]
    )
    masked = shaped.reshape(local_rows, block_size, slab_width)
    layer_index = lax.axis_index("layer")
    half_width = slab_width // layer_count
    local_slabs = masked.reshape(local_rows, 1, block_size, slab_width)
    halves = lax.all_to_all(local_slabs, "layer", split_axis=3, concat_axis=1, tiled=True)
    column_panels = lax.all_gather(halves, "col", axis=0, tiled=True)
    panels = column_panels.reshape(column_panels.shape[0] * layer_count, block_size, half_width)
    running = jnp.zeros((group_rows, block_size, half_width), jnp.float32)
    fold_slots = make_slot_fold(panels, slot_index)
    flat_values = a_blocks.reshape(1, slot_count, block_size, block_size)
    flat_rows = a_rows.reshape(1, slot_count)
    running = fold_slots(
        running,
        (
            lax.all_gather(flat_values, ("row", "layer"), axis=0, tiled=True),
            lax.all_gather(flat_rows, ("row", "layer"), axis=0, tiled=True),
        ),
        jnp.int32(0),
    )
    column_mask = lax.dynamic_index_in_dim(keep, layer_index, 1, keepdims=False).astype(jnp.float32)
    filtered = (running * column_mask[:, None, None]).astype(jnp.bfloat16)
    owner_order = owner_rows[0]
    picked = jnp.arange(layer_count, dtype=jnp.int32)[:, None] * own_count + owner_order
    picked = jnp.transpose(picked, (1, 0)).reshape(-1)
    sending = jnp.take(filtered, picked, axis=0).reshape(
        own_count * layer_count // layer_count, layer_count, block_size, half_width
    )
    received = lax.all_to_all(sending, ("col", "layer"), split_axis=0, concat_axis=0, tiled=True)
    source_cols = received.shape[0] // layer_count
    grouped = received.reshape(source_cols, layer_count, layer_count, block_size, half_width)
    grouped = jnp.transpose(grouped, (0, 2, 3, 1, 4))
    result = grouped.reshape(source_cols * layer_count, block_size, layer_count * half_width)
    return result[None]


def solution(mesh):
    return jax.shard_map(
        shards,
        mesh=mesh,
        in_specs=(
            P(("grp", "row"), "layer", "col", None, None, None),
            P(("grp", "row"), "layer", "col", None),
            P(("grp", "col"), "layer", None, "row"),
            P(("grp", "col"), "layer", "row"),
            P(("grp", "col"), "row"),
            P(("grp", "col"), None, None),
        ),
        out_specs=P(("grp", "col", "layer"), None, None, "row"),
        check_vma=False,
    )
```

profile of v0, /device:TPU:0, one launch (start us, length us, event | category | flops | bytes accessed | tf_op | source)
XLA Modules:
  0.0 70.0 jit_solution(14253039182960089956)
XLA Ops:
  6.5 0.0 copy-start
  6.5 0.0 copy-start.1
  6.5 0.0 copy-start.2
  6.5 0.0 all-gather.5.cloned.1.call-start
  6.5 0.7 %all-gather.5.cloned.1.call-update = ((bf16[1,1,1,6,128,128]{5,4,3,2,1,0:T(8,128)(2,1)}), bf16[8,1,1,6,128,128]{5,4,3,2,1,0:T(8,128)(2,1)}) async-update(((), (), s32[]{:S(2)}) %all-gather.5.cloned.1.call-start, bf16[1,1,1,6,128,128]{5,4,3,2,1,0:T(8,128)(2,1)} %param.8) | async-update | bytes 1966104
  7.3 1.0 %copy.35 = bf16[1,1,128,256]{2,1,0,3:T(2,128)(2,1)S(1)} copy(bf16[1,1,128,256]{3,2,1,0:T(8,128)(2,1)} %param.10) | data formatting | bytes 131072 | tf_op args[2]
  8.2 0.7 convert_bitcast_fusion.1
  8.9 0.1 broadcast_bitcast_fusion
  9.0 0.3 fusion.15
  9.3 0.5 broadcast.65
  9.8 1.0 %reduce = bf16[256,128]{1,0:T(8,128)(2,1)S(1)} reduce(bf16[256,1,1,128]{3,2,1,0:T(2,128)(2,1)S(1)} %fusion.15, bf16[]{:T(256)} %broadcast.65), dimensions={1,2}, to_apply=%fusion.15.reduce_sub_computation | reduce | bytes 131074
  10.8 0.6 reshape.101
  11.5 3.3 %all-to-all-start = ((bf16[2,2,8192]{2,1,0:T(2,128)(2,1)}), bf16[2,2,8192]{2,1,0:T(2,128)(2,1)S(1)}, u32[]{:S(2)}, u32[]{:S(2)}) async-start(bf16[2,2,8192]{2,1,0:T(2,128)(2,1)} %reshape.101), calls=%async_computation | async-start | bytes 131072 | tf_op jit(solution)/shard_map/all_to_all | solution.py:62
  14.8 1.4 %all-to-all-done = bf16[2,2,8192]{2,1,0:T(2,128)(2,1)S(1)} async-done(((bf16[2,2,8192]{2,1,0:T(2,128)(2,1)}), bf16[2,2,8192]{2,1,0:T(2,128)(2,1)S(1)}, u32[]{:S(2)}, u32[]{:S(2)}) %all-to-all-start) | async-done | bytes 65568 | tf_op jit(solution)/shard_map/all_to_all | solution.py:62
  16.2 0.1 reshape.102
  16.3 0.1 copy.36
  16.4 0.0 copy-done
  16.4 0.1 compare_and_fusion
  16.5 0.1 copy.38
  16.6 0.1 reshape.84
  16.7 0.1 copy.34
  16.8 0.0 copy-done.1
  16.8 13.4 %all-gather = s32[8,1,1,6]{3,2,1,0:T(1,128)S(1)} all-gather(s32[1,1,1,6]{3,2,1,0:T(1,128)S(1)} %copy-done.1), channel_id=2, replica_groups=mesh['grp'=1,'row'=4,'col'=4,'layer'=2] {'row','layer'}, dimensions={0}, use_global_device_ids=true | all-gather | bytes 216 | tf_op jit(solution)/shard_map/all_gather | solution.py:73
  30.2 9.0 %all-gather.2 = bf16[4,2,1,128,128]{4,3,2,1,0:T(8,128)(2,1)S(1)} all-gather(bf16[1,2,1,128,128]{4,3,2,1,0:T(8,128)(2,1)S(1)} %copy.36), channel_id=4, replica_groups=mesh['grp'=1,'row'=4,'col'=4,'layer'=2] {'col'}, dimensions={0}, use_global_device_ids=true | all-gather | bytes 327680 | tf_op jit(solution)/shard_map/all_gather | solution.py:63
  39.1 0.0 copy-done.2
  39.2 0.0 all-gather.5.cloned.1.call-done
  39.2 9.4 %while.14 = (s32[]{:T(128)}, f32[16,128,128]{2,1,0:T(8,128)S(1)}, s32[8,6]{1,0:T(8,128)S(1)}, bf16[8,6,128,128]{3,2,1,0:T(8,128)(2,1)}, bf16[8,128,128]{2,1,0:T(...) while((s32[]{:T(128)}, f32[16,128,128]{2,1,0:T(8,128)S(1)}, ...), condition=%wide.region_1.0_spmd.clone, body=%wide.region_0.0_spmd.clone.sunk | while | flops 141033664 | bytes 5439801 | solution.py:22
  39.2 1.0 %constant_dynamic-slice_fusion.4 = bf16[2,6,128,128]{3,2,1,0:T(8,128)(2,1)S(1)} fusion(bf16[8,6,128,128]{3,2,1,0:T(8,128)(2,1)} %get-tuple-element.209, s32[]{:T(128)S(6)} %select_n.48), kind=kLoop, calls=%fused_computation.13.clone.1 | loop fusion | bytes 786436 | tf_op jit(solution)/shard_map/while/body/eval_jaxpr/dynamic_slice | solution.py:33
  40.3 0.7 fusion.26
  41.0 0.6 fusion.27
  41.6 1.0 %constant_dynamic-slice_fusion.4 = bf16[2,6,128,128]{3,2,1,0:T(8,128)(2,1)S(1)} fusion(bf16[8,6,128,128]{3,2,1,0:T(8,128)(2,1)} %get-tuple-element.209, s32[]{:T(128)S(6)} %select_n.48), kind=kLoop, calls=%fused_computation.13.clone.1 | loop fusion | bytes 786436 | tf_op jit(solution)/shard_map/while/body/eval_jaxpr/dynamic_slice | solution.py:33
  42.6 0.7 fusion.26
  43.3 0.6 fusion.27
  43.9 1.0 %constant_dynamic-slice_fusion.4 = bf16[2,6,128,128]{3,2,1,0:T(8,128)(2,1)S(1)} fusion(bf16[8,6,128,128]{3,2,1,0:T(8,128)(2,1)} %get-tuple-element.209, s32[]{:T(128)S(6)} %select_n.48), kind=kLoop, calls=%fused_computation.13.clone.1 | loop fusion | bytes 786436 | tf_op jit(solution)/shard_map/while/body/eval_jaxpr/dynamic_slice | solution.py:33
  45.0 0.7 fusion.26
  45.6 0.6 fusion.27
  46.2 1.0 %constant_dynamic-slice_fusion.4 = bf16[2,6,128,128]{3,2,1,0:T(8,128)(2,1)S(1)} fusion(bf16[8,6,128,128]{3,2,1,0:T(8,128)(2,1)} %get-tuple-element.209, s32[]{:T(128)S(6)} %select_n.48), kind=kLoop, calls=%fused_computation.13.clone.1 | loop fusion | bytes 786436 | tf_op jit(solution)/shard_map/while/body/eval_jaxpr/dynamic_slice | solution.py:33
  47.3 0.7 fusion.26
  48.0 0.6 fusion.27
  48.6 0.2 multiply_convert_fusion
  48.7 0.6 gather_fusion
  49.4 0.1 broadcast_select_fusion
  49.5 12.3 %all_to_all.23 = bf16[8,2,128,128]{3,2,1,0:T(8,128)(2,1)S(1)} all-to-all(bf16[8,2,128,128]{3,2,1,0:T(8,128)(2,1)S(1)} %broadcast_select_fusion), channel_id=1, replica_groups=mesh['grp'=1,'row'=4,'col'=4,'layer'=2] {'col','layer'}, dimensions={0} | all-to-all | bytes 1048576 | tf_op jit(solution)/shard_map/all_to_all | solution.py:85
  61.8 0.3 copy.39
  62.1 1.0 %copy.40 = bf16[1,8,128,256]{3,2,1,0:T(8,128)(2,1)} copy(bf16[1,8,128,256]{2,3,1,0:T(8,128)(2,1)S(1)} %bitcast.52) | data formatting | bytes 1048576 | tf_op jit(solution)/shard_map/broadcast_in_dim;reshape | solution.py:90
  (10 shorter events, 0.1 us)
Async XLA Ops:
  6.5 9.9 %copy-start = (s32[1,2,8]{2,1,0:T(2,128)S(1)}, s32[1,2,8]{2,1,0:T(2,128)}, u32[]{:S(2)}) copy-start(s32[1,2,8]{2,1,0:T(2,128)} %param.13) | copy-start | bytes 196
  6.5 10.2 %copy-start.1 = (s32[1,1,1,6]{3,2,1,0:T(1,128)S(1)}, s32[1,1,1,6]{3,2,1,0:T(1,128)}, u32[]{:S(2)}) copy-start(s32[1,1,1,6]{3,2,1,0:T(1,128)} %param.9) | copy-start | bytes 76
  6.5 32.6 %copy-start.2 = (s32[16,2]{0,1:T(2,128)S(1)}, s32[16,2]{0,1:T(2,128)}, u32[]{:S(2)}) copy-start(s32[16,2]{0,1:T(2,128)} %param.12) | copy-start | bytes 388
  6.5 32.7 %all-gather.5.cloned.1.call-start = ((), (), s32[]{:S(2)}) async-start(), calls=%async_computation.2 | async-start | bytes 1769472 | tf_op jit(solution)/shard_map/all_gather | solution.py:72
  11.5 4.7 %all-to-all-start = ((bf16[2,2,8192]{2,1,0:T(2,128)(2,1)}), bf16[2,2,8192]{2,1,0:T(2,128)(2,1)S(1)}, u32[]{:S(2)}, u32[]{:S(2)}) async-start(bf16[2,2,8192]{2,1,0:T(2,128)(2,1)} %reshape.101), calls=%async_computation | async-start | bytes 131072 | tf_op jit(solution)/shard_map/all_to_all | solution.py:62
Sparse Core Ops, SparseCore 0:
  9.0 27.7 all-gather.4
where the time goes:
time: 70.5 us; the launch traced here: 70 us
  blocking collectives  34.7 us (49%)
  between operations  13.5 us (19%)
  local copies, waits for them, and re-layouts  8.74 us (12%)
  matrix products  5.02 us (7%)
  starting transfers between devices  3.3 us (5%)
  other arithmetic  2.38 us (3%)
  waiting for transfers between devices  2.12 us (3%)
    all_gather x1, blocking collectives, shards(): lax.all_gather(flat_rows, ('row', 'layer'), axis=0, tiled=True)  13.4 us
    all_to_all x1, blocking collectives, shards(): lax.all_to_all(sending, ('col', 'layer'), split_axis=0, concat_axis=0, ti...  12.3 us
    all_gather x1, blocking collectives, shards(): column_panels = lax.all_gather(halves, 'col', axis=0, tiled=True)  8.97 us
    dynamic_slice x4, local copies, waits for them, and re-layouts, add_group(): lax.dynamic_slice_in_dim(piece_values, first_row, group_size, 0)  4.11 us
    all_to_all x1, starting transfers between devices, shards(): lax.all_to_all(local_slabs, 'layer', split_axis=3, concat_axis=1, tiled=T...  3.3 us
    dot_general x4, matrix products, spread(): jnp.einsum('gms,gsab->gmab', picker, slot_values, preferred_element_type=...  2.74 us
    dot_general x4, matrix products, apply_dense(): jnp.einsum('gmab,gbc->mac', dense_part, panel_part, preferred_element_typ...  2.28 us
    unnamed x11, local copies, waits for them, and re-layouts  2.21 us
  transfers between devices with their start and end apart: 2, of which 1 were waited for; matrix products, arithmetic and copies ran while one was open for 7% of the time, Pallas kernels for 0%

commit v1 on v0

v1 whole, which is shorter than its diff:
```python
import functools

import jax
import jax.numpy as jnp
from jax import lax
from jax.experimental import pallas as pl
from jax.experimental.pallas import tpu as pltpu
from jax.sharding import PartitionSpec as P


def product_kernel(orders, place_ref, ids_ref, owner_ref, keep_ref, b_ref, *refs):
    piece_refs = refs[: len(orders)]
    out_ref, table, panels = refs[len(orders) :]
    row, layer = place_ref[0], place_ref[1]
    row_count, layer_count, slot_count = ids_ref.shape
    half_rows, group_rows = owner_ref.shape[1], keep_ref.shape[0]
    local_rows = b_ref.shape[2]
    block_size = b_ref.shape[3]
    out_count = out_ref.shape[0]
    own_cols = out_count // layer_count
    steps = []
    for ref, order in zip(piece_refs, orders):
        for at, (flip_row, flip_layer) in enumerate(order):
            steps.append((ref, at, row ^ flip_row, flip_layer))
    places = []
    for ref, at, i, flip_layer in steps:
        places.append((i, layer ^ flip_layer))
    for n, (i, which) in enumerate(places):
        for m in range(group_rows):
            table[n, m] = -1
    for n, (i, which) in enumerate(places):
        for s in range(slot_count):
            table[n, ids_ref[i, which, s]] = s
    for n, (i, which) in enumerate(places):
        panels[n * block_size : (n + 1) * block_size, :] = b_ref[i // local_rows, which, i % local_rows]
    lane = lax.broadcasted_iota(jnp.int32, (1, b_ref.shape[4]), 1)
    for q in range(out_count):
        owner, half = q // layer_count, q % layer_count
        m = half * half_rows + owner_ref[half, owner * layer_count + layer]
        parts = []
        for n, (ref, at, _, _) in enumerate(steps):
            s = table[n, m]
            block = ref[at, jnp.maximum(s, 0)]
            parts.append(jnp.where(s >= 0, block, jnp.zeros_like(block)))
        total = jnp.dot(jnp.concatenate(parts, axis=1), panels[...], preferred_element_type=jnp.float32)
        kept = jnp.zeros((1, b_ref.shape[4]), jnp.float32)
        for n in range(keep_ref.shape[1]):
            kept = jnp.where(lane // block_size == n, keep_ref[m, n].astype(jnp.float32), kept)
        out_ref[q] = (total * kept).astype(out_ref.dtype)


def product(place, ids, owner_rows, keep, panels, pieces, orders):
    layer_count = ids.shape[1]
    block_size, width = panels.shape[3:]
    step_count = sum(len(order) for order in orders)
    smem = pl.BlockSpec(memory_space=pltpu.SMEM)
    vmem = pl.BlockSpec(memory_space=pltpu.VMEM)
    out_count = owner_rows.shape[1]
    return pl.pallas_call(
        functools.partial(product_kernel, orders),
        out_shape=jax.ShapeDtypeStruct((out_count, block_size, width), panels.dtype),
        in_specs=[smem] * 4 + [vmem] * (1 + len(pieces)),
        out_specs=vmem,
        scratch_shapes=[
            pltpu.SMEM((step_count, keep.shape[0]), jnp.int32),
            pltpu.VMEM((step_count * block_size, width), panels.dtype),
        ],
        compiler_params=pltpu.CompilerParams(vmem_limit_bytes=48 * 1024 * 1024),
    )(place, ids, owner_rows, keep, panels, *pieces)


def flip(count, by):
    return [(i, i ^ by) for i in range(count)]


def shards(a_blocks, a_rows, b_blocks, b_occupied, keep, owner_rows):
    local_rows, _, block_size, width = b_blocks.shape
    col_blocks = keep.shape[1]
    slot_count = a_rows.shape[3]
    row_count = lax.axis_size("row")
    layer_count = lax.axis_size("layer")
    own = a_blocks.reshape(1, slot_count, block_size, block_size)
    place = jnp.stack([lax.axis_index("row"), lax.axis_index("layer")])

    def over_row(piece, by):
        return lax.ppermute(piece, "row", flip(row_count, by))

    def over_layer(piece):
        return lax.ppermute(piece, "layer", flip(layer_count, 1))

    occupied = jnp.repeat(b_occupied.reshape(local_rows, 1, 1, col_blocks), width // col_blocks, axis=3)
    masked = b_blocks * occupied.astype(b_blocks.dtype)
    panels = lax.all_gather(masked, ("col", "layer")).reshape(
        lax.axis_size("col"), layer_count, local_rows, block_size, width
    )
    held = {0: own}
    near, far = [0], row_count // 2
    while far:
        for by in near:
            held[by ^ far] = over_row(held[by], far)
        if far == row_count // 2:
            held[far], panels, a_rows = lax.optimization_barrier((held[far], panels, a_rows))
        near, far = list(held), far // 2
    ids = lax.all_gather(a_rows.reshape(slot_count), ("row", "layer")).reshape(row_count, layer_count, slot_count)
    last = row_count - 1
    held[last], ids = lax.optimization_barrier((held[last], ids))
    pieces, orders = [], []
    for by in held:
        pieces += [held[by], over_layer(held[by])]
        orders += [((by, 0),), ((by, 1),)]
    sending = product(place, ids, owner_rows[0], keep, panels, pieces, orders)
    return lax.all_to_all(sending, "col", split_axis=0, concat_axis=0, tiled=True)[None]


def solution(mesh):
    return jax.shard_map(
        shards,
        mesh=mesh,
        in_specs=(
            P(("grp", "row"), "layer", "col", None, None, None),
            P(("grp", "row"), "layer", "col", None),
            P(("grp", "col"), "layer", None, "row"),
            P(("grp", "col"), "layer", "row"),
            P(("grp", "col"), "row"),
            P(("grp", "col"), None, None),
        ),
        out_specs=P(("grp", "col", "layer"), None, None, "row"),
        check_vma=False,
    )
```

time: 70.5 us -> 44.5 us (0.63)
  between operations: 13.5 us -> 0.04 us
  local copies, waits for them, and re-layouts: 8.74 us -> 2.02 us
  matrix products: 5.02 us -> 0 us
  starting transfers between devices: 3.3 us -> 7.03 us
  blocking collectives: 34.7 us -> 32.3 us
  waiting for transfers between devices: 2.12 us -> 0.3 us
  Pallas kernels: 0 us -> 1.68 us
  other arithmetic: 2.38 us -> 0.93 us
    ppermute x0 -> x7, starting transfers between devices: none -> 7.03 us  [the longest x3 6.06 us: over_row(): return lax.ppermute(piece, 'row', flip(row_count, by))]
    dot_general x8 -> x0, matrix products: 5.02 us -> none  [the longest x4 2.74 us: spread(): jnp.einsum('gms,gsab->gmab', picker, slot_values, preferred_element_type=...]
    dynamic_slice x8 -> x0, local copies, waits for them, and re-layouts: 4.15 us -> none  [the longest x4 4.11 us: add_group(): lax.dynamic_slice_in_dim(piece_values, first_row, group_size, 0)]
    all_to_all x1 -> x0, starting transfers between devices: 3.3 us -> none  [shards(): lax.all_to_all(local_slabs, 'layer', split_axis=3, concat_axis=1, tiled=T...]
    pallas_call x0 -> x1, Pallas kernels: none -> 1.68 us  [product(): pl.pallas_call(functools.partial(product_kernel, orders), out_shape=jax.S...]
    all_gather x2, blocking collectives: 22.4 us -> 20.7 us  [the longest x1 10.7 us: shards(): lax.all_gather(a_rows.reshape(slot_count), ('row', 'layer'))]
    all_to_all x1 -> x0, waiting for transfers between devices: 1.39 us -> none  [shards(): lax.all_to_all(local_slabs, 'layer', split_axis=3, concat_axis=1, tiled=T...]
    unnamed x3 -> x0, other arithmetic: 1.35 us -> none
  transfers between devices with their start and end apart: 2 -> 7, of which waited for: 1 -> 1; matrix products, arithmetic and copies ran while one was open for 7% -> 2% of each run, Pallas kernels for 0% -> 0%
where the time goes in v1:
time: 44.5 us; the launch traced here: 44.3 us
  blocking collectives  32.3 us (73%)
  starting transfers between devices  7.03 us (16%)
  local copies, waits for them, and re-layouts  2.02 us (5%)
  Pallas kernels  1.68 us (4%)
  other arithmetic  0.93 us (2%)
    all_to_all x1, blocking collectives, shards(): lax.all_to_all(sending, 'col', split_axis=0, concat_axis=0, tiled=True)  11.6 us
    all_gather x1, blocking collectives, shards(): lax.all_gather(a_rows.reshape(slot_count), ('row', 'layer'))  10.7 us
    all_gather x1, blocking collectives, shards(): lax.all_gather(masked, ('col', 'layer'))  10 us
    ppermute x3, starting transfers between devices, over_row(): return lax.ppermute(piece, 'row', flip(row_count, by))  6.06 us
    unnamed x12, local copies, waits for them, and re-layouts  1.94 us
    pallas_call x1, Pallas kernels, product(): pl.pallas_call(functools.partial(product_kernel, orders), out_shape=jax.S...  1.68 us
    ppermute x4, starting transfers between devices, over_layer(): return lax.ppermute(piece, 'layer', flip(layer_count, 1))  0.97 us
  transfers between devices with their start and end apart: 7, of which 1 were waited for; matrix products, arithmetic and copies ran while one was open for 2% of the time, Pallas kernels for 0%

profile of v1, /device:TPU:0, one launch (start us, length us, event | category | flops | bytes accessed | tf_op | source)
XLA Modules:
  0.0 44.3 jit_solution(14858303513049237946)
XLA Ops:
  0.0 0.0 copy-start.4
  0.0 3.0 %collective-permute-start.4 = (bf16[1,6,128,128]{3,2,1,0:T(8,128)(2,1)}, bf16[1,6,128,128]{3,2,1,0:T(8,128)(2,1)S(1)}, u32[]{:S(2)}, u32[]{:S(2)}) collective-permute-start(bf16[1,6,128,128]{3,2,1,0:T(8,128)(2,1)} %bitcast.12), channel_id=1, source_target_pairs={{0,8},{8,0},{16,24},{24,16},{1,9},{9,1},{17,25},{25,17},{2,10},{10... | collective-permute-start | bytes 589832 | tf_op jit(solution)/shard_map/ppermute | solution.py:86
  3.0 2.6 %collective-permute-start = (bf16[1,6,128,128]{3,2,1,0:T(8,128)(2,1)}, bf16[1,6,128,128]{3,2,1,0:T(8,128)(2,1)S(1)}, u32[]{:S(2)}, u32[]{:S(2)}) collective-permute-start(bf16[1,6,128,128]{3,2,1,0:T(8,128)(2,1)} %bitcast.13), channel_id=1, source_target_pairs={{0,16},{8,24},{16,0},{24,8},{1,17},{9,25},{17,1},{25,9},{2,18},{10... | collective-permute-start | bytes 589832 | tf_op jit(solution)/shard_map/ppermute | solution.py:86
  5.6 0.0 copy-done.4
  5.6 0.1 broadcast_bitcast_fusion
  5.7 0.8 %broadcast_multiply_fusion = bf16[1,1,128,256]{3,2,1,0:T(8,128)(2,1)S(1)} fusion(bf16[1,1,128,256]{3,2,1,0:T(8,128)(2,1)} %param.8, bf16[256]{0:T(256)(128)(2,1)S(1)} %broadcast_bitcast_fusion), kind=kLoop, calls=%fused_computation | loop fusion | flops 32768 | bytes 131584 | tf_op jit(solution)/shard_map/mul | solution.py:92
  6.5 0.0 copy-start
  6.6 10.0 %all-gather = bf16[8,1,128,256]{3,2,1,0:T(8,128)(2,1)S(1)} all-gather(bf16[1,1,128,256]{3,2,1,0:T(8,128)(2,1)S(1)} %broadcast_multiply_fusion), channel_id=2, replica_groups=mesh['grp'=1,'row'=4,'col'=4,'layer'=2] {'col','layer'}, dimensions={0}, use_global_device_ids=true | all-gather | bytes 589824 | tf_op jit(solution)/shard_map/all_gather | solution.py:93
  16.6 0.0 copy-start.3
  16.6 0.0 collective-permute-done.refs_2_
  16.6 0.5 %collective-permute-start.1 = (bf16[1,6,128,128]{3,2,1,0:T(8,128)(2,1)S(1)}, bf16[1,6,128,128]{3,2,1,0:T(8,128)(2,1)S(1)}, u32[]{:S(2)}, u32[]{:S(2)}) collective-permute-start(bf16[1,6,128,128]{3,2,1,0:T(8,128)(2,1)S(1)} %collective-permute-done.refs_2_), channel_id=1, source_target_pairs={{0,8},{8,0},{16,24},{24,16},{1,9},{9,1},{17,25},{25,17},{2,10},{10... | collective-permute-start | bytes 589832 | tf_op jit(solution)/shard_map/ppermute | solution.py:86
  17.0 0.0 copy-done
  17.0 0.2 collective-permute-start.2
  17.2 0.4 collective-permute-start.3
  17.5 0.0 collective-permute-done.4.refs_4_
  17.5 0.2 collective-permute-start.5
  17.7 0.0 copy-done.3
  17.7 10.7 %all-gather.1 = s32[8,1,1,6]{3,2,1,0:T(1,128)S(1)} all-gather(s32[1,1,1,6]{3,2,1,0:T(1,128)S(1)} %copy-done.3), channel_id=3, replica_groups=mesh['grp'=1,'row'=4,'col'=4,'layer'=2] {'row','layer'}, dimensions={0}, use_global_device_ids=true | all-gather | bytes 216 | tf_op jit(solution)/shard_map/all_gather | solution.py:104
  28.4 0.0 collective-permute-done.1.refs_6_
  28.4 0.3 collective-permute-start.6
  28.7 0.0 copy-start.2
  28.7 0.7 %copy-done.2 = s32[16,2]{0,1:T(2,128)S(1)} copy-done((s32[16,2]{0,1:T(2,128)S(1)}, s32[16,2]{0,1:T(2,128)}, u32[]{:S(2)}) %copy-start.2) | copy-done | bytes 152
  29.4 0.1 copy.9.keep_ref
  29.4 0.1 pad_add_fusion.place_ref
  29.5 0.0 copy-start.1
  29.5 0.0 collective-permute-done.2.refs_1_
  29.5 0.0 collective-permute-done.5.refs_5_
  29.5 0.0 collective-permute-done.3.refs_3_
  29.5 0.3 collective-permute-done.6.refs_7_
  29.8 0.4 copy-done.1
  30.2 1.7 %shard_map.64 = bf16[8,128,256]{2,1,0:T(8,128)(2,1)S(1)} custom-call(s32[2]{0:T(128)S(1)} %pad_add_fusion.place_ref, s32[4,2,6]{2,1,0:T(2,128)S(1)} %bitcast.16, s32[2,8]{1,0:T(2,128)S(1)} %bitcast.17, s32[16,2]{1,0:T(8,128)S(1)} %copy.9.keep_ref, bf16[4,2,1,128,256]{4,3,2,1,0:T(8,128)(2,1)S(1)} %bitcast.11, bf16[1,6,128,128]{3,2,1,0:T(8,128)(2,1)S(1)} %bitcast.15, ...), custom_call_target="tpu_custom_call" | custom-call | tf_op jit(solution)/shard_map/pallas_call | solution.py:59
  31.9 11.6 %all_to_all.5 = bf16[8,128,256]{2,1,0:T(8,128)(2,1)S(1)} all-to-all(bf16[8,128,256]{2,1,0:T(8,128)(2,1)S(1)} %shard_map.64), channel_id=1, replica_groups=mesh['grp'=1,'row'=4,'col'=4,'layer'=2] {'col'}, dimensions={0} | all-to-all | bytes 1048576 | tf_op jit(solution)/shard_map/all_to_all | solution.py:112
  43.5 0.8 %copy.11 = bf16[1,8,128,256]{3,2,1,0:T(8,128)(2,1)} copy(bf16[1,8,128,256]{3,2,1,0:T(8,128)(2,1)S(1)} %bitcast.18) | data formatting | bytes 1048576
  (1 shorter events, 0.0 us)
Async XLA Ops:
  0.0 5.6 %copy-start.4 = (s32[1,1,2]{2,1,0:T(1,128)S(1)}, s32[1,1,2]{2,1,0:T(1,128)}, u32[]{:S(2)}) copy-start(s32[1,1,2]{2,1,0:T(1,128)} %param.9) | copy-start | bytes 28
  0.0 17.5 %collective-permute-start.4 = (bf16[1,6,128,128]{3,2,1,0:T(8,128)(2,1)}, bf16[1,6,128,128]{3,2,1,0:T(8,128)(2,1)S(1)}, u32[]{:S(2)}, u32[]{:S(2)}) collective-permute-start(bf16[1,6,128,128]{3,2,1,0:T(8,128)(2,1)} %bitcast.12), channel_id=1, source_target_pairs={{0,8},{8,0},{16,24},{24,16},{1,9},{9,1},{17,25},{25,17},{2,10},{10... | collective-permute-start | bytes 589832 | tf_op jit(solution)/shard_map/ppermute | solution.py:86
  3.0 13.5 %collective-permute-start = (bf16[1,6,128,128]{3,2,1,0:T(8,128)(2,1)}, bf16[1,6,128,128]{3,2,1,0:T(8,128)(2,1)S(1)}, u32[]{:S(2)}, u32[]{:S(2)}) collective-permute-start(bf16[1,6,128,128]{3,2,1,0:T(8,128)(2,1)} %bitcast.13), channel_id=1, source_target_pairs={{0,16},{8,24},{16,0},{24,8},{1,17},{9,25},{17,1},{25,9},{2,18},{10... | collective-permute-start | bytes 589832 | tf_op jit(solution)/shard_map/ppermute | solution.py:86
  6.5 10.5 %copy-start = (bf16[1,1,1,6,128,128]{5,4,3,2,1,0:T(8,128)(2,1)S(1)}, bf16[1,1,1,6,128,128]{5,4,3,2,1,0:T(8,128)(2,1)}, u32[]{:S(2)}) copy-start(bf16[1,1,1,6,128,128]{5,4,3,2,1,0:T(8,128)(2,1)} %param.6) | copy-start | bytes 589828
  16.6 1.1 %copy-start.3 = (s32[1,1,1,6]{3,2,1,0:T(1,128)S(1)}, s32[1,1,1,6]{3,2,1,0:T(1,128)}, u32[]{:S(2)}) copy-start(s32[1,1,1,6]{3,2,1,0:T(1,128)} %param.7) | copy-start | bytes 76
  16.6 11.8 %collective-permute-start.1 = (bf16[1,6,128,128]{3,2,1,0:T(8,128)(2,1)S(1)}, bf16[1,6,128,128]{3,2,1,0:T(8,128)(2,1)S(1)}, u32[]{:S(2)}, u32[]{:S(2)}) collective-permute-start(bf16[1,6,128,128]{3,2,1,0:T(8,128)(2,1)S(1)} %collective-permute-done.refs_2_), channel_id=1, source_target_pairs={{0,8},{8,0},{16,24},{24,16},{1,9},{9,1},{17,25},{25,17},{2,10},{10... | collective-permute-start | bytes 589832 | tf_op jit(solution)/shard_map/ppermute | solution.py:86
  17.0 12.5 %collective-permute-start.2 = (bf16[1,6,128,128]{3,2,1,0:T(8,128)(2,1)S(1)}, bf16[1,6,128,128]{3,2,1,0:T(8,128)(2,1)S(1)}, u32[]{:S(2)}, u32[]{:S(2)}) collective-permute-start(bf16[1,6,128,128]{3,2,1,0:T(8,128)(2,1)S(1)} %bitcast.14), channel_id=1, source_target_pairs={{0,1},{1,0},{2,3},{3,2},{4,5},{5,4},{6,7},{7,6},{8,9},{9,8},{10,11... | collective-permute-start | bytes 589832 | tf_op jit(solution)/shard_map/ppermute | solution.py:89
  17.2 12.4 %collective-permute-start.3 = (bf16[1,6,128,128]{3,2,1,0:T(8,128)(2,1)S(1)}, bf16[1,6,128,128]{3,2,1,0:T(8,128)(2,1)S(1)}, u32[]{:S(2)}, u32[]{:S(2)}) collective-permute-start(bf16[1,6,128,128]{3,2,1,0:T(8,128)(2,1)S(1)} %collective-permute-done.refs_2_), channel_id=1, source_target_pairs={{0,1},{1,0},{2,3},{3,2},{4,5},{5,4},{6,7},{7,6},{8,9},{9,8},{10,11... | collective-permute-start | bytes 589832 | tf_op jit(solution)/shard_map/ppermute | solution.py:89
  17.5 12.0 %collective-permute-start.5 = (bf16[1,6,128,128]{3,2,1,0:T(8,128)(2,1)S(1)}, bf16[1,6,128,128]{3,2,1,0:T(8,128)(2,1)S(1)}, u32[]{:S(2)}, u32[]{:S(2)}) collective-permute-start(bf16[1,6,128,128]{3,2,1,0:T(8,128)(2,1)S(1)} %collective-permute-done.4.refs_4_), channel_id=1, source_target_pairs={{0,1},{1,0},{2,3},{3,2},{4,5},{5,4},{6,7},{7,6},{8,9},{9,8},{10,11... | collective-permute-start | bytes 589832 | tf_op jit(solution)/shard_map/ppermute | solution.py:89
  28.4 1.4 %collective-permute-start.6 = (bf16[1,6,128,128]{3,2,1,0:T(8,128)(2,1)S(1)}, bf16[1,6,128,128]{3,2,1,0:T(8,128)(2,1)S(1)}, u32[]{:S(2)}, u32[]{:S(2)}) collective-permute-start(bf16[1,6,128,128]{3,2,1,0:T(8,128)(2,1)S(1)} %collective-permute-done.1.refs_6_), channel_id=1, source_target_pairs={{0,1},{1,0},{2,3},{3,2},{4,5},{5,4},{6,7},{7,6},{8,9},{9,8},{10,11... | collective-permute-start | bytes 589832 | tf_op jit(solution)/shard_map/ppermute | solution.py:89
  28.7 0.7 %copy-start.2 = (s32[16,2]{0,1:T(2,128)S(1)}, s32[16,2]{0,1:T(2,128)}, u32[]{:S(2)}) copy-start(s32[16,2]{0,1:T(2,128)} %param.10) | copy-start | bytes 388
  29.5 0.7 %copy-start.1 = (s32[1,2,8]{2,1,0:T(2,128)S(1)}, s32[1,2,8]{2,1,0:T(2,128)}, u32[]{:S(2)}) copy-start(s32[1,2,8]{2,1,0:T(2,128)} %param.11) | copy-start | bytes 196

commit v2 on v0

v2 whole, which is shorter than its diff:
```python
import functools

import jax
import jax.numpy as jnp
from jax import lax
from jax.experimental import pallas as pl
from jax.experimental.pallas import tpu as pltpu
from jax.sharding import PartitionSpec as P

SMEM = pl.BlockSpec(memory_space=pltpu.SMEM)
VMEM = pl.BlockSpec(memory_space=pltpu.VMEM)
LIMIT = pltpu.CompilerParams(vmem_limit_bytes=48 * 1024 * 1024)
ANY = pl.BlockSpec(memory_space=pl.ANY)
TALL = 16


def turn_of(source, here, row_count):
    spots = [jnp.where(n % 2 == 1, n // 2 + 1, jnp.where(n == 0, 0, row_count - n // 2)) for n in (here, source)]
    ahead = (spots[0] - spots[1]) & (row_count - 1)
    return jnp.where(ahead == 0, 0, jnp.where(ahead <= row_count // 2, 2 * ahead - 1, 2 * (row_count - ahead)))


def prepare_kernel(a_ref, ids_ref, b_ref, occupied_ref, piece_ref, masked_ref, ids, occupied, panel, piece, done):
    rows, slot_count = a_ref.shape[0], ids.shape[1]
    local_rows, block_size, width = panel.shape
    copies = [
        pltpu.make_async_copy(ids_ref, ids, done.at[0]),
        pltpu.make_async_copy(occupied_ref, occupied, done.at[1]),
        pltpu.make_async_copy(b_ref, panel, done.at[2]),
        pltpu.make_async_copy(a_ref, piece.at[pl.ds(0, rows)], done.at[3]),
    ]
    for copy in copies:
        copy.start()
    copies[0].wait()
    line = lax.broadcasted_iota(jnp.int32, (TALL, block_size), 0)
    listed = jnp.full(line.shape, -1, jnp.int32)
    for s in range(slot_count):
        listed = jnp.where(line == s, ids[0, s], listed)
    piece[rows:, :] = listed.astype(jnp.float32).astype(piece.dtype)
    copies[3].wait()
    piece_out = pltpu.make_async_copy(piece, piece_ref, done.at[4])
    piece_out.start()
    copies[1].wait()
    copies[2].wait()
    lane = lax.broadcasted_iota(jnp.int32, (1, width), 1)
    for j in range(local_rows):
        kept = jnp.zeros((1, width), jnp.int32)
        for n in range(width // block_size):
            kept = jnp.where(lane // block_size == n, occupied[j, n], kept)
        panel[j] = panel[j] * kept.astype(jnp.float32).astype(panel.dtype)
    panel_out = pltpu.make_async_copy(panel, masked_ref, done.at[5])
    panel_out.start()
    piece_out.wait()
    panel_out.wait()


def prepare(blocks, ids, b_blocks, occupied):
    rows, block_size = blocks.shape
    return pl.pallas_call(
        prepare_kernel,
        out_shape=(
            jax.ShapeDtypeStruct((rows + TALL, block_size), blocks.dtype),
            jax.ShapeDtypeStruct(b_blocks.shape, b_blocks.dtype),
        ),
        in_specs=[ANY] * 4,
        out_specs=(ANY, ANY),
        scratch_shapes=[
            pltpu.SMEM(ids.shape, jnp.int32),
            pltpu.SMEM(occupied.shape, jnp.int32),
            pltpu.VMEM(b_blocks.shape, b_blocks.dtype),
            pltpu.VMEM((rows + TALL, block_size), blocks.dtype),
            pltpu.SemaphoreType.DMA((6,)),
        ],
        compiler_params=pltpu.CompilerParams(vmem_limit_bytes=60 * 1024 * 1024),
    )(blocks, ids, b_blocks, occupied)


def early_kernel(slot_count, owner_ref, keep_ref, *refs):
    layer_count, half_rows = owner_ref.shape
    col_count = half_rows // layer_count
    slab_ref, twin_ref, *piece_refs, total_ref, last_ref, chosen_ref, kept_ref, listed, ids, slots, panels, done = refs
    steps = len(piece_refs)
    block_size = piece_refs[0].shape[1]
    rows = slot_count * block_size
    _, local_rows, _, width = slab_ref.shape
    row, col, layer = (lax.axis_index(name) for name in ("row", "col", "layer"))
    for n, ref in enumerate(piece_refs):
        listed[n] = ref[rows : rows + TALL, :].astype(jnp.float32).astype(jnp.int32)
    copy = pltpu.make_async_copy(listed, ids, done)
    copy.start()
    for n in range(steps):
        for m in range(slots.shape[1]):
            slots[n, m] = -1
    for flip_col in range(col_count):
        for flip_layer, ref in enumerate((slab_ref, twin_ref)):
            for j in range(local_rows):
                turn = turn_of((col ^ flip_col) * local_rows + j, row, col_count * local_rows)
                panels[turn * layer_count + flip_layer] = ref[flip_col, j]
    for n in range(layer_count):
        last_ref[n * block_size : (n + 1) * block_size, :] = panels[steps + n]
    copy.wait()
    for n in range(steps):
        for s in range(slot_count):
            slots[n, ids[n, s, 0]] = s
    lane = lax.broadcasted_iota(jnp.int32, (1, width), 1)
    lines = []
    for q in range(total_ref.shape[0]):
        half = q % layer_count
        m = half * half_rows + owner_ref[half, (col ^ (q // layer_count)) * layer_count + layer]
        parts = []
        for n, ref in enumerate(piece_refs):
            s = slots[n, m]
            block = ref[pl.ds(pl.multiple_of(jnp.maximum(s, 0) * block_size, block_size), block_size), :]
            parts.append(jnp.where(s >= 0, block, jnp.zeros_like(block)))
        lines.append(jnp.concatenate(parts, axis=1))
        kept = jnp.zeros((1, width), jnp.int32)
        for n in range(width // block_size):
            kept = jnp.where(lane // block_size == n, keep_ref[n, m], kept)
        kept_ref[q : q + 1, :] = kept.astype(jnp.float32)
        chosen_ref[q : q + 1, :] = jnp.full((1, block_size), m, jnp.int32).astype(jnp.float32)
        if half == layer_count - 1:
            total = jnp.dot(
                jnp.concatenate(lines, axis=0),
                panels[:steps].reshape(steps * block_size, width),
                preferred_element_type=jnp.float32,
            )
            for n in range(layer_count):
                total_ref[q - half + n] = total[n * block_size : (n + 1) * block_size]
            lines = []


def early(slot_count, owner_rows, keep, slabs, twins, pieces):
    layer_count, out_count = owner_rows.shape
    block_size, width = slabs.shape[2:]
    steps, kind = len(pieces), slabs.dtype
    return pl.pallas_call(
        functools.partial(early_kernel, slot_count),
        out_shape=(
            jax.ShapeDtypeStruct((out_count, block_size, width), jnp.float32),
            jax.ShapeDtypeStruct((layer_count * block_size, width), kind),
            jax.ShapeDtypeStruct((out_count, block_size), jnp.float32),
            jax.ShapeDtypeStruct((out_count, width), jnp.float32),
        ),
        in_specs=[SMEM] * 2 + [VMEM] * (2 + steps),
        out_specs=[VMEM] * 4,
        scratch_shapes=[
            pltpu.VMEM((steps, TALL, block_size), jnp.int32),
            pltpu.SMEM((steps, TALL, block_size), jnp.int32),
            pltpu.SMEM((steps, keep.shape[1]), jnp.int32),
            pltpu.VMEM((steps + layer_count, block_size, width), kind),
            pltpu.SemaphoreType.DMA,
        ],
        compiler_params=LIMIT,
    )(owner_rows, keep, slabs, twins, *pieces)


def late_kernel(slot_count, total_ref, last_ref, chosen_ref, kept_ref, *refs):
    layer_count = last_ref.shape[0] // total_ref.shape[1]
    piece_refs, out_refs = refs[:layer_count], refs[layer_count:]
    block_size = total_ref.shape[1]
    rows = slot_count * block_size
    listed = [ref[rows : rows + TALL, :].astype(jnp.float32) for ref in piece_refs]
    for at, out_ref in enumerate(out_refs):
        lines = []
        for q in range(at * layer_count, (at + 1) * layer_count):
            parts = []
            for n, ref in enumerate(piece_refs):
                part = None
                for s in range(slot_count):
                    same = (listed[n][s : s + 1, :] == chosen_ref[q : q + 1, :]).astype(jnp.float32)
                    same = jnp.broadcast_to(same, (TALL, block_size)).astype(ref.dtype)
                    same = jnp.concatenate([same] * (block_size // TALL), axis=0)
                    block = ref[s * block_size : (s + 1) * block_size, :] * same
                    part = block if part is None else part + block
                parts.append(part)
            lines.append(jnp.concatenate(parts, axis=1))
        total = jnp.dot(jnp.concatenate(lines, axis=0), last_ref[...], preferred_element_type=jnp.float32)
        for n in range(layer_count):
            q = at * layer_count + n
            part = total[n * block_size : (n + 1) * block_size] + total_ref[q]
            out_ref[n] = (part * kept_ref[q : q + 1, :]).astype(out_ref.dtype)


def late(slot_count, totals, pieces):
    total, last = totals[:2]
    out_count, block_size, width = total.shape
    layer_count = last.shape[0] // block_size
    shape = jax.ShapeDtypeStruct((layer_count, block_size, width), last.dtype)
    return pl.pallas_call(
        functools.partial(late_kernel, slot_count),
        out_shape=[shape] * (out_count // layer_count),
        in_specs=[VMEM] * (4 + layer_count),
        out_specs=[VMEM] * (out_count // layer_count),
        compiler_params=LIMIT,
    )(*totals, *pieces)


def collect_kernel(*refs):
    *part_refs, out_ref, done = refs
    count, col = part_refs[0].shape[0], lax.axis_index("col")
    copies = []
    for flip_col, ref in enumerate(part_refs):
        at = pl.multiple_of((col ^ flip_col) * count, count)
        copies.append(pltpu.make_async_copy(ref, out_ref.at[pl.ds(at, count)], done.at[flip_col]))
    for copy in copies:
        copy.start()
    for copy in copies:
        copy.wait()


def collect(parts):
    count, block_size, width = parts[0].shape
    return pl.pallas_call(
        collect_kernel,
        out_shape=jax.ShapeDtypeStruct((count * len(parts), block_size, width), parts[0].dtype),
        in_specs=[VMEM] * len(parts),
        out_specs=ANY,
        scratch_shapes=[pltpu.SemaphoreType.DMA((len(parts),))],
        compiler_params=LIMIT,
    )(*parts)


def swap(value, axis, by):
    return lax.ppermute(value, axis, [(i, i ^ by) for i in range(lax.axis_size(axis))])


def shards(a_blocks, a_rows, b_blocks, b_occupied, keep, owner_rows):
    local_rows, _, block_size, width = b_blocks.shape
    slot_count = a_rows.shape[3]
    row_count, col_count, layer_count = (lax.axis_size(name) for name in ("row", "col", "layer"))
    ring = list(range(0, row_count, 2))[:1] + list(range(1, row_count, 2)) + list(range(row_count - 2, 0, -2))
    turns = [(n // 2 + 1) * (1 if n % 2 == 0 else -1) for n in range(row_count - 1)]
    turns = [0] + sorted(turns, key=abs)

    own, masked = prepare(
        a_blocks.reshape(slot_count * block_size, block_size),
        a_rows.reshape(1, slot_count),
        b_blocks.reshape(local_rows, block_size, width),
        b_occupied.reshape(local_rows, -1),
    )
    held, slabs = {0: own}, [masked]
    for turn in turns[1:]:
        step = 1 if turn > 0 else -1
        before = held[turn - step]
        held[turn] = lax.ppermute(
            before, "row", [(name, ring[(at + step) % row_count]) for at, name in enumerate(ring)]
        )
        if turn == turns[2]:
            slabs += [swap(masked, "col", by) for by in range(1, col_count)]
    slabs = jnp.stack(slabs)
    twins = swap(slabs, "layer", 1)
    pieces = []
    for turn in turns[:-1]:
        pieces += [held[turn], swap(held[turn], "layer", 1)]
    totals = early(slot_count, owner_rows[0], keep.T, slabs, twins, pieces)
    final = held[turns[-1]]
    parts = list(late(slot_count, totals, [final, swap(final, "layer", 1)]))
    for by in sorted(range(1, col_count), key=lambda n: -bin(n).count("1")):
        parts[by] = swap(parts[by], "col", by)
    return collect(parts)[None]


def solution(mesh):
    return jax.shard_map(
        shards,
        mesh=mesh,
        in_specs=(
            P(("grp", "row"), "layer", "col", None, None, None),
            P(("grp", "row"), "layer", "col", None),
            P(("grp", "col"), "layer", None, "row"),
            P(("grp", "col"), "layer", "row"),
            P(("grp", "col"), "row"),
            P(("grp", "col"), None, None),
        ),
        out_specs=P(("grp", "col", "layer"), None, None, "row"),
        check_vma=False,
    )
```

time: 70.5 us -> 36.2 us (0.51)
  blocking collectives: 34.7 us -> 0 us
  starting transfers between devices: 3.3 us -> 17.4 us
  between operations: 13.5 us -> 0.11 us
  waiting for transfers between devices: 2.12 us -> 11.2 us
  local copies, waits for them, and re-layouts: 8.74 us -> 0.68 us
  Pallas kernels: 0 us -> 5.71 us
  matrix products: 5.02 us -> 0 us
  other arithmetic: 2.38 us -> 0.91 us
    all_gather x2 -> x0, blocking collectives: 22.4 us -> none  [the longest x1 13.4 us: shards(): lax.all_gather(flat_rows, ('row', 'layer'), axis=0, tiled=True)]
    ppermute x0 -> x14, starting transfers between devices: none -> 17.4 us  [the longest x3 9.32 us: shards(): lax.ppermute(before, 'row', [(name, ring[(at + step) % row_count]) for at...]
    all_to_all x1 -> x0, blocking collectives: 12.3 us -> none  [shards(): lax.all_to_all(sending, ('col', 'layer'), split_axis=0, concat_axis=0, ti...]
    ppermute x0 -> x14, waiting for transfers between devices: none -> 11.2 us  [the longest x11 6.46 us: swap(): lax.ppermute(value, axis, [(i, i ^ by) for i in range(lax.axis_size(axis))])]
    pallas_call x0 -> x4, Pallas kernels: none -> 5.71 us  [the longest x1 2.57 us: early(): pl.pallas_call(functools.partial(early_kernel, slot_count), out_shape=(ja...]
    dot_general x8 -> x0, matrix products: 5.02 us -> none  [the longest x4 2.74 us: spread(): jnp.einsum('gms,gsab->gmab', picker, slot_values, preferred_element_type=...]
    dynamic_slice x8 -> x0, local copies, waits for them, and re-layouts: 4.15 us -> none  [the longest x4 4.11 us: add_group(): lax.dynamic_slice_in_dim(piece_values, first_row, group_size, 0)]
    all_to_all x1 -> x0, starting transfers between devices: 3.3 us -> none  [shards(): lax.all_to_all(local_slabs, 'layer', split_axis=3, concat_axis=1, tiled=T...]
  transfers between devices with their start and end apart: 2 -> 14, of which waited for: 1 -> 4; matrix products, arithmetic and copies ran while one was open for 7% -> 3% of each run, Pallas kernels for 0% -> 7%
where the time goes in v2:
time: 36.2 us; the launch traced here: 36.1 us
  starting transfers between devices  17.4 us (48%)
  waiting for transfers between devices  11.2 us (31%)
  Pallas kernels  5.71 us (16%)
  other arithmetic  0.91 us (3%)
  local copies, waits for them, and re-layouts  0.68 us (2%)
    ppermute x3, starting transfers between devices, shards(): lax.ppermute(before, 'row', [(name, ring[(at + step) % row_count]) for at...  9.32 us
    ppermute x11, starting transfers between devices, swap(): lax.ppermute(value, axis, [(i, i ^ by) for i in range(lax.axis_size(axis))])  8.11 us
    ppermute x11, waiting for transfers between devices, swap(): lax.ppermute(value, axis, [(i, i ^ by) for i in range(lax.axis_size(axis))])  6.46 us
    ppermute x3, waiting for transfers between devices, shards(): lax.ppermute(before, 'row', [(name, ring[(at + step) % row_count]) for at...  4.75 us
    pallas_call x1, Pallas kernels, early(): pl.pallas_call(functools.partial(early_kernel, slot_count), out_shape=(ja...  2.57 us
    pallas_call x1, Pallas kernels, prepare(): pl.pallas_call(prepare_kernel, out_shape=(jax.ShapeDtypeStruct((rows + TA...  1.71 us
    another operation x1, other arithmetic, shards(): slabs = jnp.stack(slabs)  0.91 us
    pallas_call x1, Pallas kernels, collect(): pl.pallas_call(collect_kernel, out_shape=jax.ShapeDtypeStruct((count * le...  0.82 us
  transfers between devices with their start and end apart: 14, of which 4 were waited for; matrix products, arithmetic and copies ran while one was open for 3% of the time, Pallas kernels for 7%

profile of v2, /device:TPU:0, one launch (start us, length us, event | category | flops | bytes accessed | tf_op | source)
XLA Modules:
  0.0 36.1 jit_solution(340413925577562493)
XLA Ops:
  0.0 1.7 %shard_map.64 = (bf16[784,128]{1,0:T(8,128)(2,1)}, bf16[1,128,256]{2,1,0:T(8,128)(2,1)}) custom-call(bf16[768,128]{1,0:T(8,128)(2,1)} %bitcast.13, s32[1,6]{1,0:T(1,128)} %bitcast.19, bf16[1,128,256]{2,1,0:T(8,128)(2,1)} %bitcast.14, s32[1,2]{1,0:T(1,128)} %bitcast.20), custom_call_target="tpu_custom_call" | custom-call | tf_op jit(solution)/shard_map/pallas_call | solution.py:59
  1.7 3.1 %collective-permute-start.5 = (bf16[784,128]{1,0:T(8,128)(2,1)}, bf16[784,128]{1,0:T(8,128)(2,1)S(1)}, u32[]{:S(2)}, u32[]{:S(2)}) collective-permute-start(bf16[784,128]{1,0:T(8,128)(2,1)} %get-tuple-element.16.refs_2_), channel_id=1, source_target_pairs={{0,8},{8,24},{24,16},{16,0},{1,9},{9,25},{25,17},{17,1},{2,10},{10... | collective-permute-start | bytes 602120 | tf_op jit(solution)/shard_map/ppermute | solution.py:245
  4.8 1.5 %collective-permute-start = (bf16[1,128,256]{2,1,0:T(8,128)(2,1)}, bf16[1,128,256]{2,1,0:T(8,128)(2,1)S(1)}, u32[]{:S(2)}, u32[]{:S(2)}) collective-permute-start(bf16[1,128,256]{2,1,0:T(8,128)(2,1)} %get-tuple-element.15), channel_id=1, source_target_pairs={{0,2},{2,0},{4,6},{6,4},{1,3},{3,1},{5,7},{7,5},{8,10},{10,8},{12,... | collective-permute-start | bytes 196616 | tf_op jit(solution)/shard_map/ppermute | solution.py:224
  6.3 1.5 %collective-permute-start.1 = (bf16[1,128,256]{2,1,0:T(8,128)(2,1)}, bf16[1,128,256]{2,1,0:T(8,128)(2,1)S(1)}, u32[]{:S(2)}, u32[]{:S(2)}) collective-permute-start(bf16[1,128,256]{2,1,0:T(8,128)(2,1)} %get-tuple-element.15), channel_id=1, source_target_pairs={{0,4},{2,6},{4,0},{6,2},{1,5},{3,7},{5,1},{7,3},{8,12},{10,14},{12... | collective-permute-start | bytes 196616 | tf_op jit(solution)/shard_map/ppermute | solution.py:224
  7.8 0.5 %collective-permute-start.2 = (bf16[1,128,256]{2,1,0:T(8,128)(2,1)}, bf16[1,128,256]{2,1,0:T(8,128)(2,1)S(1)}, u32[]{:S(2)}, u32[]{:S(2)}) collective-permute-start(bf16[1,128,256]{2,1,0:T(8,128)(2,1)} %get-tuple-element.15), channel_id=1, source_target_pairs={{0,6},{2,4},{4,2},{6,0},{1,7},{3,5},{5,3},{7,1},{8,14},{10,12},{12... | collective-permute-start | bytes 196616 | tf_op jit(solution)/shard_map/ppermute | solution.py:224
  8.3 1.1 %collective-permute-start.7 = (bf16[784,128]{1,0:T(8,128)(2,1)}, bf16[784,128]{1,0:T(8,128)(2,1)S(1)}, u32[]{:S(2)}, u32[]{:S(2)}) collective-permute-start(bf16[784,128]{1,0:T(8,128)(2,1)} %get-tuple-element.16.refs_2_), channel_id=1, source_target_pairs={{0,16},{8,0},{24,8},{16,24},{1,17},{9,1},{25,9},{17,25},{2,18},{10... | collective-permute-start | bytes 602120 | tf_op jit(solution)/shard_map/ppermute | solution.py:245
  9.4 1.7 %collective-permute-done.5.refs_4_ = bf16[784,128]{1,0:T(8,128)(2,1)S(1)} collective-permute-done((bf16[784,128]{1,0:T(8,128)(2,1)}, bf16[784,128]{1,0:T(8,128)(2,1)S(1)}, u32[]{:S(2)}, u32[]{:S(2)}) %collective-permute-start.5) | collective-permute-done | bytes 200736 | tf_op jit(solution)/shard_map/ppermute | solution.py:245
  11.0 5.2 %collective-permute-start.9 = (bf16[784,128]{1,0:T(8,128)(2,1)S(1)}, bf16[784,128]{1,0:T(8,128)(2,1)S(1)}, u32[]{:S(2)}, u32[]{:S(2)}) collective-permute-start(bf16[784,128]{1,0:T(8,128)(2,1)S(1)} %collective-permute-done.5.refs_4_), channel_id=1, source_target_pairs={{0,8},{8,24},{24,16},{16,0},{1,9},{9,25},{25,17},{17,1},{2,10},{10... | collective-permute-start | bytes 602120 | tf_op jit(solution)/shard_map/ppermute | solution.py:245
  16.2 0.0 collective-permute-done
  16.2 0.0 collective-permute-done.1
  16.2 0.0 collective-permute-done.2
  16.2 0.0 copy-start
  16.2 0.0 copy-start.2
  16.2 0.9 %pad_maximum_fusion.refs_0_ = bf16[4,1,128,256]{3,2,1,0:T(8,128)(2,1)S(1)} fusion(bf16[1,1,128,256]{3,2,1,0:T(8,128)(2,1)S(1)} %bitcast.18, bf16[1,1,128,256]{3,2,1,0:T(8,128)(2,1)S(1)} %bitcast.17, bf16[1,1,128,256]{3,2,1,0:T(8,128)(2,1)S(1)} %bitcast.16, bf16[1,1,128,256]{3,2,1,0:T(8,128)(2,1)} %bitcast.15), kind=kLoop, calls=%fused_computation | loop fusion | flops 393216 | bytes 524288 | tf_op jit(solution)/shard_map/stack | solution.py:250
  17.2 0.1 collective-permute-start.3
  17.2 0.0 copy-done
  17.2 0.5 %collective-permute-start.4 = (bf16[784,128]{1,0:T(8,128)(2,1)S(1)}, bf16[784,128]{1,0:T(8,128)(2,1)S(1)}, u32[]{:S(2)}, u32[]{:S(2)}) collective-permute-start(bf16[784,128]{1,0:T(8,128)(2,1)S(1)} %copy-done), channel_id=1, source_target_pairs={{0,1},{1,0},{2,3},{3,2},{4,5},{5,4},{6,7},{7,6},{8,9},{9,8},{10,11... | collective-permute-start | bytes 602120 | tf_op jit(solution)/shard_map/ppermute | solution.py:224
  17.7 0.1 collective-permute-start.6
  17.8 0.0 collective-permute-done.7.refs_6_
  17.8 0.4 %collective-permute-start.8 = (bf16[784,128]{1,0:T(8,128)(2,1)S(1)}, bf16[784,128]{1,0:T(8,128)(2,1)S(1)}, u32[]{:S(2)}, u32[]{:S(2)}) collective-permute-start(bf16[784,128]{1,0:T(8,128)(2,1)S(1)} %collective-permute-done.7.refs_6_), channel_id=1, source_target_pairs={{0,1},{1,0},{2,3},{3,2},{4,5},{5,4},{6,7},{7,6},{8,9},{9,8},{10,11... | collective-permute-start | bytes 602120 | tf_op jit(solution)/shard_map/ppermute | solution.py:224
  18.2 3.1 %collective-permute-done.9.refs_0_ = bf16[784,128]{1,0:T(8,128)(2,1)S(1)} collective-permute-done((bf16[784,128]{1,0:T(8,128)(2,1)S(1)}, bf16[784,128]{1,0:T(8,128)(2,1)S(1)}, u32[]{:S(2)}, u32[]{:S(2)}) %collective-permute-start.9) | collective-permute-done | bytes 200736 | tf_op jit(solution)/shard_map/ppermute | solution.py:245
  21.3 0.0 collective-permute-start.10
  21.3 0.0 collective-permute-done.4.refs_3_
  21.3 0.0 collective-permute-done.3.refs_1_
  21.3 0.0 collective-permute-done.6.refs_5_
  21.4 0.0 collective-permute-done.8.refs_7_
  21.4 0.0 copy-start.1
  21.4 0.0 copy-done.2
  21.4 0.7 %copy-done.1 = s32[1,2,8]{2,1,0:T(2,128)S(1)} copy-done((s32[1,2,8]{2,1,0:T(2,128)S(1)}, s32[1,2,8]{2,1,0:T(2,128)}, u32[]{:S(2)}) %copy-start.1) | copy-done | bytes 88
  22.0 2.6 %shard_map.65 = (f32[8,128,256]{2,1,0:T(8,128)S(1)}, bf16[256,256]{1,0:T(8,128)(2,1)S(1)}, f32[8,128]{1,0:T(8,128)S(1)}, f32[8,256]{1,0:T(8,128)S(1)}) custom-call(s32[2,8]{1,0:T(2,128)S(1)} %bitcast.11, s32[2,16]{1,0:T(2,128)S(1)} %bitcast.12, bf16[4,1,128,256]{3,2,1,0:T(8,128)(2,1)S(1)} %pad_maximum_fusion.refs_0_, ...), custom_call_target="tpu_custom_call" | custom-call | tf_op jit(solution)/shard_map/pallas_call | solution.py:136
  24.6 0.0 collective-permute-done.10.refs_1_
  24.6 0.6 %shard_map.66 = (bf16[2,128,256]{2,1,0:T(8,128)(2,1)S(1)}, bf16[2,128,256]{2,1,0:T(8,128)(2,1)S(1)}, bf16[2,128,256]{2,1,0:T(8,128)(2,1)S(1)}, bf16[2,128,256]{2,1,0:T(8,128)(2,1)S(1)}) custom-call(f32[8,128,256]{2,1,0:T(8,128)S(1)} %get-tuple-element.17.total_ref, bf16[256,256]{1,0:T(8,128)(2,1)S(1)} %get-tuple-element.18.last_ref, ...), custom_call_target="tpu_custom_call" | custom-call | tf_op jit(solution)/shard_map/pallas_call | solution.py:189
  25.3 1.6 %collective-permute-start.11 = (bf16[2,128,256]{2,1,0:T(8,128)(2,1)S(1)}, bf16[2,128,256]{2,1,0:T(8,128)(2,1)S(1)}, u32[]{:S(2)}, u32[]{:S(2)}) collective-permute-start(bf16[2,128,256]{2,1,0:T(8,128)(2,1)S(1)} %get-tuple-element.22), channel_id=1, source_target_pairs={{0,2},{2,0},{4,6},{6,4},{1,3},{3,1},{5,7},{7,5},{8,10},{10,8},{12,... | collective-permute-start | bytes 393224 | tf_op jit(solution)/shard_map/ppermute | solution.py:224
  26.8 1.5 %collective-permute-start.12 = (bf16[2,128,256]{2,1,0:T(8,128)(2,1)S(1)}, bf16[2,128,256]{2,1,0:T(8,128)(2,1)S(1)}, u32[]{:S(2)}, u32[]{:S(2)}) collective-permute-start(bf16[2,128,256]{2,1,0:T(8,128)(2,1)S(1)} %get-tuple-element.23), channel_id=1, source_target_pairs={{0,4},{2,6},{4,0},{6,2},{1,5},{3,7},{5,1},{7,3},{8,12},{10,14},{12... | collective-permute-start | bytes 393224 | tf_op jit(solution)/shard_map/ppermute | solution.py:224
  28.3 0.5 %collective-permute-start.13 = (bf16[2,128,256]{2,1,0:T(8,128)(2,1)S(1)}, bf16[2,128,256]{2,1,0:T(8,128)(2,1)S(1)}, u32[]{:S(2)}, u32[]{:S(2)}) collective-permute-start(bf16[2,128,256]{2,1,0:T(8,128)(2,1)S(1)} %get-tuple-element.24), channel_id=1, source_target_pairs={{0,6},{2,4},{4,2},{6,0},{1,7},{3,5},{5,3},{7,1},{8,14},{10,12},{12... | collective-permute-start | bytes 393224 | tf_op jit(solution)/shard_map/ppermute | solution.py:224
  28.8 2.8 %collective-permute-done.11.refs_1_ = bf16[2,128,256]{2,1,0:T(8,128)(2,1)S(1)} collective-permute-done((bf16[2,128,256]{2,1,0:T(8,128)(2,1)S(1)}, bf16[2,128,256]{2,1,0:T(8,128)(2,1)S(1)}, u32[]{:S(2)}, u32[]{:S(2)}) %collective-permute-start.11) | collective-permute-done | bytes 131104 | tf_op jit(solution)/shard_map/ppermute | solution.py:224
  31.6 3.6 %collective-permute-done.12.refs_2_ = bf16[2,128,256]{2,1,0:T(8,128)(2,1)S(1)} collective-permute-done((bf16[2,128,256]{2,1,0:T(8,128)(2,1)S(1)}, bf16[2,128,256]{2,1,0:T(8,128)(2,1)S(1)}, u32[]{:S(2)}, u32[]{:S(2)}) %collective-permute-start.12) | collective-permute-done | bytes 131104 | tf_op jit(solution)/shard_map/ppermute | solution.py:224
  35.2 0.0 collective-permute-done.13.refs_3_
  35.2 0.8 %shard_map.67 = bf16[8,128,256]{2,1,0:T(8,128)(2,1)} custom-call(bf16[2,128,256]{2,1,0:T(8,128)(2,1)S(1)} %get-tuple-element.21.refs_0_, bf16[2,128,256]{2,1,0:T(8,128)(2,1)S(1)} %collective-permute-done.11.refs_1_, bf16[2,128,256]{2,1,0:T(8,128)(2,1)S(1)} %collective-permute-done.12.refs_2_, bf16[2,128,256]{2,1,0:T(8,128)(2,1)S(1)} %collective-permute-done.13.refs_3_), custom_call_target="tpu_custom_call" | custom-call | tf_op jit(solution)/shard_map/pallas_call | solution.py:213
Async XLA Ops:
  1.7 9.3 %collective-permute-start.5 = (bf16[784,128]{1,0:T(8,128)(2,1)}, bf16[784,128]{1,0:T(8,128)(2,1)S(1)}, u32[]{:S(2)}, u32[]{:S(2)}) collective-permute-start(bf16[784,128]{1,0:T(8,128)(2,1)} %get-tuple-element.16.refs_2_), channel_id=1, source_target_pairs={{0,8},{8,24},{24,16},{16,0},{1,9},{9,25},{25,17},{17,1},{2,10},{10... | collective-permute-start | bytes 602120 | tf_op jit(solution)/shard_map/ppermute | solution.py:245
  4.8 11.4 %collective-permute-start = (bf16[1,128,256]{2,1,0:T(8,128)(2,1)}, bf16[1,128,256]{2,1,0:T(8,128)(2,1)S(1)}, u32[]{:S(2)}, u32[]{:S(2)}) collective-permute-start(bf16[1,128,256]{2,1,0:T(8,128)(2,1)} %get-tuple-element.15), channel_id=1, source_target_pairs={{0,2},{2,0},{4,6},{6,4},{1,3},{3,1},{5,7},{7,5},{8,10},{10,8},{12,... | collective-permute-start | bytes 196616 | tf_op jit(solution)/shard_map/ppermute | solution.py:224
  6.3 9.9 %collective-permute-start.1 = (bf16[1,128,256]{2,1,0:T(8,128)(2,1)}, bf16[1,128,256]{2,1,0:T(8,128)(2,1)S(1)}, u32[]{:S(2)}, u32[]{:S(2)}) collective-permute-start(bf16[1,128,256]{2,1,0:T(8,128)(2,1)} %get-tuple-element.15), channel_id=1, source_target_pairs={{0,4},{2,6},{4,0},{6,2},{1,5},{3,7},{5,1},{7,3},{8,12},{10,14},{12... | collective-permute-start | bytes 196616 | tf_op jit(solution)/shard_map/ppermute | solution.py:224
  7.8 8.4 %collective-permute-start.2 = (bf16[1,128,256]{2,1,0:T(8,128)(2,1)}, bf16[1,128,256]{2,1,0:T(8,128)(2,1)S(1)}, u32[]{:S(2)}, u32[]{:S(2)}) collective-permute-start(bf16[1,128,256]{2,1,0:T(8,128)(2,1)} %get-tuple-element.15), channel_id=1, source_target_pairs={{0,6},{2,4},{4,2},{6,0},{1,7},{3,5},{5,3},{7,1},{8,14},{10,12},{12... | collective-permute-start | bytes 196616 | tf_op jit(solution)/shard_map/ppermute | solution.py:224
  8.3 9.5 %collective-permute-start.7 = (bf16[784,128]{1,0:T(8,128)(2,1)}, bf16[784,128]{1,0:T(8,128)(2,1)S(1)}, u32[]{:S(2)}, u32[]{:S(2)}) collective-permute-start(bf16[784,128]{1,0:T(8,128)(2,1)} %get-tuple-element.16.refs_2_), channel_id=1, source_target_pairs={{0,16},{8,0},{24,8},{16,24},{1,17},{9,1},{25,9},{17,25},{2,18},{10... | collective-permute-start | bytes 602120 | tf_op jit(solution)/shard_map/ppermute | solution.py:245
  11.0 10.3 %collective-permute-start.9 = (bf16[784,128]{1,0:T(8,128)(2,1)S(1)}, bf16[784,128]{1,0:T(8,128)(2,1)S(1)}, u32[]{:S(2)}, u32[]{:S(2)}) collective-permute-start(bf16[784,128]{1,0:T(8,128)(2,1)S(1)} %collective-permute-done.5.refs_4_), channel_id=1, source_target_pairs={{0,8},{8,24},{24,16},{16,0},{1,9},{9,25},{25,17},{17,1},{2,10},{10... | collective-permute-start | bytes 602120 | tf_op jit(solution)/shard_map/ppermute | solution.py:245
  16.2 1.0 %copy-start = (bf16[784,128]{1,0:T(8,128)(2,1)S(1)}, bf16[784,128]{1,0:T(8,128)(2,1)}, u32[]{:S(2)}) copy-start(bf16[784,128]{1,0:T(8,128)(2,1)} %get-tuple-element.16.refs_2_) | copy-start | bytes 602116
  16.2 5.2 %copy-start.2 = (s32[16,2]{0,1:T(2,128)S(1)}, s32[16,2]{0,1:T(2,128)}, u32[]{:S(2)}) copy-start(s32[16,2]{0,1:T(2,128)} %param.10) | copy-start | bytes 388
  17.2 4.2 %collective-permute-start.3 = (bf16[4,1,128,256]{3,2,1,0:T(8,128)(2,1)S(1)}, bf16[4,1,128,256]{3,2,1,0:T(8,128)(2,1)S(1)}, u32[]{:S(2)}, u32[]{:S(2)}) collective-permute-start(bf16[4,1,128,256]{3,2,1,0:T(8,128)(2,1)S(1)} %pad_maximum_fusion.refs_0_), channel_id=1, source_target_pairs={{0,1},{1,0},{2,3},{3,2},{4,5},{5,4},{6,7},{7,6},{8,9},{9,8},{10,11... | collective-permute-start | bytes 786440 | tf_op jit(solution)/shard_map/ppermute | solution.py:224
  17.2 4.1 %collective-permute-start.4 = (bf16[784,128]{1,0:T(8,128)(2,1)S(1)}, bf16[784,128]{1,0:T(8,128)(2,1)S(1)}, u32[]{:S(2)}, u32[]{:S(2)}) collective-permute-start(bf16[784,128]{1,0:T(8,128)(2,1)S(1)} %copy-done), channel_id=1, source_target_pairs={{0,1},{1,0},{2,3},{3,2},{4,5},{5,4},{6,7},{7,6},{8,9},{9,8},{10,11... | collective-permute-start | bytes 602120 | tf_op jit(solution)/shard_map/ppermute | solution.py:224
  17.7 3.6 %collective-permute-start.6 = (bf16[784,128]{1,0:T(8,128)(2,1)S(1)}, bf16[784,128]{1,0:T(8,128)(2,1)S(1)}, u32[]{:S(2)}, u32[]{:S(2)}) collective-permute-start(bf16[784,128]{1,0:T(8,128)(2,1)S(1)} %collective-permute-done.5.refs_4_), channel_id=1, source_target_pairs={{0,1},{1,0},{2,3},{3,2},{4,5},{5,4},{6,7},{7,6},{8,9},{9,8},{10,11... | collective-permute-start | bytes 602120 | tf_op jit(solution)/shard_map/ppermute | solution.py:224
  17.8 3.5 %collective-permute-start.8 = (bf16[784,128]{1,0:T(8,128)(2,1)S(1)}, bf16[784,128]{1,0:T(8,128)(2,1)S(1)}, u32[]{:S(2)}, u32[]{:S(2)}) collective-permute-start(bf16[784,128]{1,0:T(8,128)(2,1)S(1)} %collective-permute-done.7.refs_6_), channel_id=1, source_target_pairs={{0,1},{1,0},{2,3},{3,2},{4,5},{5,4},{6,7},{7,6},{8,9},{9,8},{10,11... | collective-permute-start | bytes 602120 | tf_op jit(solution)/shard_map/ppermute | solution.py:224
  21.3 3.3 %collective-permute-start.10 = (bf16[784,128]{1,0:T(8,128)(2,1)S(1)}, bf16[784,128]{1,0:T(8,128)(2,1)S(1)}, u32[]{:S(2)}, u32[]{:S(2)}) collective-permute-start(bf16[784,128]{1,0:T(8,128)(2,1)S(1)} %collective-permute-done.9.refs_0_), channel_id=1, source_target_pairs={{0,1},{1,0},{2,3},{3,2},{4,5},{5,4},{6,7},{7,6},{8,9},{9,8},{10,11... | collective-permute-start | bytes 602120 | tf_op jit(solution)/shard_map/ppermute | solution.py:224
  21.4 0.7 %copy-start.1 = (s32[1,2,8]{2,1,0:T(2,128)S(1)}, s32[1,2,8]{2,1,0:T(2,128)}, u32[]{:S(2)}) copy-start(s32[1,2,8]{2,1,0:T(2,128)} %param.11) | copy-start | bytes 196
  25.3 6.4 %collective-permute-start.11 = (bf16[2,128,256]{2,1,0:T(8,128)(2,1)S(1)}, bf16[2,128,256]{2,1,0:T(8,128)(2,1)S(1)}, u32[]{:S(2)}, u32[]{:S(2)}) collective-permute-start(bf16[2,128,256]{2,1,0:T(8,128)(2,1)S(1)} %get-tuple-element.22), channel_id=1, source_target_pairs={{0,2},{2,0},{4,6},{6,4},{1,3},{3,1},{5,7},{7,5},{8,10},{10,8},{12,... | collective-permute-start | bytes 393224 | tf_op jit(solution)/shard_map/ppermute | solution.py:224
  26.8 8.4 %collective-permute-start.12 = (bf16[2,128,256]{2,1,0:T(8,128)(2,1)S(1)}, bf16[2,128,256]{2,1,0:T(8,128)(2,1)S(1)}, u32[]{:S(2)}, u32[]{:S(2)}) collective-permute-start(bf16[2,128,256]{2,1,0:T(8,128)(2,1)S(1)} %get-tuple-element.23), channel_id=1, source_target_pairs={{0,4},{2,6},{4,0},{6,2},{1,5},{3,7},{5,1},{7,3},{8,12},{10,14},{12... | collective-permute-start | bytes 393224 | tf_op jit(solution)/shard_map/ppermute | solution.py:224
  28.3 6.9 %collective-permute-start.13 = (bf16[2,128,256]{2,1,0:T(8,128)(2,1)S(1)}, bf16[2,128,256]{2,1,0:T(8,128)(2,1)S(1)}, u32[]{:S(2)}, u32[]{:S(2)}) collective-permute-start(bf16[2,128,256]{2,1,0:T(8,128)(2,1)S(1)} %get-tuple-element.24), channel_id=1, source_target_pairs={{0,6},{2,4},{4,2},{6,0},{1,7},{3,5},{5,3},{7,1},{8,14},{10,12},{12... | collective-permute-start | bytes 393224 | tf_op jit(solution)/shard_map/ppermute | solution.py:224

commit v3 on v2

v3 whole, which is shorter than its diff:
```python
import functools

import jax
import jax.numpy as jnp
from jax import lax
from jax.experimental import pallas as pl
from jax.experimental.pallas import tpu as pltpu
from jax.sharding import PartitionSpec as P

SMEM = pl.BlockSpec(memory_space=pltpu.SMEM)
VMEM = pl.BlockSpec(memory_space=pltpu.VMEM)
LIMIT = pltpu.CompilerParams(vmem_limit_bytes=48 * 1024 * 1024)
ANY = pl.BlockSpec(memory_space=pl.ANY)
TALL = 16


def turn_of(source, here, row_count):
    spots = [jnp.where(n % 2 == 1, n // 2 + 1, jnp.where(n == 0, 0, row_count - n // 2)) for n in (here, source)]
    ahead = (spots[0] - spots[1]) & (row_count - 1)
    return jnp.where(ahead == 0, 0, jnp.where(ahead <= row_count // 2, 2 * ahead - 1, 2 * (row_count - ahead)))


def prepare_kernel(a_ref, ids_ref, b_ref, occupied_ref, piece_ref, masked_ref, ids, occupied, panel, piece, done):
    rows, slot_count = a_ref.shape[0], ids.shape[1]
    local_rows, block_size, width = panel.shape
    copies = [
        pltpu.make_async_copy(ids_ref, ids, done.at[0]),
        pltpu.make_async_copy(occupied_ref, occupied, done.at[1]),
        pltpu.make_async_copy(b_ref, panel, done.at[2]),
        pltpu.make_async_copy(a_ref, piece.at[pl.ds(0, rows)], done.at[3]),
    ]
    for copy in copies:
        copy.start()
    copies[0].wait()
    line = lax.broadcasted_iota(jnp.int32, (TALL, block_size), 0)
    listed = jnp.full(line.shape, -1, jnp.int32)
    for s in range(slot_count):
        listed = jnp.where(line == s, ids[0, s], listed)
    piece[rows:, :] = listed.astype(jnp.float32).astype(piece.dtype)
    copies[3].wait()
    piece_out = pltpu.make_async_copy(piece, piece_ref, done.at[4])
    piece_out.start()
    copies[1].wait()
    copies[2].wait()
    lane = lax.broadcasted_iota(jnp.int32, (1, width), 1)
    for j in range(local_rows):
        kept = jnp.zeros((1, width), jnp.int32)
        for n in range(width // block_size):
            kept = jnp.where(lane // block_size == n, occupied[j, n], kept)
        panel[j] = panel[j] * kept.astype(jnp.float32).astype(panel.dtype)
    panel_out = pltpu.make_async_copy(panel, masked_ref, done.at[5])
    panel_out.start()
    piece_out.wait()
    panel_out.wait()


def prepare(blocks, ids, b_blocks, occupied):
    rows, block_size = blocks.shape
    return pl.pallas_call(
        prepare_kernel,
        out_shape=(
            jax.ShapeDtypeStruct((rows + TALL, block_size), blocks.dtype),
            jax.ShapeDtypeStruct(b_blocks.shape, b_blocks.dtype),
        ),
        in_specs=[ANY] * 4,
        out_specs=(ANY, ANY),
        scratch_shapes=[
            pltpu.SMEM(ids.shape, jnp.int32),
            pltpu.SMEM(occupied.shape, jnp.int32),
            pltpu.VMEM(b_blocks.shape, b_blocks.dtype),
            pltpu.VMEM((rows + TALL, block_size), blocks.dtype),
            pltpu.SemaphoreType.DMA((6,)),
        ],
        compiler_params=pltpu.CompilerParams(vmem_limit_bytes=60 * 1024 * 1024),
    )(blocks, ids, b_blocks, occupied)


def choose_kernel(owner_ref, keep_ref, chosen_ref, kept_ref):
    layer_count, half_rows = owner_ref.shape
    out_count, block_size = chosen_ref.shape
    width = kept_ref.shape[1]
    col, layer = lax.axis_index("col"), lax.axis_index("layer")
    lane = lax.broadcasted_iota(jnp.int32, (1, width), 1)
    for q in range(out_count):
        half = q % layer_count
        m = half * half_rows + owner_ref[half, (col ^ (q // layer_count)) * layer_count + layer]
        kept = jnp.zeros((1, width), jnp.int32)
        for n in range(width // block_size):
            kept = jnp.where(lane // block_size == n, keep_ref[n, m], kept)
        kept_ref[q : q + 1, :] = kept.astype(jnp.float32)
        chosen_ref[q : q + 1, :] = jnp.full((1, block_size), m, jnp.int32).astype(jnp.float32)


def choose(owner_rows, keep, block_size):
    out_count = owner_rows.shape[1]
    return pl.pallas_call(
        choose_kernel,
        out_shape=(
            jax.ShapeDtypeStruct((out_count, block_size), jnp.float32),
            jax.ShapeDtypeStruct((out_count, keep.shape[0] * block_size), jnp.float32),
        ),
        in_specs=[SMEM] * 2,
        out_specs=[VMEM] * 2,
        compiler_params=LIMIT,
    )(owner_rows, keep)


def pick(slot_count, piece_refs, chosen_ref, queries):
    block_size = chosen_ref.shape[1]
    rows = slot_count * block_size
    listed = [ref[rows : rows + TALL, :].astype(jnp.float32) for ref in piece_refs]
    lines = []
    for q in queries:
        parts = []
        for n, ref in enumerate(piece_refs):
            part = None
            for s in range(slot_count):
                same = (listed[n][s : s + 1, :] == chosen_ref[pl.ds(q, 1), :]).astype(jnp.float32)
                same = jnp.broadcast_to(same, (TALL, block_size)).astype(ref.dtype)
                same = jnp.concatenate([same] * (block_size // TALL), axis=0)
                block = ref[s * block_size : (s + 1) * block_size, :] * same
                part = block if part is None else part + block
            parts.append(part)
        lines.append(jnp.concatenate(parts, axis=1))
    return jnp.concatenate(lines, axis=0)


def early_kernel(slot_count, chosen_ref, slab_ref, twin_ref, *refs):
    *piece_refs, total_ref, last_ref, panels = refs
    steps = len(piece_refs)
    col_count, local_rows, block_size, width = slab_ref.shape
    out_count = total_ref.shape[0]
    layer_count = out_count // col_count
    row, col = lax.axis_index("row"), lax.axis_index("col")
    for flip_col in range(col_count):
        for flip_layer, ref in enumerate((slab_ref, twin_ref)):
            for j in range(local_rows):
                turn = turn_of((col ^ flip_col) * local_rows + j, row, col_count * local_rows)
                panels[turn * layer_count + flip_layer] = ref[flip_col, j]
    for n in range(last_ref.shape[0] // block_size):
        last_ref[n * block_size : (n + 1) * block_size, :] = panels[steps + n]

    def add(at, carry):
        queries = [at * layer_count + n for n in range(layer_count)]
        total = jnp.dot(
            pick(slot_count, piece_refs, chosen_ref, queries),
            panels[:steps].reshape(steps * block_size, width),
            preferred_element_type=jnp.float32,
        )
        for n, q in enumerate(queries):
            total_ref[q] = total[n * block_size : (n + 1) * block_size]
        return carry

    if steps > 16:
        lax.fori_loop(0, col_count, add, 0)
    else:
        for at in range(col_count):
            add(at, 0)


def early(slot_count, late_count, chosen, slabs, twins, pieces):
    block_size, width = slabs.shape[2:]
    steps, kind = len(pieces), slabs.dtype
    return pl.pallas_call(
        functools.partial(early_kernel, slot_count),
        out_shape=(
            jax.ShapeDtypeStruct((chosen.shape[0], block_size, width), jnp.float32),
            jax.ShapeDtypeStruct((late_count * block_size, width), kind),
        ),
        in_specs=[VMEM] * (3 + steps),
        out_specs=[VMEM] * 2,
        scratch_shapes=[pltpu.VMEM((steps + late_count, block_size, width), kind)],
        compiler_params=LIMIT,
    )(chosen, slabs, twins, *pieces)


def late_kernel(slot_count, col_count, total_ref, last_ref, chosen_ref, kept_ref, *refs):
    piece_refs, out_refs = refs[:-col_count], refs[-col_count:]
    block_size = total_ref.shape[1]
    layer_count = total_ref.shape[0] // col_count
    for at, out_ref in enumerate(out_refs):
        queries = range(at * layer_count, (at + 1) * layer_count)
        lines = pick(slot_count, piece_refs, chosen_ref, queries)
        total = jnp.dot(lines, last_ref[...], preferred_element_type=jnp.float32)
        for n, q in enumerate(queries):
            part = total[n * block_size : (n + 1) * block_size] + total_ref[q]
            out_ref[n] = (part * kept_ref[q : q + 1, :]).astype(out_ref.dtype)


def late(slot_count, col_count, totals, chosen, kept, pieces):
    total, last = totals
    out_count, block_size, width = total.shape
    shape = jax.ShapeDtypeStruct((out_count // col_count, block_size, width), last.dtype)
    return pl.pallas_call(
        functools.partial(late_kernel, slot_count, col_count),
        out_shape=[shape] * col_count,
        in_specs=[VMEM] * (4 + len(pieces)),
        out_specs=[VMEM] * col_count,
        compiler_params=LIMIT,
    )(total, last, chosen, kept, *pieces)


def collect_kernel(*refs):
    *part_refs, out_ref, done = refs
    count, col = part_refs[0].shape[0], lax.axis_index("col")
    copies = []
    for flip_col, ref in enumerate(part_refs[::-1]):
        at = pl.multiple_of((col ^ flip_col) * count, count)
        copies.append(pltpu.make_async_copy(ref, out_ref.at[pl.ds(at, count)], done.at[flip_col]))
    for copy in copies:
        copy.start()
    for copy in copies:
        copy.wait()


def collect(parts):
    count, block_size, width = parts[0].shape
    return pl.pallas_call(
        collect_kernel,
        out_shape=jax.ShapeDtypeStruct((count * len(parts), block_size, width), parts[0].dtype),
        in_specs=[VMEM] * len(parts),
        out_specs=ANY,
        scratch_shapes=[pltpu.SemaphoreType.DMA((len(parts),))],
        compiler_params=LIMIT,
    )(*parts[::-1])


def swap(value, axis, by):
    return lax.ppermute(value, axis, [(i, i ^ by) for i in range(lax.axis_size(axis))])


def shards(a_blocks, a_rows, b_blocks, b_occupied, keep, owner_rows):
    local_rows, _, block_size, width = b_blocks.shape
    slot_count = a_rows.shape[3]
    row_count, col_count, layer_count = (lax.axis_size(name) for name in ("row", "col", "layer"))
    ring = list(range(0, row_count, 2))[:1] + list(range(1, row_count, 2)) + list(range(row_count - 2, 0, -2))
    turns = [(n // 2 + 1) * (1 if n % 2 == 0 else -1) for n in range(row_count - 1)]
    turns = [0] + sorted(turns, key=abs)

    own, masked = prepare(
        a_blocks.reshape(slot_count * block_size, block_size),
        a_rows.reshape(1, slot_count),
        b_blocks.reshape(local_rows, block_size, width),
        b_occupied.reshape(local_rows, -1),
    )
    chosen, kept = choose(owner_rows[0], keep.T, block_size)
    slabs = [masked] + [swap(masked, "col", by) for by in range(1, col_count)]
    chosen, kept, *slabs = lax.optimization_barrier((chosen, kept, *slabs))
    slabs = jnp.stack(slabs)
    twins = swap(slabs, "layer", 1)
    held = {0: own}
    for turn in turns[1:]:
        step = 1 if turn > 0 else -1
        held[turn] = lax.ppermute(
            held[turn - step], "row", [(name, ring[(at + step) % row_count]) for at, name in enumerate(ring)]
        )
    split = row_count - 1
    pieces = [one for turn in turns for one in (held[turn], swap(held[turn], "layer", 1))]
    steps = split * layer_count
    totals = early(slot_count, len(pieces) - steps, chosen, slabs, twins, pieces[:steps])
    parts = list(late(slot_count, col_count, totals, chosen, kept, pieces[steps:]))
    for by in sorted(range(1, col_count), key=lambda n: -bin(n).count("1")):
        parts[by] = swap(parts[by], "col", by)
    return collect(parts)[None]


def solution(mesh):
    return jax.shard_map(
        shards,
        mesh=mesh,
        in_specs=(
            P(("grp", "row"), "layer", "col", None, None, None),
            P(("grp", "row"), "layer", "col", None),
            P(("grp", "col"), "layer", None, "row"),
            P(("grp", "col"), "layer", "row"),
            P(("grp", "col"), "row"),
            P(("grp", "col"), None, None),
        ),
        out_specs=P(("grp", "col", "layer"), None, None, "row"),
        check_vma=False,
    )
```

time: 36.2 us -> 34.3 us (0.948)
  waiting for transfers between devices: 11.2 us -> 9.7 us
  Pallas kernels: 5.71 us -> 5.28 us
    ppermute x3, waiting for transfers between devices: 4.75 us -> 3.46 us  [shards(): lax.ppermute(held[turn - step], 'row', [(name, ring[(at + step) % row_cou...]
    pallas_call x1, Pallas kernels: 2.57 us -> 1.54 us  [early(): pl.pallas_call(functools.partial(early_kernel, slot_count), out_shape=(ja...]
    pallas_call x1 -> x2, Pallas kernels: 0.62 us -> 1.23 us  [the longest x1 0.62 us: late(): pl.pallas_call(functools.partial(late_kernel, slot_count, col_count), out...]
  transfers between devices with their start and end apart: 14 -> 14, of which waited for: 4 -> 5; matrix products, arithmetic and copies ran while one was open for 3% -> 3% of each run, Pallas kernels for 7% -> 6%
where the time goes in v3:
time: 34.3 us; the launch traced here: 34.1 us
  starting transfers between devices  17.4 us (51%)
  waiting for transfers between devices  9.7 us (28%)
  Pallas kernels  5.28 us (15%)
  other arithmetic  0.91 us (3%)
  local copies, waits for them, and re-layouts  0.69 us (2%)
    ppermute x3, starting transfers between devices, shards(): lax.ppermute(held[turn - step], 'row', [(name, ring[(at + step) % row_cou...  9.32 us
    ppermute x11, starting transfers between devices, swap(): lax.ppermute(value, axis, [(i, i ^ by) for i in range(lax.axis_size(axis))])  8.12 us
    ppermute x11, waiting for transfers between devices, swap(): lax.ppermute(value, axis, [(i, i ^ by) for i in range(lax.axis_size(axis))])  6.24 us
    ppermute x3, waiting for transfers between devices, shards(): lax.ppermute(held[turn - step], 'row', [(name, ring[(at + step) % row_cou...  3.46 us
    pallas_call x1, Pallas kernels, prepare(): pl.pallas_call(prepare_kernel, out_shape=(jax.ShapeDtypeStruct((rows + TA...  1.7 us
    pallas_call x1, Pallas kernels, early(): pl.pallas_call(functools.partial(early_kernel, slot_count), out_shape=(ja...  1.54 us
    another operation x1, other arithmetic, shards(): slabs = jnp.stack(slabs)  0.91 us
    pallas_call x1, Pallas kernels, collect(): pl.pallas_call(collect_kernel, out_shape=jax.ShapeDtypeStruct((count * le...  0.82 us
  transfers between devices with their start and end apart: 14, of which 5 were waited for; matrix products, arithmetic and copies ran while one was open for 3% of the time, Pallas kernels for 6%

profile of v3, /device:TPU:0, one launch (start us, length us, event | category | flops | bytes accessed | tf_op | source)
XLA Modules:
  0.0 34.1 jit_solution(349522078788448237)
XLA Ops:
  0.0 1.7 %shard_map.65 = (bf16[784,128]{1,0:T(8,128)(2,1)}, bf16[1,128,256]{2,1,0:T(8,128)(2,1)}) custom-call(bf16[768,128]{1,0:T(8,128)(2,1)} %bitcast.13, s32[1,6]{1,0:T(1,128)} %bitcast.19, bf16[1,128,256]{2,1,0:T(8,128)(2,1)} %bitcast.14, s32[1,2]{1,0:T(1,128)} %bitcast.20), custom_call_target="tpu_custom_call" | custom-call | tf_op jit(solution)/shard_map/pallas_call | solution.py:59
  1.7 3.1 %collective-permute-start.5 = (bf16[784,128]{1,0:T(8,128)(2,1)}, bf16[784,128]{1,0:T(8,128)(2,1)S(1)}, u32[]{:S(2)}, u32[]{:S(2)}) collective-permute-start(bf16[784,128]{1,0:T(8,128)(2,1)} %get-tuple-element.29.refs_0_), channel_id=1, source_target_pairs={{0,8},{8,24},{24,16},{16,0},{1,9},{9,25},{25,17},{17,1},{2,10},{10... | collective-permute-start | bytes 602120 | tf_op jit(solution)/shard_map/ppermute | solution.py:254
  4.8 0.0 copy-start.2
  4.8 1.5 %collective-permute-start = (bf16[1,128,256]{2,1,0:T(8,128)(2,1)}, bf16[1,128,256]{2,1,0:T(8,128)(2,1)S(1)}, u32[]{:S(2)}, u32[]{:S(2)}) collective-permute-start(bf16[1,128,256]{2,1,0:T(8,128)(2,1)} %get-tuple-element.25), channel_id=1, source_target_pairs={{0,2},{2,0},{4,6},{6,4},{1,3},{3,1},{5,7},{7,5},{8,10},{10,8},{12,... | collective-permute-start | bytes 196616 | tf_op jit(solution)/shard_map/ppermute | solution.py:229
  6.3 1.5 %collective-permute-start.1 = (bf16[1,128,256]{2,1,0:T(8,128)(2,1)}, bf16[1,128,256]{2,1,0:T(8,128)(2,1)S(1)}, u32[]{:S(2)}, u32[]{:S(2)}) collective-permute-start(bf16[1,128,256]{2,1,0:T(8,128)(2,1)} %get-tuple-element.25), channel_id=1, source_target_pairs={{0,4},{2,6},{4,0},{6,2},{1,5},{3,7},{5,1},{7,3},{8,12},{10,14},{12... | collective-permute-start | bytes 196616 | tf_op jit(solution)/shard_map/ppermute | solution.py:229
  7.8 0.5 %collective-permute-start.2 = (bf16[1,128,256]{2,1,0:T(8,128)(2,1)}, bf16[1,128,256]{2,1,0:T(8,128)(2,1)S(1)}, u32[]{:S(2)}, u32[]{:S(2)}) collective-permute-start(bf16[1,128,256]{2,1,0:T(8,128)(2,1)} %get-tuple-element.25), channel_id=1, source_target_pairs={{0,6},{2,4},{4,2},{6,0},{1,7},{3,5},{5,3},{7,1},{8,14},{10,12},{12... | collective-permute-start | bytes 196616 | tf_op jit(solution)/shard_map/ppermute | solution.py:229
  8.3 1.1 %collective-permute-start.7 = (bf16[784,128]{1,0:T(8,128)(2,1)}, bf16[784,128]{1,0:T(8,128)(2,1)S(1)}, u32[]{:S(2)}, u32[]{:S(2)}) collective-permute-start(bf16[784,128]{1,0:T(8,128)(2,1)} %get-tuple-element.29.refs_0_), channel_id=1, source_target_pairs={{0,16},{8,0},{24,8},{16,24},{1,17},{9,1},{25,9},{17,25},{2,18},{10... | collective-permute-start | bytes 602120 | tf_op jit(solution)/shard_map/ppermute | solution.py:254
  9.4 1.7 %collective-permute-done.5.refs_2_ = bf16[784,128]{1,0:T(8,128)(2,1)S(1)} collective-permute-done((bf16[784,128]{1,0:T(8,128)(2,1)}, bf16[784,128]{1,0:T(8,128)(2,1)S(1)}, u32[]{:S(2)}, u32[]{:S(2)}) %collective-permute-start.5) | collective-permute-done | bytes 200736 | tf_op jit(solution)/shard_map/ppermute | solution.py:254
  11.0 5.1 %collective-permute-start.9 = (bf16[784,128]{1,0:T(8,128)(2,1)S(1)}, bf16[784,128]{1,0:T(8,128)(2,1)S(1)}, u32[]{:S(2)}, u32[]{:S(2)}) collective-permute-start(bf16[784,128]{1,0:T(8,128)(2,1)S(1)} %collective-permute-done.5.refs_2_), channel_id=1, source_target_pairs={{0,8},{8,24},{24,16},{16,0},{1,9},{9,25},{25,17},{17,1},{2,10},{10... | collective-permute-start | bytes 602120 | tf_op jit(solution)/shard_map/ppermute | solution.py:254
  16.2 0.0 copy-start.1
  16.2 0.0 copy-done.2
  16.2 0.7 %copy-done.1 = s32[1,2,8]{2,1,0:T(2,128)S(1)} copy-done((s32[1,2,8]{2,1,0:T(2,128)S(1)}, s32[1,2,8]{2,1,0:T(2,128)}, u32[]{:S(2)}) %copy-start.1) | copy-done | bytes 88
  16.8 0.6 %shard_map.64 = (f32[8,128]{1,0:T(8,128)S(1)}, f32[8,256]{1,0:T(8,128)S(1)}) custom-call(s32[2,8]{1,0:T(2,128)S(1)} %bitcast.11, s32[2,16]{1,0:T(2,128)S(1)} %bitcast.12), custom_call_target="tpu_custom_call" | custom-call | tf_op jit(solution)/shard_map/pallas_call | solution.py:96
  17.5 0.0 collective-permute-done
  17.5 0.0 collective-permute-done.1
  17.5 0.0 collective-permute-done.2
  17.5 0.0 copy-start
  17.5 0.9 %pad_maximum_fusion.slab_ref = bf16[4,1,128,256]{3,2,1,0:T(8,128)(2,1)S(1)} fusion(bf16[1,1,128,256]{3,2,1,0:T(8,128)(2,1)S(1)} %bitcast.18, bf16[1,1,128,256]{3,2,1,0:T(8,128)(2,1)S(1)} %bitcast.17, bf16[1,1,128,256]{3,2,1,0:T(8,128)(2,1)S(1)} %bitcast.16, bf16[1,1,128,256]{3,2,1,0:T(8,128)(2,1)} %bitcast.15), kind=kLoop, calls=%fused_computation | loop fusion | flops 393216 | bytes 524288 | tf_op jit(solution)/shard_map/stack | solution.py:249
  18.4 0.1 collective-permute-start.3
  18.5 0.0 copy-done
  18.5 0.5 %collective-permute-start.4 = (bf16[784,128]{1,0:T(8,128)(2,1)S(1)}, bf16[784,128]{1,0:T(8,128)(2,1)S(1)}, u32[]{:S(2)}, u32[]{:S(2)}) collective-permute-start(bf16[784,128]{1,0:T(8,128)(2,1)S(1)} %copy-done), channel_id=1, source_target_pairs={{0,1},{1,0},{2,3},{3,2},{4,5},{5,4},{6,7},{7,6},{8,9},{9,8},{10,11... | collective-permute-start | bytes 602120 | tf_op jit(solution)/shard_map/ppermute | solution.py:229
  19.0 0.1 collective-permute-start.6
  19.1 0.0 collective-permute-done.7.refs_4_
  19.1 0.4 %collective-permute-start.8 = (bf16[784,128]{1,0:T(8,128)(2,1)S(1)}, bf16[784,128]{1,0:T(8,128)(2,1)S(1)}, u32[]{:S(2)}, u32[]{:S(2)}) collective-permute-start(bf16[784,128]{1,0:T(8,128)(2,1)S(1)} %collective-permute-done.7.refs_4_), channel_id=1, source_target_pairs={{0,1},{1,0},{2,3},{3,2},{4,5},{5,4},{6,7},{7,6},{8,9},{9,8},{10,11... | collective-permute-start | bytes 602120 | tf_op jit(solution)/shard_map/ppermute | solution.py:229
  19.5 1.8 %collective-permute-done.9.refs_0_ = bf16[784,128]{1,0:T(8,128)(2,1)S(1)} collective-permute-done((bf16[784,128]{1,0:T(8,128)(2,1)S(1)}, bf16[784,128]{1,0:T(8,128)(2,1)S(1)}, u32[]{:S(2)}, u32[]{:S(2)}) %collective-permute-start.9) | collective-permute-done | bytes 200736 | tf_op jit(solution)/shard_map/ppermute | solution.py:254
  21.3 0.0 collective-permute-start.10
  21.3 0.0 collective-permute-done.4.refs_1_
  21.3 0.0 collective-permute-done.3.twin_ref
  21.3 0.0 collective-permute-done.6.refs_3_
  21.3 0.0 collective-permute-done.8.refs_5_
  21.4 1.5 %shard_map.66 = (f32[8,128,256]{2,1,0:T(8,128)S(1)}, bf16[256,256]{1,0:T(8,128)(2,1)S(1)}) custom-call(f32[8,128]{1,0:T(8,128)S(1)} %get-tuple-element.24.chosen_ref, bf16[4,1,128,256]{3,2,1,0:T(8,128)(2,1)S(1)} %pad_maximum_fusion.slab_ref, bf16[4,1,128,256]{3,2,1,0:T(8,128)(2,1)S(1)} %collective-permute-done.3.twin_ref, bf16[784,128]{1,0:T(8,128)(2,1)S(1)} %copy-done, ...), custom_call_target="tpu_custom_call" | custom-call | tf_op jit(solution)/shard_map/pallas_call | solution.py:164
  22.9 0.0 collective-permute-done.10.refs_1_
  22.9 0.6 %shard_map.67 = (bf16[2,128,256]{2,1,0:T(8,128)(2,1)S(1)}, bf16[2,128,256]{2,1,0:T(8,128)(2,1)S(1)}, bf16[2,128,256]{2,1,0:T(8,128)(2,1)S(1)}, bf16[2,128,256]{2,1,0:T(8,128)(2,1)S(1)}) custom-call(f32[8,128,256]{2,1,0:T(8,128)S(1)} %get-tuple-element.30.total_ref, bf16[256,256]{1,0:T(8,128)(2,1)S(1)} %get-tuple-element.31.last_ref, ...), custom_call_target="tpu_custom_call" | custom-call | tf_op jit(solution)/shard_map/pallas_call | solution.py:194
  23.5 2.5 %collective-permute-start.11 = (bf16[2,128,256]{2,1,0:T(8,128)(2,1)S(1)}, bf16[2,128,256]{2,1,0:T(8,128)(2,1)S(1)}, u32[]{:S(2)}, u32[]{:S(2)}) collective-permute-start(bf16[2,128,256]{2,1,0:T(8,128)(2,1)S(1)} %get-tuple-element.33), channel_id=1, source_target_pairs={{0,6},{2,4},{4,2},{6,0},{1,7},{3,5},{5,3},{7,1},{8,14},{10,12},{12... | collective-permute-start | bytes 393224 | tf_op jit(solution)/shard_map/ppermute | solution.py:229
  26.0 0.5 %collective-permute-start.12 = (bf16[2,128,256]{2,1,0:T(8,128)(2,1)S(1)}, bf16[2,128,256]{2,1,0:T(8,128)(2,1)S(1)}, u32[]{:S(2)}, u32[]{:S(2)}) collective-permute-start(bf16[2,128,256]{2,1,0:T(8,128)(2,1)S(1)} %get-tuple-element.34), channel_id=1, source_target_pairs={{0,4},{2,6},{4,0},{6,2},{1,5},{3,7},{5,1},{7,3},{8,12},{10,14},{12... | collective-permute-start | bytes 393224 | tf_op jit(solution)/shard_map/ppermute | solution.py:229
  26.5 0.5 %collective-permute-start.13 = (bf16[2,128,256]{2,1,0:T(8,128)(2,1)S(1)}, bf16[2,128,256]{2,1,0:T(8,128)(2,1)S(1)}, u32[]{:S(2)}, u32[]{:S(2)}) collective-permute-start(bf16[2,128,256]{2,1,0:T(8,128)(2,1)S(1)} %get-tuple-element.35), channel_id=1, source_target_pairs={{0,2},{2,0},{4,6},{6,4},{1,3},{3,1},{5,7},{7,5},{8,10},{10,8},{12,... | collective-permute-start | bytes 393224 | tf_op jit(solution)/shard_map/ppermute | solution.py:229
  27.1 3.6 %collective-permute-done.11.refs_0_ = bf16[2,128,256]{2,1,0:T(8,128)(2,1)S(1)} collective-permute-done((bf16[2,128,256]{2,1,0:T(8,128)(2,1)S(1)}, bf16[2,128,256]{2,1,0:T(8,128)(2,1)S(1)}, u32[]{:S(2)}, u32[]{:S(2)}) %collective-permute-start.11) | collective-permute-done | bytes 131104 | tf_op jit(solution)/shard_map/ppermute | solution.py:229
  30.7 2.5 %collective-permute-done.12.refs_1_ = bf16[2,128,256]{2,1,0:T(8,128)(2,1)S(1)} collective-permute-done((bf16[2,128,256]{2,1,0:T(8,128)(2,1)S(1)}, bf16[2,128,256]{2,1,0:T(8,128)(2,1)S(1)}, u32[]{:S(2)}, u32[]{:S(2)}) %collective-permute-start.12) | collective-permute-done | bytes 131104 | tf_op jit(solution)/shard_map/ppermute | solution.py:229
  33.2 0.1 collective-permute-done.13.refs_2_
  33.3 0.8 %shard_map.68 = bf16[8,128,256]{2,1,0:T(8,128)(2,1)} custom-call(bf16[2,128,256]{2,1,0:T(8,128)(2,1)S(1)} %collective-permute-done.11.refs_0_, bf16[2,128,256]{2,1,0:T(8,128)(2,1)S(1)} %collective-permute-done.12.refs_1_, bf16[2,128,256]{2,1,0:T(8,128)(2,1)S(1)} %collective-permute-done.13.refs_2_, bf16[2,128,256]{2,1,0:T(8,128)(2,1)S(1)} %get-tuple-element.36.refs_3_), custom_call_target="tpu_custom_call" | custom-call | tf_op jit(solution)/shard_map/pallas_call | solution.py:218
Async XLA Ops:
  1.7 9.3 %collective-permute-start.5 = (bf16[784,128]{1,0:T(8,128)(2,1)}, bf16[784,128]{1,0:T(8,128)(2,1)S(1)}, u32[]{:S(2)}, u32[]{:S(2)}) collective-permute-start(bf16[784,128]{1,0:T(8,128)(2,1)} %get-tuple-element.29.refs_0_), channel_id=1, source_target_pairs={{0,8},{8,24},{24,16},{16,0},{1,9},{9,25},{25,17},{17,1},{2,10},{10... | collective-permute-start | bytes 602120 | tf_op jit(solution)/shard_map/ppermute | solution.py:254
  4.8 11.4 %copy-start.2 = (s32[16,2]{0,1:T(2,128)S(1)}, s32[16,2]{0,1:T(2,128)}, u32[]{:S(2)}) copy-start(s32[16,2]{0,1:T(2,128)} %param.10) | copy-start | bytes 388
  4.8 12.7 %collective-permute-start = (bf16[1,128,256]{2,1,0:T(8,128)(2,1)}, bf16[1,128,256]{2,1,0:T(8,128)(2,1)S(1)}, u32[]{:S(2)}, u32[]{:S(2)}) collective-permute-start(bf16[1,128,256]{2,1,0:T(8,128)(2,1)} %get-tuple-element.25), channel_id=1, source_target_pairs={{0,2},{2,0},{4,6},{6,4},{1,3},{3,1},{5,7},{7,5},{8,10},{10,8},{12,... | collective-permute-start | bytes 196616 | tf_op jit(solution)/shard_map/ppermute | solution.py:229
  6.3 11.2 %collective-permute-start.1 = (bf16[1,128,256]{2,1,0:T(8,128)(2,1)}, bf16[1,128,256]{2,1,0:T(8,128)(2,1)S(1)}, u32[]{:S(2)}, u32[]{:S(2)}) collective-permute-start(bf16[1,128,256]{2,1,0:T(8,128)(2,1)} %get-tuple-element.25), channel_id=1, source_target_pairs={{0,4},{2,6},{4,0},{6,2},{1,5},{3,7},{5,1},{7,3},{8,12},{10,14},{12... | collective-permute-start | bytes 196616 | tf_op jit(solution)/shard_map/ppermute | solution.py:229
  7.8 9.7 %collective-permute-start.2 = (bf16[1,128,256]{2,1,0:T(8,128)(2,1)}, bf16[1,128,256]{2,1,0:T(8,128)(2,1)S(1)}, u32[]{:S(2)}, u32[]{:S(2)}) collective-permute-start(bf16[1,128,256]{2,1,0:T(8,128)(2,1)} %get-tuple-element.25), channel_id=1, source_target_pairs={{0,6},{2,4},{4,2},{6,0},{1,7},{3,5},{5,3},{7,1},{8,14},{10,12},{12... | collective-permute-start | bytes 196616 | tf_op jit(solution)/shard_map/ppermute | solution.py:229
  8.3 10.8 %collective-permute-start.7 = (bf16[784,128]{1,0:T(8,128)(2,1)}, bf16[784,128]{1,0:T(8,128)(2,1)S(1)}, u32[]{:S(2)}, u32[]{:S(2)}) collective-permute-start(bf16[784,128]{1,0:T(8,128)(2,1)} %get-tuple-element.29.refs_0_), channel_id=1, source_target_pairs={{0,16},{8,0},{24,8},{16,24},{1,17},{9,1},{25,9},{17,25},{2,18},{10... | collective-permute-start | bytes 602120 | tf_op jit(solution)/shard_map/ppermute | solution.py:254
  11.0 10.3 %collective-permute-start.9 = (bf16[784,128]{1,0:T(8,128)(2,1)S(1)}, bf16[784,128]{1,0:T(8,128)(2,1)S(1)}, u32[]{:S(2)}, u32[]{:S(2)}) collective-permute-start(bf16[784,128]{1,0:T(8,128)(2,1)S(1)} %collective-permute-done.5.refs_2_), channel_id=1, source_target_pairs={{0,8},{8,24},{24,16},{16,0},{1,9},{9,25},{25,17},{17,1},{2,10},{10... | collective-permute-start | bytes 602120 | tf_op jit(solution)/shard_map/ppermute | solution.py:254
  16.2 0.7 %copy-start.1 = (s32[1,2,8]{2,1,0:T(2,128)S(1)}, s32[1,2,8]{2,1,0:T(2,128)}, u32[]{:S(2)}) copy-start(s32[1,2,8]{2,1,0:T(2,128)} %param.11) | copy-start | bytes 196
  17.5 1.0 %copy-start = (bf16[784,128]{1,0:T(8,128)(2,1)S(1)}, bf16[784,128]{1,0:T(8,128)(2,1)}, u32[]{:S(2)}) copy-start(bf16[784,128]{1,0:T(8,128)(2,1)} %get-tuple-element.29.refs_0_) | copy-start | bytes 602116
  18.4 2.9 %collective-permute-start.3 = (bf16[4,1,128,256]{3,2,1,0:T(8,128)(2,1)S(1)}, bf16[4,1,128,256]{3,2,1,0:T(8,128)(2,1)S(1)}, u32[]{:S(2)}, u32[]{:S(2)}) collective-permute-start(bf16[4,1,128,256]{3,2,1,0:T(8,128)(2,1)S(1)} %pad_maximum_fusion.slab_ref), channel_id=1, source_target_pairs={{0,1},{1,0},{2,3},{3,2},{4,5},{5,4},{6,7},{7,6},{8,9},{9,8},{10,11... | collective-permute-start | bytes 786440 | tf_op jit(solution)/shard_map/ppermute | solution.py:229
  18.5 2.8 %collective-permute-start.4 = (bf16[784,128]{1,0:T(8,128)(2,1)S(1)}, bf16[784,128]{1,0:T(8,128)(2,1)S(1)}, u32[]{:S(2)}, u32[]{:S(2)}) collective-permute-start(bf16[784,128]{1,0:T(8,128)(2,1)S(1)} %copy-done), channel_id=1, source_target_pairs={{0,1},{1,0},{2,3},{3,2},{4,5},{5,4},{6,7},{7,6},{8,9},{9,8},{10,11... | collective-permute-start | bytes 602120 | tf_op jit(solution)/shard_map/ppermute | solution.py:229
  19.0 2.3 %collective-permute-start.6 = (bf16[784,128]{1,0:T(8,128)(2,1)S(1)}, bf16[784,128]{1,0:T(8,128)(2,1)S(1)}, u32[]{:S(2)}, u32[]{:S(2)}) collective-permute-start(bf16[784,128]{1,0:T(8,128)(2,1)S(1)} %collective-permute-done.5.refs_2_), channel_id=1, source_target_pairs={{0,1},{1,0},{2,3},{3,2},{4,5},{5,4},{6,7},{7,6},{8,9},{9,8},{10,11... | collective-permute-start | bytes 602120 | tf_op jit(solution)/shard_map/ppermute | solution.py:229
  19.1 2.3 %collective-permute-start.8 = (bf16[784,128]{1,0:T(8,128)(2,1)S(1)}, bf16[784,128]{1,0:T(8,128)(2,1)S(1)}, u32[]{:S(2)}, u32[]{:S(2)}) collective-permute-start(bf16[784,128]{1,0:T(8,128)(2,1)S(1)} %collective-permute-done.7.refs_4_), channel_id=1, source_target_pairs={{0,1},{1,0},{2,3},{3,2},{4,5},{5,4},{6,7},{7,6},{8,9},{9,8},{10,11... | collective-permute-start | bytes 602120 | tf_op jit(solution)/shard_map/ppermute | solution.py:229
  21.3 1.6 %collective-permute-start.10 = (bf16[784,128]{1,0:T(8,128)(2,1)S(1)}, bf16[784,128]{1,0:T(8,128)(2,1)S(1)}, u32[]{:S(2)}, u32[]{:S(2)}) collective-permute-start(bf16[784,128]{1,0:T(8,128)(2,1)S(1)} %collective-permute-done.9.refs_0_), channel_id=1, source_target_pairs={{0,1},{1,0},{2,3},{3,2},{4,5},{5,4},{6,7},{7,6},{8,9},{9,8},{10,11... | collective-permute-start | bytes 602120 | tf_op jit(solution)/shard_map/ppermute | solution.py:229
  23.5 7.2 %collective-permute-start.11 = (bf16[2,128,256]{2,1,0:T(8,128)(2,1)S(1)}, bf16[2,128,256]{2,1,0:T(8,128)(2,1)S(1)}, u32[]{:S(2)}, u32[]{:S(2)}) collective-permute-start(bf16[2,128,256]{2,1,0:T(8,128)(2,1)S(1)} %get-tuple-element.33), channel_id=1, source_target_pairs={{0,6},{2,4},{4,2},{6,0},{1,7},{3,5},{5,3},{7,1},{8,14},{10,12},{12... | collective-permute-start | bytes 393224 | tf_op jit(solution)/shard_map/ppermute | solution.py:229
  26.0 7.2 %collective-permute-start.12 = (bf16[2,128,256]{2,1,0:T(8,128)(2,1)S(1)}, bf16[2,128,256]{2,1,0:T(8,128)(2,1)S(1)}, u32[]{:S(2)}, u32[]{:S(2)}) collective-permute-start(bf16[2,128,256]{2,1,0:T(8,128)(2,1)S(1)} %get-tuple-element.34), channel_id=1, source_target_pairs={{0,4},{2,6},{4,0},{6,2},{1,5},{3,7},{5,1},{7,3},{8,12},{10,14},{12... | collective-permute-start | bytes 393224 | tf_op jit(solution)/shard_map/ppermute | solution.py:229
  26.5 6.8 %collective-permute-start.13 = (bf16[2,128,256]{2,1,0:T(8,128)(2,1)S(1)}, bf16[2,128,256]{2,1,0:T(8,128)(2,1)S(1)}, u32[]{:S(2)}, u32[]{:S(2)}) collective-permute-start(bf16[2,128,256]{2,1,0:T(8,128)(2,1)S(1)} %get-tuple-element.35), channel_id=1, source_target_pairs={{0,2},{2,0},{4,6},{6,4},{1,3},{3,1},{5,7},{7,5},{8,10},{10,8},{12,... | collective-permute-start | bytes 393224 | tf_op jit(solution)/shard_map/ppermute | solution.py:229

commit v4 on v3

--- a/solution.py
+++ b/solution.py
@@ -16,7 +16,7 @@
 
 def turn_of(source, here, row_count):
     spots = [jnp.where(n % 2 == 1, n // 2 + 1, jnp.where(n == 0, 0, row_count - n // 2)) for n in (here, source)]
-    ahead = (spots[0] - spots[1]) & (row_count - 1)
+    ahead = (spots[1] - spots[0]) & (row_count - 1)
     return jnp.where(ahead == 0, 0, jnp.where(ahead <= row_count // 2, 2 * ahead - 1, 2 * (row_count - ahead)))
 
 
@@ -233,7 +233,7 @@
     local_rows, _, block_size, width = b_blocks.shape
     slot_count = a_rows.shape[3]
     row_count, col_count, layer_count = (lax.axis_size(name) for name in ("row", "col", "layer"))
-    ring = list(range(0, row_count, 2))[:1] + list(range(1, row_count, 2)) + list(range(row_count - 2, 0, -2))
+    ring = list(range(0, row_count, 2)) + list(range(row_count - 1, 0, -2))
     turns = [(n // 2 + 1) * (1 if n % 2 == 0 else -1) for n in range(row_count - 1)]
     turns = [0] + sorted(turns, key=abs)
 

time: 34.3 us -> 33.6 us (0.980)
  starting transfers between devices: 17.4 us -> 15.1 us
  waiting for transfers between devices: 9.7 us -> 11.4 us
    ppermute x3, starting transfers between devices: 9.32 us -> 7.37 us  [shards(): lax.ppermute(held[turn - step], 'row', [(name, ring[(at + step) % row_cou...]
    ppermute x3, waiting for transfers between devices: 3.46 us -> 5.17 us  [shards(): lax.ppermute(held[turn - step], 'row', [(name, ring[(at + step) % row_cou...]
    ppermute x11, starting transfers between devices: 8.12 us -> 7.69 us  [swap(): lax.ppermute(value, axis, [(i, i ^ by) for i in range(lax.axis_size(axis))])]
  transfers between devices with their start and end apart: 14 -> 14, of which waited for: 5 -> 6; matrix products, arithmetic and copies ran while one was open for 3% -> 3% of each run, Pallas kernels for 6% -> 6%
where the time goes in v4:
time: 33.6 us; the launch traced here: 33.5 us
  starting transfers between devices  15.1 us (45%)
  waiting for transfers between devices  11.4 us (34%)
  Pallas kernels  5.27 us (16%)
  other arithmetic  0.91 us (3%)
  local copies, waits for them, and re-layouts  0.69 us (2%)
    ppermute x11, starting transfers between devices, swap(): lax.ppermute(value, axis, [(i, i ^ by) for i in range(lax.axis_size(axis))])  7.69 us
    ppermute x3, starting transfers between devices, shards(): lax.ppermute(held[turn - step], 'row', [(name, ring[(at + step) % row_cou...  7.37 us
    ppermute x11, waiting for transfers between devices, swap(): lax.ppermute(value, axis, [(i, i ^ by) for i in range(lax.axis_size(axis))])  6.24 us
    ppermute x3, waiting for transfers between devices, shards(): lax.ppermute(held[turn - step], 'row', [(name, ring[(at + step) % row_cou...  5.17 us
    pallas_call x1, Pallas kernels, prepare(): pl.pallas_call(prepare_kernel, out_shape=(jax.ShapeDtypeStruct((rows + TA...  1.7 us
    pallas_call x1, Pallas kernels, early(): pl.pallas_call(functools.partial(early_kernel, slot_count), out_shape=(ja...  1.54 us
    another operation x1, other arithmetic, shards(): slabs = jnp.stack(slabs)  0.91 us
    pallas_call x1, Pallas kernels, collect(): pl.pallas_call(collect_kernel, out_shape=jax.ShapeDtypeStruct((count * le...  0.82 us
  transfers between devices with their start and end apart: 14, of which 6 were waited for; matrix products, arithmetic and copies ran while one was open for 3% of the time, Pallas kernels for 6%

profile of v4, /device:TPU:0, one launch (start us, length us, event | category | flops | bytes accessed | tf_op | source)
XLA Modules:
  0.0 33.5 jit_solution(9330539865927768212)
XLA Ops:
  0.0 1.7 %shard_map.65 = (bf16[784,128]{1,0:T(8,128)(2,1)}, bf16[1,128,256]{2,1,0:T(8,128)(2,1)}) custom-call(bf16[768,128]{1,0:T(8,128)(2,1)} %bitcast.13, s32[1,6]{1,0:T(1,128)} %bitcast.19, bf16[1,128,256]{2,1,0:T(8,128)(2,1)} %bitcast.14, s32[1,2]{1,0:T(1,128)} %bitcast.20), custom_call_target="tpu_custom_call" | custom-call | tf_op jit(solution)/shard_map/pallas_call | solution.py:59
  1.7 4.1 %collective-permute-start.5 = (bf16[784,128]{1,0:T(8,128)(2,1)}, bf16[784,128]{1,0:T(8,128)(2,1)S(1)}, u32[]{:S(2)}, u32[]{:S(2)}) collective-permute-start(bf16[784,128]{1,0:T(8,128)(2,1)} %get-tuple-element.29.refs_0_), channel_id=1, source_target_pairs={{0,16},{16,24},{24,8},{8,0},{1,17},{17,25},{25,9},{9,1},{2,18},{18... | collective-permute-start | bytes 602120 | tf_op jit(solution)/shard_map/ppermute | solution.py:254
  5.8 0.0 copy-start.2
  5.8 1.5 %collective-permute-start = (bf16[1,128,256]{2,1,0:T(8,128)(2,1)}, bf16[1,128,256]{2,1,0:T(8,128)(2,1)S(1)}, u32[]{:S(2)}, u32[]{:S(2)}) collective-permute-start(bf16[1,128,256]{2,1,0:T(8,128)(2,1)} %get-tuple-element.25), channel_id=1, source_target_pairs={{0,2},{2,0},{4,6},{6,4},{1,3},{3,1},{5,7},{7,5},{8,10},{10,8},{12,... | collective-permute-start | bytes 196616 | tf_op jit(solution)/shard_map/ppermute | solution.py:229
  7.3 1.5 %collective-permute-start.1 = (bf16[1,128,256]{2,1,0:T(8,128)(2,1)}, bf16[1,128,256]{2,1,0:T(8,128)(2,1)S(1)}, u32[]{:S(2)}, u32[]{:S(2)}) collective-permute-start(bf16[1,128,256]{2,1,0:T(8,128)(2,1)} %get-tuple-element.25), channel_id=1, source_target_pairs={{0,4},{2,6},{4,0},{6,2},{1,5},{3,7},{5,1},{7,3},{8,12},{10,14},{12... | collective-permute-start | bytes 196616 | tf_op jit(solution)/shard_map/ppermute | solution.py:229
  8.8 0.5 %collective-permute-start.2 = (bf16[1,128,256]{2,1,0:T(8,128)(2,1)}, bf16[1,128,256]{2,1,0:T(8,128)(2,1)S(1)}, u32[]{:S(2)}, u32[]{:S(2)}) collective-permute-start(bf16[1,128,256]{2,1,0:T(8,128)(2,1)} %get-tuple-element.25), channel_id=1, source_target_pairs={{0,6},{2,4},{4,2},{6,0},{1,7},{3,5},{5,3},{7,1},{8,14},{10,12},{12... | collective-permute-start | bytes 196616 | tf_op jit(solution)/shard_map/ppermute | solution.py:229
  9.3 0.0 collective-permute-start.7
  9.3 2.2 %collective-permute-done.5.refs_2_ = bf16[784,128]{1,0:T(8,128)(2,1)S(1)} collective-permute-done((bf16[784,128]{1,0:T(8,128)(2,1)}, bf16[784,128]{1,0:T(8,128)(2,1)S(1)}, u32[]{:S(2)}, u32[]{:S(2)}) %collective-permute-start.5) | collective-permute-done | bytes 200736 | tf_op jit(solution)/shard_map/ppermute | solution.py:254
  11.5 3.3 %collective-permute-start.9 = (bf16[784,128]{1,0:T(8,128)(2,1)S(1)}, bf16[784,128]{1,0:T(8,128)(2,1)S(1)}, u32[]{:S(2)}, u32[]{:S(2)}) collective-permute-start(bf16[784,128]{1,0:T(8,128)(2,1)S(1)} %collective-permute-done.5.refs_2_), channel_id=1, source_target_pairs={{0,16},{16,24},{24,8},{8,0},{1,17},{17,25},{25,9},{9,1},{2,18},{18... | collective-permute-start | bytes 602120 | tf_op jit(solution)/shard_map/ppermute | solution.py:254
  14.8 0.0 copy-start.1
  14.8 0.0 copy-done.2
  14.8 0.7 %copy-done.1 = s32[1,2,8]{2,1,0:T(2,128)S(1)} copy-done((s32[1,2,8]{2,1,0:T(2,128)S(1)}, s32[1,2,8]{2,1,0:T(2,128)}, u32[]{:S(2)}) %copy-start.1) | copy-done | bytes 88
  15.5 0.6 %shard_map.64 = (f32[8,128]{1,0:T(8,128)S(1)}, f32[8,256]{1,0:T(8,128)S(1)}) custom-call(s32[2,8]{1,0:T(2,128)S(1)} %bitcast.11, s32[2,16]{1,0:T(2,128)S(1)} %bitcast.12), custom_call_target="tpu_custom_call" | custom-call | tf_op jit(solution)/shard_map/pallas_call | solution.py:96
  16.1 0.0 collective-permute-done
  16.1 0.0 collective-permute-done.1
  16.1 0.0 collective-permute-done.2
  16.1 0.0 copy-start
  16.1 0.9 %pad_maximum_fusion.slab_ref = bf16[4,1,128,256]{3,2,1,0:T(8,128)(2,1)S(1)} fusion(bf16[1,1,128,256]{3,2,1,0:T(8,128)(2,1)S(1)} %bitcast.18, bf16[1,1,128,256]{3,2,1,0:T(8,128)(2,1)S(1)} %bitcast.17, bf16[1,1,128,256]{3,2,1,0:T(8,128)(2,1)S(1)} %bitcast.16, bf16[1,1,128,256]{3,2,1,0:T(8,128)(2,1)} %bitcast.15), kind=kLoop, calls=%fused_computation | loop fusion | flops 393216 | bytes 524288 | tf_op jit(solution)/shard_map/stack | solution.py:249
  17.0 0.1 collective-permute-start.3
  17.1 0.0 copy-done
  17.1 0.5 %collective-permute-start.4 = (bf16[784,128]{1,0:T(8,128)(2,1)S(1)}, bf16[784,128]{1,0:T(8,128)(2,1)S(1)}, u32[]{:S(2)}, u32[]{:S(2)}) collective-permute-start(bf16[784,128]{1,0:T(8,128)(2,1)S(1)} %copy-done), channel_id=1, source_target_pairs={{0,1},{1,0},{2,3},{3,2},{4,5},{5,4},{6,7},{7,6},{8,9},{9,8},{10,11... | collective-permute-start | bytes 602120 | tf_op jit(solution)/shard_map/ppermute | solution.py:229
  17.6 0.1 collective-permute-start.6
  17.7 0.6 %collective-permute-done.7.refs_4_ = bf16[784,128]{1,0:T(8,128)(2,1)S(1)} collective-permute-done((bf16[784,128]{1,0:T(8,128)(2,1)}, bf16[784,128]{1,0:T(8,128)(2,1)S(1)}, u32[]{:S(2)}, u32[]{:S(2)}) %collective-permute-start.7) | collective-permute-done | bytes 200736 | tf_op jit(solution)/shard_map/ppermute | solution.py:254
  18.3 0.0 collective-permute-start.8
  18.3 2.4 %collective-permute-done.9.refs_0_ = bf16[784,128]{1,0:T(8,128)(2,1)S(1)} collective-permute-done((bf16[784,128]{1,0:T(8,128)(2,1)S(1)}, bf16[784,128]{1,0:T(8,128)(2,1)S(1)}, u32[]{:S(2)}, u32[]{:S(2)}) %collective-permute-start.9) | collective-permute-done | bytes 200736 | tf_op jit(solution)/shard_map/ppermute | solution.py:254
  20.7 0.0 collective-permute-start.10
  20.7 0.0 collective-permute-done.4.refs_1_
  20.7 0.0 collective-permute-done.3.twin_ref
  20.7 0.0 collective-permute-done.6.refs_3_
  20.7 0.0 collective-permute-done.8.refs_5_
  20.7 1.5 %shard_map.66 = (f32[8,128,256]{2,1,0:T(8,128)S(1)}, bf16[256,256]{1,0:T(8,128)(2,1)S(1)}) custom-call(f32[8,128]{1,0:T(8,128)S(1)} %get-tuple-element.24.chosen_ref, bf16[4,1,128,256]{3,2,1,0:T(8,128)(2,1)S(1)} %pad_maximum_fusion.slab_ref, bf16[4,1,128,256]{3,2,1,0:T(8,128)(2,1)S(1)} %collective-permute-done.3.twin_ref, bf16[784,128]{1,0:T(8,128)(2,1)S(1)} %copy-done, ...), custom_call_target="tpu_custom_call" | custom-call | tf_op jit(solution)/shard_map/pallas_call | solution.py:164
  22.2 0.0 collective-permute-done.10.refs_1_
  22.2 0.6 %shard_map.67 = (bf16[2,128,256]{2,1,0:T(8,128)(2,1)S(1)}, bf16[2,128,256]{2,1,0:T(8,128)(2,1)S(1)}, bf16[2,128,256]{2,1,0:T(8,128)(2,1)S(1)}, bf16[2,128,256]{2,1,0:T(8,128)(2,1)S(1)}) custom-call(f32[8,128,256]{2,1,0:T(8,128)S(1)} %get-tuple-element.30.total_ref, bf16[256,256]{1,0:T(8,128)(2,1)S(1)} %get-tuple-element.31.last_ref, ...), custom_call_target="tpu_custom_call" | custom-call | tf_op jit(solution)/shard_map/pallas_call | solution.py:194
  22.9 2.5 %collective-permute-start.11 = (bf16[2,128,256]{2,1,0:T(8,128)(2,1)S(1)}, bf16[2,128,256]{2,1,0:T(8,128)(2,1)S(1)}, u32[]{:S(2)}, u32[]{:S(2)}) collective-permute-start(bf16[2,128,256]{2,1,0:T(8,128)(2,1)S(1)} %get-tuple-element.33), channel_id=1, source_target_pairs={{0,6},{2,4},{4,2},{6,0},{1,7},{3,5},{5,3},{7,1},{8,14},{10,12},{12... | collective-permute-start | bytes 393224 | tf_op jit(solution)/shard_map/ppermute | solution.py:229
  25.4 0.5 %collective-permute-start.12 = (bf16[2,128,256]{2,1,0:T(8,128)(2,1)S(1)}, bf16[2,128,256]{2,1,0:T(8,128)(2,1)S(1)}, u32[]{:S(2)}, u32[]{:S(2)}) collective-permute-start(bf16[2,128,256]{2,1,0:T(8,128)(2,1)S(1)} %get-tuple-element.34), channel_id=1, source_target_pairs={{0,4},{2,6},{4,0},{6,2},{1,5},{3,7},{5,1},{7,3},{8,12},{10,14},{12... | collective-permute-start | bytes 393224 | tf_op jit(solution)/shard_map/ppermute | solution.py:229
  25.9 0.5 %collective-permute-start.13 = (bf16[2,128,256]{2,1,0:T(8,128)(2,1)S(1)}, bf16[2,128,256]{2,1,0:T(8,128)(2,1)S(1)}, u32[]{:S(2)}, u32[]{:S(2)}) collective-permute-start(bf16[2,128,256]{2,1,0:T(8,128)(2,1)S(1)} %get-tuple-element.35), channel_id=1, source_target_pairs={{0,2},{2,0},{4,6},{6,4},{1,3},{3,1},{5,7},{7,5},{8,10},{10,8},{12,... | collective-permute-start | bytes 393224 | tf_op jit(solution)/shard_map/ppermute | solution.py:229
  26.4 3.6 %collective-permute-done.11.refs_0_ = bf16[2,128,256]{2,1,0:T(8,128)(2,1)S(1)} collective-permute-done((bf16[2,128,256]{2,1,0:T(8,128)(2,1)S(1)}, bf16[2,128,256]{2,1,0:T(8,128)(2,1)S(1)}, u32[]{:S(2)}, u32[]{:S(2)}) %collective-permute-start.11) | collective-permute-done | bytes 131104 | tf_op jit(solution)/shard_map/ppermute | solution.py:229
  30.0 2.5 %collective-permute-done.12.refs_1_ = bf16[2,128,256]{2,1,0:T(8,128)(2,1)S(1)} collective-permute-done((bf16[2,128,256]{2,1,0:T(8,128)(2,1)S(1)}, bf16[2,128,256]{2,1,0:T(8,128)(2,1)S(1)}, u32[]{:S(2)}, u32[]{:S(2)}) %collective-permute-start.12) | collective-permute-done | bytes 131104 | tf_op jit(solution)/shard_map/ppermute | solution.py:229
  32.5 0.1 collective-permute-done.13.refs_2_
  32.6 0.8 %shard_map.68 = bf16[8,128,256]{2,1,0:T(8,128)(2,1)} custom-call(bf16[2,128,256]{2,1,0:T(8,128)(2,1)S(1)} %collective-permute-done.11.refs_0_, bf16[2,128,256]{2,1,0:T(8,128)(2,1)S(1)} %collective-permute-done.12.refs_1_, bf16[2,128,256]{2,1,0:T(8,128)(2,1)S(1)} %collective-permute-done.13.refs_2_, bf16[2,128,256]{2,1,0:T(8,128)(2,1)S(1)} %get-tuple-element.36.refs_3_), custom_call_target="tpu_custom_call" | custom-call | tf_op jit(solution)/shard_map/pallas_call | solution.py:218
Async XLA Ops:
  1.7 9.8 %collective-permute-start.5 = (bf16[784,128]{1,0:T(8,128)(2,1)}, bf16[784,128]{1,0:T(8,128)(2,1)S(1)}, u32[]{:S(2)}, u32[]{:S(2)}) collective-permute-start(bf16[784,128]{1,0:T(8,128)(2,1)} %get-tuple-element.29.refs_0_), channel_id=1, source_target_pairs={{0,16},{16,24},{24,8},{8,0},{1,17},{17,25},{25,9},{9,1},{2,18},{18... | collective-permute-start | bytes 602120 | tf_op jit(solution)/shard_map/ppermute | solution.py:254
  5.8 9.0 %copy-start.2 = (s32[16,2]{0,1:T(2,128)S(1)}, s32[16,2]{0,1:T(2,128)}, u32[]{:S(2)}) copy-start(s32[16,2]{0,1:T(2,128)} %param.10) | copy-start | bytes 388
  5.8 10.3 %collective-permute-start = (bf16[1,128,256]{2,1,0:T(8,128)(2,1)}, bf16[1,128,256]{2,1,0:T(8,128)(2,1)S(1)}, u32[]{:S(2)}, u32[]{:S(2)}) collective-permute-start(bf16[1,128,256]{2,1,0:T(8,128)(2,1)} %get-tuple-element.25), channel_id=1, source_target_pairs={{0,2},{2,0},{4,6},{6,4},{1,3},{3,1},{5,7},{7,5},{8,10},{10,8},{12,... | collective-permute-start | bytes 196616 | tf_op jit(solution)/shard_map/ppermute | solution.py:229
  7.3 8.8 %collective-permute-start.1 = (bf16[1,128,256]{2,1,0:T(8,128)(2,1)}, bf16[1,128,256]{2,1,0:T(8,128)(2,1)S(1)}, u32[]{:S(2)}, u32[]{:S(2)}) collective-permute-start(bf16[1,128,256]{2,1,0:T(8,128)(2,1)} %get-tuple-element.25), channel_id=1, source_target_pairs={{0,4},{2,6},{4,0},{6,2},{1,5},{3,7},{5,1},{7,3},{8,12},{10,14},{12... | collective-permute-start | bytes 196616 | tf_op jit(solution)/shard_map/ppermute | solution.py:229
  8.8 7.3 %collective-permute-start.2 = (bf16[1,128,256]{2,1,0:T(8,128)(2,1)}, bf16[1,128,256]{2,1,0:T(8,128)(2,1)S(1)}, u32[]{:S(2)}, u32[]{:S(2)}) collective-permute-start(bf16[1,128,256]{2,1,0:T(8,128)(2,1)} %get-tuple-element.25), channel_id=1, source_target_pairs={{0,6},{2,4},{4,2},{6,0},{1,7},{3,5},{5,3},{7,1},{8,14},{10,12},{12... | collective-permute-start | bytes 196616 | tf_op jit(solution)/shard_map/ppermute | solution.py:229
  9.3 9.0 %collective-permute-start.7 = (bf16[784,128]{1,0:T(8,128)(2,1)}, bf16[784,128]{1,0:T(8,128)(2,1)S(1)}, u32[]{:S(2)}, u32[]{:S(2)}) collective-permute-start(bf16[784,128]{1,0:T(8,128)(2,1)} %get-tuple-element.29.refs_0_), channel_id=1, source_target_pairs={{0,8},{16,0},{24,16},{8,24},{1,9},{17,1},{25,17},{9,25},{2,10},{18... | collective-permute-start | bytes 602120 | tf_op jit(solution)/shard_map/ppermute | solution.py:254
  11.5 9.2 %collective-permute-start.9 = (bf16[784,128]{1,0:T(8,128)(2,1)S(1)}, bf16[784,128]{1,0:T(8,128)(2,1)S(1)}, u32[]{:S(2)}, u32[]{:S(2)}) collective-permute-start(bf16[784,128]{1,0:T(8,128)(2,1)S(1)} %collective-permute-done.5.refs_2_), channel_id=1, source_target_pairs={{0,16},{16,24},{24,8},{8,0},{1,17},{17,25},{25,9},{9,1},{2,18},{18... | collective-permute-start | bytes 602120 | tf_op jit(solution)/shard_map/ppermute | solution.py:254
  14.8 0.7 %copy-start.1 = (s32[1,2,8]{2,1,0:T(2,128)S(1)}, s32[1,2,8]{2,1,0:T(2,128)}, u32[]{:S(2)}) copy-start(s32[1,2,8]{2,1,0:T(2,128)} %param.11) | copy-start | bytes 196
  16.1 1.0 %copy-start = (bf16[784,128]{1,0:T(8,128)(2,1)S(1)}, bf16[784,128]{1,0:T(8,128)(2,1)}, u32[]{:S(2)}) copy-start(bf16[784,128]{1,0:T(8,128)(2,1)} %get-tuple-element.29.refs_0_) | copy-start | bytes 602116
  17.0 3.6 %collective-permute-start.3 = (bf16[4,1,128,256]{3,2,1,0:T(8,128)(2,1)S(1)}, bf16[4,1,128,256]{3,2,1,0:T(8,128)(2,1)S(1)}, u32[]{:S(2)}, u32[]{:S(2)}) collective-permute-start(bf16[4,1,128,256]{3,2,1,0:T(8,128)(2,1)S(1)} %pad_maximum_fusion.slab_ref), channel_id=1, source_target_pairs={{0,1},{1,0},{2,3},{3,2},{4,5},{5,4},{6,7},{7,6},{8,9},{9,8},{10,11... | collective-permute-start | bytes 786440 | tf_op jit(solution)/shard_map/ppermute | solution.py:229
  17.1 3.5 %collective-permute-start.4 = (bf16[784,128]{1,0:T(8,128)(2,1)S(1)}, bf16[784,128]{1,0:T(8,128)(2,1)S(1)}, u32[]{:S(2)}, u32[]{:S(2)}) collective-permute-start(bf16[784,128]{1,0:T(8,128)(2,1)S(1)} %copy-done), channel_id=1, source_target_pairs={{0,1},{1,0},{2,3},{3,2},{4,5},{5,4},{6,7},{7,6},{8,9},{9,8},{10,11... | collective-permute-start | bytes 602120 | tf_op jit(solution)/shard_map/ppermute | solution.py:229
  17.6 3.1 %collective-permute-start.6 = (bf16[784,128]{1,0:T(8,128)(2,1)S(1)}, bf16[784,128]{1,0:T(8,128)(2,1)S(1)}, u32[]{:S(2)}, u32[]{:S(2)}) collective-permute-start(bf16[784,128]{1,0:T(8,128)(2,1)S(1)} %collective-permute-done.5.refs_2_), channel_id=1, source_target_pairs={{0,1},{1,0},{2,3},{3,2},{4,5},{5,4},{6,7},{7,6},{8,9},{9,8},{10,11... | collective-permute-start | bytes 602120 | tf_op jit(solution)/shard_map/ppermute | solution.py:229
  18.3 2.4 %collective-permute-start.8 = (bf16[784,128]{1,0:T(8,128)(2,1)S(1)}, bf16[784,128]{1,0:T(8,128)(2,1)S(1)}, u32[]{:S(2)}, u32[]{:S(2)}) collective-permute-start(bf16[784,128]{1,0:T(8,128)(2,1)S(1)} %collective-permute-done.7.refs_4_), channel_id=1, source_target_pairs={{0,1},{1,0},{2,3},{3,2},{4,5},{5,4},{6,7},{7,6},{8,9},{9,8},{10,11... | collective-permute-start | bytes 602120 | tf_op jit(solution)/shard_map/ppermute | solution.py:229
  20.7 1.6 %collective-permute-start.10 = (bf16[784,128]{1,0:T(8,128)(2,1)S(1)}, bf16[784,128]{1,0:T(8,128)(2,1)S(1)}, u32[]{:S(2)}, u32[]{:S(2)}) collective-permute-start(bf16[784,128]{1,0:T(8,128)(2,1)S(1)} %collective-permute-done.9.refs_0_), channel_id=1, source_target_pairs={{0,1},{1,0},{2,3},{3,2},{4,5},{5,4},{6,7},{7,6},{8,9},{9,8},{10,11... | collective-permute-start | bytes 602120 | tf_op jit(solution)/shard_map/ppermute | solution.py:229
  22.9 7.2 %collective-permute-start.11 = (bf16[2,128,256]{2,1,0:T(8,128)(2,1)S(1)}, bf16[2,128,256]{2,1,0:T(8,128)(2,1)S(1)}, u32[]{:S(2)}, u32[]{:S(2)}) collective-permute-start(bf16[2,128,256]{2,1,0:T(8,128)(2,1)S(1)} %get-tuple-element.33), channel_id=1, source_target_pairs={{0,6},{2,4},{4,2},{6,0},{1,7},{3,5},{5,3},{7,1},{8,14},{10,12},{12... | collective-permute-start | bytes 393224 | tf_op jit(solution)/shard_map/ppermute | solution.py:229
  25.4 7.2 %collective-permute-start.12 = (bf16[2,128,256]{2,1,0:T(8,128)(2,1)S(1)}, bf16[2,128,256]{2,1,0:T(8,128)(2,1)S(1)}, u32[]{:S(2)}, u32[]{:S(2)}) collective-permute-start(bf16[2,128,256]{2,1,0:T(8,128)(2,1)S(1)} %get-tuple-element.34), channel_id=1, source_target_pairs={{0,4},{2,6},{4,0},{6,2},{1,5},{3,7},{5,1},{7,3},{8,12},{10,14},{12... | collective-permute-start | bytes 393224 | tf_op jit(solution)/shard_map/ppermute | solution.py:229
  25.9 6.8 %collective-permute-start.13 = (bf16[2,128,256]{2,1,0:T(8,128)(2,1)S(1)}, bf16[2,128,256]{2,1,0:T(8,128)(2,1)S(1)}, u32[]{:S(2)}, u32[]{:S(2)}) collective-permute-start(bf16[2,128,256]{2,1,0:T(8,128)(2,1)S(1)} %get-tuple-element.35), channel_id=1, source_target_pairs={{0,2},{2,0},{4,6},{6,4},{1,3},{3,1},{5,7},{7,5},{8,10},{10,8},{12,... | collective-permute-start | bytes 393224 | tf_op jit(solution)/shard_map/ppermute | solution.py:229

commit v5 on v4

--- a/solution.py
+++ b/solution.py
@@ -174,11 +174,11 @@
     )(chosen, slabs, twins, *pieces)
 
 
-def late_kernel(slot_count, col_count, total_ref, last_ref, chosen_ref, kept_ref, *refs):
-    piece_refs, out_refs = refs[:-col_count], refs[-col_count:]
+def late_kernel(slot_count, col_count, chips, total_ref, last_ref, chosen_ref, kept_ref, *refs):
+    piece_refs, out_refs = refs[: -len(chips)], refs[-len(chips) :]
     block_size = total_ref.shape[1]
     layer_count = total_ref.shape[0] // col_count
-    for at, out_ref in enumerate(out_refs):
+    for at, out_ref in zip(chips, out_refs):
         queries = range(at * layer_count, (at + 1) * layer_count)
         lines = pick(slot_count, piece_refs, chosen_ref, queries)
         total = jnp.dot(lines, last_ref[...], preferred_element_type=jnp.float32)
@@ -187,15 +187,15 @@
             out_ref[n] = (part * kept_ref[q : q + 1, :]).astype(out_ref.dtype)
 
 
-def late(slot_count, col_count, totals, chosen, kept, pieces):
+def late(slot_count, col_count, chips, totals, chosen, kept, pieces):
     total, last = totals
     out_count, block_size, width = total.shape
     shape = jax.ShapeDtypeStruct((out_count // col_count, block_size, width), last.dtype)
     return pl.pallas_call(
-        functools.partial(late_kernel, slot_count, col_count),
-        out_shape=[shape] * col_count,
+        functools.partial(late_kernel, slot_count, col_count, chips),
+        out_shape=[shape] * len(chips),
         in_specs=[VMEM] * (4 + len(pieces)),
-        out_specs=[VMEM] * col_count,
+        out_specs=[VMEM] * len(chips),
         compiler_params=LIMIT,
     )(total, last, chosen, kept, *pieces)
 
@@ -258,8 +258,11 @@
     pieces = [one for turn in turns for one in (held[turn], swap(held[turn], "layer", 1))]
     steps = split * layer_count
     totals = early(slot_count, len(pieces) - steps, chosen, slabs, twins, pieces[:steps])
-    parts = list(late(slot_count, col_count, totals, chosen, kept, pieces[steps:]))
-    for by in sorted(range(1, col_count), key=lambda n: -bin(n).count("1")):
+    far, final = col_count - 1, pieces[split * layer_count :]
+    parts = list(late(slot_count, col_count, (far,), totals, chosen, kept, final))
+    kept, parts[0] = lax.optimization_barrier((kept, parts[0]))
+    parts = list(late(slot_count, col_count, tuple(range(far)), totals, chosen, kept, final)) + parts
+    for by in range(far, 0, -1):
         parts[by] = swap(parts[by], "col", by)
     return collect(parts)[None]
 

time: 33.6 us -> 33.2 us (0.988)
  waiting for transfers between devices: 11.4 us -> 10.8 us
    ppermute x11, waiting for transfers between devices: 6.24 us -> 5.67 us  [swap(): lax.ppermute(value, axis, [(i, i ^ by) for i in range(lax.axis_size(axis))])]
    pallas_call x1 -> x2, Pallas kernels: 0.62 us -> 0.72 us  [late(): pl.pallas_call(functools.partial(late_kernel, slot_count, col_count, chip...]
  transfers between devices with their start and end apart: 14 -> 14, of which waited for: 6 -> 6; matrix products, arithmetic and copies ran while one was open for 3% -> 3% of each run, Pallas kernels for 6% -> 8%
where the time goes in v5:
time: 33.2 us; the launch traced here: 33 us
  starting transfers between devices  15.1 us (45%)
  waiting for transfers between devices  10.8 us (33%)
  Pallas kernels  5.38 us (16%)
  other arithmetic  0.91 us (3%)
  local copies, waits for them, and re-layouts  0.69 us (2%)
    ppermute x11, starting transfers between devices, swap(): lax.ppermute(value, axis, [(i, i ^ by) for i in range(lax.axis_size(axis))])  7.75 us
    ppermute x3, starting transfers between devices, shards(): lax.ppermute(held[turn - step], 'row', [(name, ring[(at + step) % row_cou...  7.37 us
    ppermute x11, waiting for transfers between devices, swap(): lax.ppermute(value, axis, [(i, i ^ by) for i in range(lax.axis_size(axis))])  5.67 us
    ppermute x3, waiting for transfers between devices, shards(): lax.ppermute(held[turn - step], 'row', [(name, ring[(at + step) % row_cou...  5.17 us
    pallas_call x1, Pallas kernels, prepare(): pl.pallas_call(prepare_kernel, out_shape=(jax.ShapeDtypeStruct((rows + TA...  1.7 us
    pallas_call x1, Pallas kernels, early(): pl.pallas_call(functools.partial(early_kernel, slot_count), out_shape=(ja...  1.53 us
    another operation x1, other arithmetic, shards(): slabs = jnp.stack(slabs)  0.91 us
    pallas_call x1, Pallas kernels, collect(): pl.pallas_call(collect_kernel, out_shape=jax.ShapeDtypeStruct((count * le...  0.82 us
  transfers between devices with their start and end apart: 14, of which 6 were waited for; matrix products, arithmetic and copies ran while one was open for 3% of the time, Pallas kernels for 8%

profile of v5, /device:TPU:0, one launch (start us, length us, event | category | flops | bytes accessed | tf_op | source)
XLA Modules:
  0.0 33.0 jit_solution(11690727150657547032)
XLA Ops:
  0.0 1.7 %shard_map.65 = (bf16[784,128]{1,0:T(8,128)(2,1)}, bf16[1,128,256]{2,1,0:T(8,128)(2,1)}) custom-call(bf16[768,128]{1,0:T(8,128)(2,1)} %bitcast.13, s32[1,6]{1,0:T(1,128)} %bitcast.19, bf16[1,128,256]{2,1,0:T(8,128)(2,1)} %bitcast.14, s32[1,2]{1,0:T(1,128)} %bitcast.20), custom_call_target="tpu_custom_call" | custom-call | tf_op jit(solution)/shard_map/pallas_call | solution.py:59
  1.7 4.1 %collective-permute-start.5 = (bf16[784,128]{1,0:T(8,128)(2,1)}, bf16[784,128]{1,0:T(8,128)(2,1)S(1)}, u32[]{:S(2)}, u32[]{:S(2)}) collective-permute-start(bf16[784,128]{1,0:T(8,128)(2,1)} %get-tuple-element.31.refs_0_), channel_id=1, source_target_pairs={{0,16},{16,24},{24,8},{8,0},{1,17},{17,25},{25,9},{9,1},{2,18},{18... | collective-permute-start | bytes 602120 | tf_op jit(solution)/shard_map/ppermute | solution.py:254
  5.8 0.0 copy-start.2
  5.8 1.5 %collective-permute-start = (bf16[1,128,256]{2,1,0:T(8,128)(2,1)}, bf16[1,128,256]{2,1,0:T(8,128)(2,1)S(1)}, u32[]{:S(2)}, u32[]{:S(2)}) collective-permute-start(bf16[1,128,256]{2,1,0:T(8,128)(2,1)} %get-tuple-element.27), channel_id=1, source_target_pairs={{0,2},{2,0},{4,6},{6,4},{1,3},{3,1},{5,7},{7,5},{8,10},{10,8},{12,... | collective-permute-start | bytes 196616 | tf_op jit(solution)/shard_map/ppermute | solution.py:229
  7.3 1.5 %collective-permute-start.1 = (bf16[1,128,256]{2,1,0:T(8,128)(2,1)}, bf16[1,128,256]{2,1,0:T(8,128)(2,1)S(1)}, u32[]{:S(2)}, u32[]{:S(2)}) collective-permute-start(bf16[1,128,256]{2,1,0:T(8,128)(2,1)} %get-tuple-element.27), channel_id=1, source_target_pairs={{0,4},{2,6},{4,0},{6,2},{1,5},{3,7},{5,1},{7,3},{8,12},{10,14},{12... | collective-permute-start | bytes 196616 | tf_op jit(solution)/shard_map/ppermute | solution.py:229
  8.8 0.5 %collective-permute-start.2 = (bf16[1,128,256]{2,1,0:T(8,128)(2,1)}, bf16[1,128,256]{2,1,0:T(8,128)(2,1)S(1)}, u32[]{:S(2)}, u32[]{:S(2)}) collective-permute-start(bf16[1,128,256]{2,1,0:T(8,128)(2,1)} %get-tuple-element.27), channel_id=1, source_target_pairs={{0,6},{2,4},{4,2},{6,0},{1,7},{3,5},{5,3},{7,1},{8,14},{10,12},{12... | collective-permute-start | bytes 196616 | tf_op jit(solution)/shard_map/ppermute | solution.py:229
  9.3 0.0 collective-permute-start.7
  9.3 2.2 %collective-permute-done.5.refs_2_ = bf16[784,128]{1,0:T(8,128)(2,1)S(1)} collective-permute-done((bf16[784,128]{1,0:T(8,128)(2,1)}, bf16[784,128]{1,0:T(8,128)(2,1)S(1)}, u32[]{:S(2)}, u32[]{:S(2)}) %collective-permute-start.5) | collective-permute-done | bytes 200736 | tf_op jit(solution)/shard_map/ppermute | solution.py:254
  11.5 3.3 %collective-permute-start.9 = (bf16[784,128]{1,0:T(8,128)(2,1)S(1)}, bf16[784,128]{1,0:T(8,128)(2,1)S(1)}, u32[]{:S(2)}, u32[]{:S(2)}) collective-permute-start(bf16[784,128]{1,0:T(8,128)(2,1)S(1)} %collective-permute-done.5.refs_2_), channel_id=1, source_target_pairs={{0,16},{16,24},{24,8},{8,0},{1,17},{17,25},{25,9},{9,1},{2,18},{18... | collective-permute-start | bytes 602120 | tf_op jit(solution)/shard_map/ppermute | solution.py:254
  14.8 0.0 copy-start.1
  14.8 0.0 copy-done.2
  14.8 0.7 %copy-done.1 = s32[1,2,8]{2,1,0:T(2,128)S(1)} copy-done((s32[1,2,8]{2,1,0:T(2,128)S(1)}, s32[1,2,8]{2,1,0:T(2,128)}, u32[]{:S(2)}) %copy-start.1) | copy-done | bytes 88
  15.5 0.6 %shard_map.64 = (f32[8,128]{1,0:T(8,128)S(1)}, f32[8,256]{1,0:T(8,128)S(1)}) custom-call(s32[2,8]{1,0:T(2,128)S(1)} %bitcast.11, s32[2,16]{1,0:T(2,128)S(1)} %bitcast.12), custom_call_target="tpu_custom_call" | custom-call | tf_op jit(solution)/shard_map/pallas_call | solution.py:96
  16.1 0.0 collective-permute-done
  16.1 0.0 collective-permute-done.1
  16.1 0.0 collective-permute-done.2
  16.1 0.0 copy-start
  16.1 0.9 %pad_maximum_fusion.slab_ref = bf16[4,1,128,256]{3,2,1,0:T(8,128)(2,1)S(1)} fusion(bf16[1,1,128,256]{3,2,1,0:T(8,128)(2,1)S(1)} %bitcast.18, bf16[1,1,128,256]{3,2,1,0:T(8,128)(2,1)S(1)} %bitcast.17, bf16[1,1,128,256]{3,2,1,0:T(8,128)(2,1)S(1)} %bitcast.16, bf16[1,1,128,256]{3,2,1,0:T(8,128)(2,1)} %bitcast.15), kind=kLoop, calls=%fused_computation | loop fusion | flops 393216 | bytes 524288 | tf_op jit(solution)/shard_map/stack | solution.py:249
  17.0 0.1 collective-permute-start.3
  17.1 0.0 copy-done
  17.1 0.5 %collective-permute-start.4 = (bf16[784,128]{1,0:T(8,128)(2,1)S(1)}, bf16[784,128]{1,0:T(8,128)(2,1)S(1)}, u32[]{:S(2)}, u32[]{:S(2)}) collective-permute-start(bf16[784,128]{1,0:T(8,128)(2,1)S(1)} %copy-done), channel_id=1, source_target_pairs={{0,1},{1,0},{2,3},{3,2},{4,5},{5,4},{6,7},{7,6},{8,9},{9,8},{10,11... | collective-permute-start | bytes 602120 | tf_op jit(solution)/shard_map/ppermute | solution.py:229
  17.6 0.1 collective-permute-start.6
  17.7 0.6 %collective-permute-done.7.refs_4_ = bf16[784,128]{1,0:T(8,128)(2,1)S(1)} collective-permute-done((bf16[784,128]{1,0:T(8,128)(2,1)}, bf16[784,128]{1,0:T(8,128)(2,1)S(1)}, u32[]{:S(2)}, u32[]{:S(2)}) %collective-permute-start.7) | collective-permute-done | bytes 200736 | tf_op jit(solution)/shard_map/ppermute | solution.py:254
  18.3 0.0 collective-permute-start.8
  18.3 2.4 %collective-permute-done.9.refs_0_ = bf16[784,128]{1,0:T(8,128)(2,1)S(1)} collective-permute-done((bf16[784,128]{1,0:T(8,128)(2,1)S(1)}, bf16[784,128]{1,0:T(8,128)(2,1)S(1)}, u32[]{:S(2)}, u32[]{:S(2)}) %collective-permute-start.9) | collective-permute-done | bytes 200736 | tf_op jit(solution)/shard_map/ppermute | solution.py:254
  20.7 0.0 collective-permute-start.10
  20.7 0.0 collective-permute-done.4.refs_1_
  20.7 0.0 collective-permute-done.3.twin_ref
  20.7 0.0 collective-permute-done.6.refs_3_
  20.7 0.0 collective-permute-done.8.refs_5_
  20.7 1.5 %shard_map.66 = (f32[8,128,256]{2,1,0:T(8,128)S(1)}, bf16[256,256]{1,0:T(8,128)(2,1)S(1)}) custom-call(f32[8,128]{1,0:T(8,128)S(1)} %get-tuple-element.26.chosen_ref, bf16[4,1,128,256]{3,2,1,0:T(8,128)(2,1)S(1)} %pad_maximum_fusion.slab_ref, bf16[4,1,128,256]{3,2,1,0:T(8,128)(2,1)S(1)} %collective-permute-done.3.twin_ref, bf16[784,128]{1,0:T(8,128)(2,1)S(1)} %copy-done, ...), custom_call_target="tpu_custom_call" | custom-call | tf_op jit(solution)/shard_map/pallas_call | solution.py:164
  22.2 0.0 collective-permute-done.10.refs_1_
  22.2 0.2 shard_map.67
  22.5 2.5 %collective-permute-start.11 = (bf16[2,128,256]{2,1,0:T(8,128)(2,1)S(1)}, bf16[2,128,256]{2,1,0:T(8,128)(2,1)S(1)}, u32[]{:S(2)}, u32[]{:S(2)}) collective-permute-start(bf16[2,128,256]{2,1,0:T(8,128)(2,1)S(1)} %shard_map.67), channel_id=1, source_target_pairs={{0,6},{2,4},{4,2},{6,0},{1,7},{3,5},{5,3},{7,1},{8,14},{10,12},{12... | collective-permute-start | bytes 393224 | tf_op jit(solution)/shard_map/ppermute | solution.py:229
  25.0 0.5 %shard_map.68 = (bf16[2,128,256]{2,1,0:T(8,128)(2,1)S(1)}, bf16[2,128,256]{2,1,0:T(8,128)(2,1)S(1)}, bf16[2,128,256]{2,1,0:T(8,128)(2,1)S(1)}) custom-call(f32[8,128,256]{2,1,0:T(8,128)S(1)} %get-tuple-element.32.total_ref, bf16[256,256]{1,0:T(8,128)(2,1)S(1)} %get-tuple-element.33.last_ref, f32[8,128]{1,0:T(8,128)S(1)} %get-tuple-element.26.chosen_ref, ...), custom_call_target="tpu_custom_call" | custom-call | tf_op jit(solution)/shard_map/pallas_call | solution.py:194
  25.5 0.6 %collective-permute-start.12 = (bf16[2,128,256]{2,1,0:T(8,128)(2,1)S(1)}, bf16[2,128,256]{2,1,0:T(8,128)(2,1)S(1)}, u32[]{:S(2)}, u32[]{:S(2)}) collective-permute-start(bf16[2,128,256]{2,1,0:T(8,128)(2,1)S(1)} %get-tuple-element.36), channel_id=1, source_target_pairs={{0,4},{2,6},{4,0},{6,2},{1,5},{3,7},{5,1},{7,3},{8,12},{10,14},{12... | collective-permute-start | bytes 393224 | tf_op jit(solution)/shard_map/ppermute | solution.py:229
  26.0 0.5 %collective-permute-start.13 = (bf16[2,128,256]{2,1,0:T(8,128)(2,1)S(1)}, bf16[2,128,256]{2,1,0:T(8,128)(2,1)S(1)}, u32[]{:S(2)}, u32[]{:S(2)}) collective-permute-start(bf16[2,128,256]{2,1,0:T(8,128)(2,1)S(1)} %get-tuple-element.37), channel_id=1, source_target_pairs={{0,2},{2,0},{4,6},{6,4},{1,3},{3,1},{5,7},{7,5},{8,10},{10,8},{12,... | collective-permute-start | bytes 393224 | tf_op jit(solution)/shard_map/ppermute | solution.py:229
  26.6 2.9 %collective-permute-done.11.refs_0_ = bf16[2,128,256]{2,1,0:T(8,128)(2,1)S(1)} collective-permute-done((bf16[2,128,256]{2,1,0:T(8,128)(2,1)S(1)}, bf16[2,128,256]{2,1,0:T(8,128)(2,1)S(1)}, u32[]{:S(2)}, u32[]{:S(2)}) %collective-permute-start.11) | collective-permute-done | bytes 131104 | tf_op jit(solution)/shard_map/ppermute | solution.py:229
  29.4 2.7 %collective-permute-done.12.refs_1_ = bf16[2,128,256]{2,1,0:T(8,128)(2,1)S(1)} collective-permute-done((bf16[2,128,256]{2,1,0:T(8,128)(2,1)S(1)}, bf16[2,128,256]{2,1,0:T(8,128)(2,1)S(1)}, u32[]{:S(2)}, u32[]{:S(2)}) %collective-permute-start.12) | collective-permute-done | bytes 131104 | tf_op jit(solution)/shard_map/ppermute | solution.py:229
  32.2 0.1 collective-permute-done.13.refs_2_
  32.2 0.8 %shard_map.69 = bf16[8,128,256]{2,1,0:T(8,128)(2,1)} custom-call(bf16[2,128,256]{2,1,0:T(8,128)(2,1)S(1)} %collective-permute-done.11.refs_0_, bf16[2,128,256]{2,1,0:T(8,128)(2,1)S(1)} %collective-permute-done.12.refs_1_, bf16[2,128,256]{2,1,0:T(8,128)(2,1)S(1)} %collective-permute-done.13.refs_2_, bf16[2,128,256]{2,1,0:T(8,128)(2,1)S(1)} %get-tuple-element.38.refs_3_), custom_call_target="tpu_custom_call" | custom-call | tf_op jit(solution)/shard_map/pallas_call | solution.py:218
Async XLA Ops:
  1.7 9.8 %collective-permute-start.5 = (bf16[784,128]{1,0:T(8,128)(2,1)}, bf16[784,128]{1,0:T(8,128)(2,1)S(1)}, u32[]{:S(2)}, u32[]{:S(2)}) collective-permute-start(bf16[784,128]{1,0:T(8,128)(2,1)} %get-tuple-element.31.refs_0_), channel_id=1, source_target_pairs={{0,16},{16,24},{24,8},{8,0},{1,17},{17,25},{25,9},{9,1},{2,18},{18... | collective-permute-start | bytes 602120 | tf_op jit(solution)/shard_map/ppermute | solution.py:254
  5.8 9.0 %copy-start.2 = (s32[16,2]{0,1:T(2,128)S(1)}, s32[16,2]{0,1:T(2,128)}, u32[]{:S(2)}) copy-start(s32[16,2]{0,1:T(2,128)} %param.10) | copy-start | bytes 388
  5.8 10.3 %collective-permute-start = (bf16[1,128,256]{2,1,0:T(8,128)(2,1)}, bf16[1,128,256]{2,1,0:T(8,128)(2,1)S(1)}, u32[]{:S(2)}, u32[]{:S(2)}) collective-permute-start(bf16[1,128,256]{2,1,0:T(8,128)(2,1)} %get-tuple-element.27), channel_id=1, source_target_pairs={{0,2},{2,0},{4,6},{6,4},{1,3},{3,1},{5,7},{7,5},{8,10},{10,8},{12,... | collective-permute-start | bytes 196616 | tf_op jit(solution)/shard_map/ppermute | solution.py:229
  7.3 8.8 %collective-permute-start.1 = (bf16[1,128,256]{2,1,0:T(8,128)(2,1)}, bf16[1,128,256]{2,1,0:T(8,128)(2,1)S(1)}, u32[]{:S(2)}, u32[]{:S(2)}) collective-permute-start(bf16[1,128,256]{2,1,0:T(8,128)(2,1)} %get-tuple-element.27), channel_id=1, source_target_pairs={{0,4},{2,6},{4,0},{6,2},{1,5},{3,7},{5,1},{7,3},{8,12},{10,14},{12... | collective-permute-start | bytes 196616 | tf_op jit(solution)/shard_map/ppermute | solution.py:229
  8.8 7.3 %collective-permute-start.2 = (bf16[1,128,256]{2,1,0:T(8,128)(2,1)}, bf16[1,128,256]{2,1,0:T(8,128)(2,1)S(1)}, u32[]{:S(2)}, u32[]{:S(2)}) collective-permute-start(bf16[1,128,256]{2,1,0:T(8,128)(2,1)} %get-tuple-element.27), channel_id=1, source_target_pairs={{0,6},{2,4},{4,2},{6,0},{1,7},{3,5},{5,3},{7,1},{8,14},{10,12},{12... | collective-permute-start | bytes 196616 | tf_op jit(solution)/shard_map/ppermute | solution.py:229
  9.3 9.0 %collective-permute-start.7 = (bf16[784,128]{1,0:T(8,128)(2,1)}, bf16[784,128]{1,0:T(8,128)(2,1)S(1)}, u32[]{:S(2)}, u32[]{:S(2)}) collective-permute-start(bf16[784,128]{1,0:T(8,128)(2,1)} %get-tuple-element.31.refs_0_), channel_id=1, source_target_pairs={{0,8},{16,0},{24,16},{8,24},{1,9},{17,1},{25,17},{9,25},{2,10},{18... | collective-permute-start | bytes 602120 | tf_op jit(solution)/shard_map/ppermute | solution.py:254
  11.5 9.2 %collective-permute-start.9 = (bf16[784,128]{1,0:T(8,128)(2,1)S(1)}, bf16[784,128]{1,0:T(8,128)(2,1)S(1)}, u32[]{:S(2)}, u32[]{:S(2)}) collective-permute-start(bf16[784,128]{1,0:T(8,128)(2,1)S(1)} %collective-permute-done.5.refs_2_), channel_id=1, source_target_pairs={{0,16},{16,24},{24,8},{8,0},{1,17},{17,25},{25,9},{9,1},{2,18},{18... | collective-permute-start | bytes 602120 | tf_op jit(solution)/shard_map/ppermute | solution.py:254
  14.8 0.7 %copy-start.1 = (s32[1,2,8]{2,1,0:T(2,128)S(1)}, s32[1,2,8]{2,1,0:T(2,128)}, u32[]{:S(2)}) copy-start(s32[1,2,8]{2,1,0:T(2,128)} %param.11) | copy-start | bytes 196
  16.1 1.0 %copy-start = (bf16[784,128]{1,0:T(8,128)(2,1)S(1)}, bf16[784,128]{1,0:T(8,128)(2,1)}, u32[]{:S(2)}) copy-start(bf16[784,128]{1,0:T(8,128)(2,1)} %get-tuple-element.31.refs_0_) | copy-start | bytes 602116
  17.0 3.6 %collective-permute-start.3 = (bf16[4,1,128,256]{3,2,1,0:T(8,128)(2,1)S(1)}, bf16[4,1,128,256]{3,2,1,0:T(8,128)(2,1)S(1)}, u32[]{:S(2)}, u32[]{:S(2)}) collective-permute-start(bf16[4,1,128,256]{3,2,1,0:T(8,128)(2,1)S(1)} %pad_maximum_fusion.slab_ref), channel_id=1, source_target_pairs={{0,1},{1,0},{2,3},{3,2},{4,5},{5,4},{6,7},{7,6},{8,9},{9,8},{10,11... | collective-permute-start | bytes 786440 | tf_op jit(solution)/shard_map/ppermute | solution.py:229
  17.1 3.5 %collective-permute-start.4 = (bf16[784,128]{1,0:T(8,128)(2,1)S(1)}, bf16[784,128]{1,0:T(8,128)(2,1)S(1)}, u32[]{:S(2)}, u32[]{:S(2)}) collective-permute-start(bf16[784,128]{1,0:T(8,128)(2,1)S(1)} %copy-done), channel_id=1, source_target_pairs={{0,1},{1,0},{2,3},{3,2},{4,5},{5,4},{6,7},{7,6},{8,9},{9,8},{10,11... | collective-permute-start | bytes 602120 | tf_op jit(solution)/shard_map/ppermute | solution.py:229
  17.6 3.1 %collective-permute-start.6 = (bf16[784,128]{1,0:T(8,128)(2,1)S(1)}, bf16[784,128]{1,0:T(8,128)(2,1)S(1)}, u32[]{:S(2)}, u32[]{:S(2)}) collective-permute-start(bf16[784,128]{1,0:T(8,128)(2,1)S(1)} %collective-permute-done.5.refs_2_), channel_id=1, source_target_pairs={{0,1},{1,0},{2,3},{3,2},{4,5},{5,4},{6,7},{7,6},{8,9},{9,8},{10,11... | collective-permute-start | bytes 602120 | tf_op jit(solution)/shard_map/ppermute | solution.py:229
  18.3 2.4 %collective-permute-start.8 = (bf16[784,128]{1,0:T(8,128)(2,1)S(1)}, bf16[784,128]{1,0:T(8,128)(2,1)S(1)}, u32[]{:S(2)}, u32[]{:S(2)}) collective-permute-start(bf16[784,128]{1,0:T(8,128)(2,1)S(1)} %collective-permute-done.7.refs_4_), channel_id=1, source_target_pairs={{0,1},{1,0},{2,3},{3,2},{4,5},{5,4},{6,7},{7,6},{8,9},{9,8},{10,11... | collective-permute-start | bytes 602120 | tf_op jit(solution)/shard_map/ppermute | solution.py:229
  20.7 1.6 %collective-permute-start.10 = (bf16[784,128]{1,0:T(8,128)(2,1)S(1)}, bf16[784,128]{1,0:T(8,128)(2,1)S(1)}, u32[]{:S(2)}, u32[]{:S(2)}) collective-permute-start(bf16[784,128]{1,0:T(8,128)(2,1)S(1)} %collective-permute-done.9.refs_0_), channel_id=1, source_target_pairs={{0,1},{1,0},{2,3},{3,2},{4,5},{5,4},{6,7},{7,6},{8,9},{9,8},{10,11... | collective-permute-start | bytes 602120 | tf_op jit(solution)/shard_map/ppermute | solution.py:229
  22.5 7.0 %collective-permute-start.11 = (bf16[2,128,256]{2,1,0:T(8,128)(2,1)S(1)}, bf16[2,128,256]{2,1,0:T(8,128)(2,1)S(1)}, u32[]{:S(2)}, u32[]{:S(2)}) collective-permute-start(bf16[2,128,256]{2,1,0:T(8,128)(2,1)S(1)} %shard_map.67), channel_id=1, source_target_pairs={{0,6},{2,4},{4,2},{6,0},{1,7},{3,5},{5,3},{7,1},{8,14},{10,12},{12... | collective-permute-start | bytes 393224 | tf_op jit(solution)/shard_map/ppermute | solution.py:229
  25.5 6.7 %collective-permute-start.12 = (bf16[2,128,256]{2,1,0:T(8,128)(2,1)S(1)}, bf16[2,128,256]{2,1,0:T(8,128)(2,1)S(1)}, u32[]{:S(2)}, u32[]{:S(2)}) collective-permute-start(bf16[2,128,256]{2,1,0:T(8,128)(2,1)S(1)} %get-tuple-element.36), channel_id=1, source_target_pairs={{0,4},{2,6},{4,0},{6,2},{1,5},{3,7},{5,1},{7,3},{8,12},{10,14},{12... | collective-permute-start | bytes 393224 | tf_op jit(solution)/shard_map/ppermute | solution.py:229
  26.0 6.2 %collective-permute-start.13 = (bf16[2,128,256]{2,1,0:T(8,128)(2,1)S(1)}, bf16[2,128,256]{2,1,0:T(8,128)(2,1)S(1)}, u32[]{:S(2)}, u32[]{:S(2)}) collective-permute-start(bf16[2,128,256]{2,1,0:T(8,128)(2,1)S(1)} %get-tuple-element.37), channel_id=1, source_target_pairs={{0,2},{2,0},{4,6},{6,4},{1,3},{3,1},{5,7},{7,5},{8,10},{10,8},{12,... | collective-permute-start | bytes 393224 | tf_op jit(solution)/shard_map/ppermute | solution.py:229

commit v6 on v5

--- a/solution.py
+++ b/solution.py
@@ -254,7 +254,7 @@
         held[turn] = lax.ppermute(
             held[turn - step], "row", [(name, ring[(at + step) % row_count]) for at, name in enumerate(ring)]
         )
-    split = row_count - 1
+    split = row_count - 2
     pieces = [one for turn in turns for one in (held[turn], swap(held[turn], "layer", 1))]
     steps = split * layer_count
     totals = early(slot_count, len(pieces) - steps, chosen, slabs, twins, pieces[:steps])

time: 33.2 us -> 32.9 us (level)
  waiting for transfers between devices: 10.8 us -> 10.4 us
    pallas_call x2, Pallas kernels: 0.72 us -> 1.28 us  [late(): pl.pallas_call(functools.partial(late_kernel, slot_count, col_count, chip...]
    pallas_call x1, Pallas kernels: 1.53 us -> 1.1 us  [early(): pl.pallas_call(functools.partial(early_kernel, slot_count), out_shape=(ja...]
    ppermute x11, waiting for transfers between devices: 5.67 us -> 5.25 us  [swap(): lax.ppermute(value, axis, [(i, i ^ by) for i in range(lax.axis_size(axis))])]
  transfers between devices with their start and end apart: 14 -> 14, of which waited for: 6 -> 7; matrix products, arithmetic and copies ran while one was open for 3% -> 3% of each run, Pallas kernels for 8% -> 8%
where the time goes in v6:
time: 32.9 us; the launch traced here: 32.7 us
  starting transfers between devices  15.1 us (46%)
  waiting for transfers between devices  10.4 us (32%)
  Pallas kernels  5.49 us (17%)
  other arithmetic  0.91 us (3%)
  local copies, waits for them, and re-layouts  0.69 us (2%)
    ppermute x11, starting transfers between devices, swap(): lax.ppermute(value, axis, [(i, i ^ by) for i in range(lax.axis_size(axis))])  7.75 us
    ppermute x3, starting transfers between devices, shards(): lax.ppermute(held[turn - step], 'row', [(name, ring[(at + step) % row_cou...  7.37 us
    ppermute x11, waiting for transfers between devices, swap(): lax.ppermute(value, axis, [(i, i ^ by) for i in range(lax.axis_size(axis))])  5.25 us
    ppermute x3, waiting for transfers between devices, shards(): lax.ppermute(held[turn - step], 'row', [(name, ring[(at + step) % row_cou...  5.17 us
    pallas_call x1, Pallas kernels, prepare(): pl.pallas_call(prepare_kernel, out_shape=(jax.ShapeDtypeStruct((rows + TA...  1.7 us
    pallas_call x2, Pallas kernels, late(): pl.pallas_call(functools.partial(late_kernel, slot_count, col_count, chip...  1.28 us
    pallas_call x1, Pallas kernels, early(): pl.pallas_call(functools.partial(early_kernel, slot_count), out_shape=(ja...  1.1 us
    another operation x1, other arithmetic, shards(): slabs = jnp.stack(slabs)  0.91 us
  transfers between devices with their start and end apart: 14, of which 7 were waited for; matrix products, arithmetic and copies ran while one was open for 3% of the time, Pallas kernels for 8%

profile of v6, /device:TPU:0, one launch (start us, length us, event | category | flops | bytes accessed | tf_op | source)
XLA Modules:
  0.0 32.7 jit_solution(8737241491920625003)
XLA Ops:
  0.0 1.7 %shard_map.65 = (bf16[784,128]{1,0:T(8,128)(2,1)}, bf16[1,128,256]{2,1,0:T(8,128)(2,1)}) custom-call(bf16[768,128]{1,0:T(8,128)(2,1)} %bitcast.13, s32[1,6]{1,0:T(1,128)} %bitcast.19, bf16[1,128,256]{2,1,0:T(8,128)(2,1)} %bitcast.14, s32[1,2]{1,0:T(1,128)} %bitcast.20), custom_call_target="tpu_custom_call" | custom-call | tf_op jit(solution)/shard_map/pallas_call | solution.py:59
  1.7 4.1 %collective-permute-start.5 = (bf16[784,128]{1,0:T(8,128)(2,1)}, bf16[784,128]{1,0:T(8,128)(2,1)S(1)}, u32[]{:S(2)}, u32[]{:S(2)}) collective-permute-start(bf16[784,128]{1,0:T(8,128)(2,1)} %get-tuple-element.31.refs_0_), channel_id=1, source_target_pairs={{0,16},{16,24},{24,8},{8,0},{1,17},{17,25},{25,9},{9,1},{2,18},{18... | collective-permute-start | bytes 602120 | tf_op jit(solution)/shard_map/ppermute | solution.py:254
  5.8 0.0 copy-start.2
  5.8 1.5 %collective-permute-start = (bf16[1,128,256]{2,1,0:T(8,128)(2,1)}, bf16[1,128,256]{2,1,0:T(8,128)(2,1)S(1)}, u32[]{:S(2)}, u32[]{:S(2)}) collective-permute-start(bf16[1,128,256]{2,1,0:T(8,128)(2,1)} %get-tuple-element.27), channel_id=1, source_target_pairs={{0,2},{2,0},{4,6},{6,4},{1,3},{3,1},{5,7},{7,5},{8,10},{10,8},{12,... | collective-permute-start | bytes 196616 | tf_op jit(solution)/shard_map/ppermute | solution.py:229
  7.3 1.5 %collective-permute-start.1 = (bf16[1,128,256]{2,1,0:T(8,128)(2,1)}, bf16[1,128,256]{2,1,0:T(8,128)(2,1)S(1)}, u32[]{:S(2)}, u32[]{:S(2)}) collective-permute-start(bf16[1,128,256]{2,1,0:T(8,128)(2,1)} %get-tuple-element.27), channel_id=1, source_target_pairs={{0,4},{2,6},{4,0},{6,2},{1,5},{3,7},{5,1},{7,3},{8,12},{10,14},{12... | collective-permute-start | bytes 196616 | tf_op jit(solution)/shard_map/ppermute | solution.py:229
  8.8 0.5 %collective-permute-start.2 = (bf16[1,128,256]{2,1,0:T(8,128)(2,1)}, bf16[1,128,256]{2,1,0:T(8,128)(2,1)S(1)}, u32[]{:S(2)}, u32[]{:S(2)}) collective-permute-start(bf16[1,128,256]{2,1,0:T(8,128)(2,1)} %get-tuple-element.27), channel_id=1, source_target_pairs={{0,6},{2,4},{4,2},{6,0},{1,7},{3,5},{5,3},{7,1},{8,14},{10,12},{12... | collective-permute-start | bytes 196616 | tf_op jit(solution)/shard_map/ppermute | solution.py:229
  9.3 0.0 collective-permute-start.7
  9.3 2.2 %collective-permute-done.5.refs_2_ = bf16[784,128]{1,0:T(8,128)(2,1)S(1)} collective-permute-done((bf16[784,128]{1,0:T(8,128)(2,1)}, bf16[784,128]{1,0:T(8,128)(2,1)S(1)}, u32[]{:S(2)}, u32[]{:S(2)}) %collective-permute-start.5) | collective-permute-done | bytes 200736 | tf_op jit(solution)/shard_map/ppermute | solution.py:254
  11.5 3.3 %collective-permute-start.9 = (bf16[784,128]{1,0:T(8,128)(2,1)S(1)}, bf16[784,128]{1,0:T(8,128)(2,1)S(1)}, u32[]{:S(2)}, u32[]{:S(2)}) collective-permute-start(bf16[784,128]{1,0:T(8,128)(2,1)S(1)} %collective-permute-done.5.refs_2_), channel_id=1, source_target_pairs={{0,16},{16,24},{24,8},{8,0},{1,17},{17,25},{25,9},{9,1},{2,18},{18... | collective-permute-start | bytes 602120 | tf_op jit(solution)/shard_map/ppermute | solution.py:254
  14.8 0.0 copy-start.1
  14.8 0.0 copy-done.2
  14.8 0.7 %copy-done.1 = s32[1,2,8]{2,1,0:T(2,128)S(1)} copy-done((s32[1,2,8]{2,1,0:T(2,128)S(1)}, s32[1,2,8]{2,1,0:T(2,128)}, u32[]{:S(2)}) %copy-start.1) | copy-done | bytes 88
  15.5 0.6 %shard_map.64 = (f32[8,128]{1,0:T(8,128)S(1)}, f32[8,256]{1,0:T(8,128)S(1)}) custom-call(s32[2,8]{1,0:T(2,128)S(1)} %bitcast.11, s32[2,16]{1,0:T(2,128)S(1)} %bitcast.12), custom_call_target="tpu_custom_call" | custom-call | tf_op jit(solution)/shard_map/pallas_call | solution.py:96
  16.1 0.0 collective-permute-done
  16.1 0.0 collective-permute-done.1
  16.1 0.0 collective-permute-done.2
  16.1 0.0 copy-start
  16.1 0.9 %pad_maximum_fusion.slab_ref = bf16[4,1,128,256]{3,2,1,0:T(8,128)(2,1)S(1)} fusion(bf16[1,1,128,256]{3,2,1,0:T(8,128)(2,1)S(1)} %bitcast.18, bf16[1,1,128,256]{3,2,1,0:T(8,128)(2,1)S(1)} %bitcast.17, bf16[1,1,128,256]{3,2,1,0:T(8,128)(2,1)S(1)} %bitcast.16, bf16[1,1,128,256]{3,2,1,0:T(8,128)(2,1)} %bitcast.15), kind=kLoop, calls=%fused_computation | loop fusion | flops 393216 | bytes 524288 | tf_op jit(solution)/shard_map/stack | solution.py:249
  17.0 0.1 collective-permute-start.3
  17.1 0.0 copy-done
  17.1 0.5 %collective-permute-start.4 = (bf16[784,128]{1,0:T(8,128)(2,1)S(1)}, bf16[784,128]{1,0:T(8,128)(2,1)S(1)}, u32[]{:S(2)}, u32[]{:S(2)}) collective-permute-start(bf16[784,128]{1,0:T(8,128)(2,1)S(1)} %copy-done), channel_id=1, source_target_pairs={{0,1},{1,0},{2,3},{3,2},{4,5},{5,4},{6,7},{7,6},{8,9},{9,8},{10,11... | collective-permute-start | bytes 602120 | tf_op jit(solution)/shard_map/ppermute | solution.py:229
  17.6 0.1 collective-permute-start.6
  17.7 0.6 %collective-permute-done.7.refs_0_ = bf16[784,128]{1,0:T(8,128)(2,1)S(1)} collective-permute-done((bf16[784,128]{1,0:T(8,128)(2,1)}, bf16[784,128]{1,0:T(8,128)(2,1)S(1)}, u32[]{:S(2)}, u32[]{:S(2)}) %collective-permute-start.7) | collective-permute-done | bytes 200736 | tf_op jit(solution)/shard_map/ppermute | solution.py:254
  18.3 0.0 collective-permute-start.8
  18.3 2.4 %collective-permute-done.9.refs_2_ = bf16[784,128]{1,0:T(8,128)(2,1)S(1)} collective-permute-done((bf16[784,128]{1,0:T(8,128)(2,1)S(1)}, bf16[784,128]{1,0:T(8,128)(2,1)S(1)}, u32[]{:S(2)}, u32[]{:S(2)}) %collective-permute-start.9) | collective-permute-done | bytes 200736 | tf_op jit(solution)/shard_map/ppermute | solution.py:254
  20.7 0.0 collective-permute-start.10
  20.7 0.0 collective-permute-done.4.refs_1_
  20.7 0.0 collective-permute-done.3.twin_ref
  20.7 0.0 collective-permute-done.6.refs_3_
  20.7 1.1 %shard_map.66 = (f32[8,128,256]{2,1,0:T(8,128)S(1)}, bf16[512,256]{1,0:T(8,128)(2,1)S(1)}) custom-call(f32[8,128]{1,0:T(8,128)S(1)} %get-tuple-element.26.chosen_ref, bf16[4,1,128,256]{3,2,1,0:T(8,128)(2,1)S(1)} %pad_maximum_fusion.slab_ref, bf16[4,1,128,256]{3,2,1,0:T(8,128)(2,1)S(1)} %collective-permute-done.3.twin_ref, bf16[784,128]{1,0:T(8,128)(2,1)S(1)} %copy-done, ...), custom_call_target="tpu_custom_call" | custom-call | tf_op jit(solution)/shard_map/pallas_call | solution.py:164
  21.8 0.0 collective-permute-done.8.refs_1_
  21.8 0.3 collective-permute-done.10.refs_3_
  22.1 0.4 %shard_map.67 = bf16[2,128,256]{2,1,0:T(8,128)(2,1)S(1)} custom-call(f32[8,128,256]{2,1,0:T(8,128)S(1)} %get-tuple-element.32.total_ref, bf16[512,256]{1,0:T(8,128)(2,1)S(1)} %get-tuple-element.33.last_ref, f32[8,128]{1,0:T(8,128)S(1)} %get-tuple-element.26.chosen_ref, f32[8,256]{1,0:T(8,128)S(1)} %get-tuple-element.35.kept_ref, ...), custom_call_target="tpu_custom_call" | custom-call | tf_op jit(solution)/shard_map/pallas_call | solution.py:194
  22.5 2.5 %collective-permute-start.11 = (bf16[2,128,256]{2,1,0:T(8,128)(2,1)S(1)}, bf16[2,128,256]{2,1,0:T(8,128)(2,1)S(1)}, u32[]{:S(2)}, u32[]{:S(2)}) collective-permute-start(bf16[2,128,256]{2,1,0:T(8,128)(2,1)S(1)} %shard_map.67), channel_id=1, source_target_pairs={{0,6},{2,4},{4,2},{6,0},{1,7},{3,5},{5,3},{7,1},{8,14},{10,12},{12... | collective-permute-start | bytes 393224 | tf_op jit(solution)/shard_map/ppermute | solution.py:229
  25.0 0.9 %shard_map.68 = (bf16[2,128,256]{2,1,0:T(8,128)(2,1)S(1)}, bf16[2,128,256]{2,1,0:T(8,128)(2,1)S(1)}, bf16[2,128,256]{2,1,0:T(8,128)(2,1)S(1)}) custom-call(f32[8,128,256]{2,1,0:T(8,128)S(1)} %get-tuple-element.32.total_ref, bf16[512,256]{1,0:T(8,128)(2,1)S(1)} %get-tuple-element.33.last_ref, f32[8,128]{1,0:T(8,128)S(1)} %get-tuple-element.26.chosen_ref, ...), custom_call_target="tpu_custom_call" | custom-call | tf_op jit(solution)/shard_map/pallas_call | solution.py:194
  25.9 0.6 %collective-permute-start.12 = (bf16[2,128,256]{2,1,0:T(8,128)(2,1)S(1)}, bf16[2,128,256]{2,1,0:T(8,128)(2,1)S(1)}, u32[]{:S(2)}, u32[]{:S(2)}) collective-permute-start(bf16[2,128,256]{2,1,0:T(8,128)(2,1)S(1)} %get-tuple-element.36), channel_id=1, source_target_pairs={{0,4},{2,6},{4,0},{6,2},{1,5},{3,7},{5,1},{7,3},{8,12},{10,14},{12... | collective-permute-start | bytes 393224 | tf_op jit(solution)/shard_map/ppermute | solution.py:229
  26.5 0.5 %collective-permute-start.13 = (bf16[2,128,256]{2,1,0:T(8,128)(2,1)S(1)}, bf16[2,128,256]{2,1,0:T(8,128)(2,1)S(1)}, u32[]{:S(2)}, u32[]{:S(2)}) collective-permute-start(bf16[2,128,256]{2,1,0:T(8,128)(2,1)S(1)} %get-tuple-element.37), channel_id=1, source_target_pairs={{0,2},{2,0},{4,6},{6,4},{1,3},{3,1},{5,7},{7,5},{8,10},{10,8},{12,... | collective-permute-start | bytes 393224 | tf_op jit(solution)/shard_map/ppermute | solution.py:229
  27.0 2.1 %collective-permute-done.11.refs_0_ = bf16[2,128,256]{2,1,0:T(8,128)(2,1)S(1)} collective-permute-done((bf16[2,128,256]{2,1,0:T(8,128)(2,1)S(1)}, bf16[2,128,256]{2,1,0:T(8,128)(2,1)S(1)}, u32[]{:S(2)}, u32[]{:S(2)}) %collective-permute-start.11) | collective-permute-done | bytes 131104 | tf_op jit(solution)/shard_map/ppermute | solution.py:229
  29.1 2.7 %collective-permute-done.12.refs_1_ = bf16[2,128,256]{2,1,0:T(8,128)(2,1)S(1)} collective-permute-done((bf16[2,128,256]{2,1,0:T(8,128)(2,1)S(1)}, bf16[2,128,256]{2,1,0:T(8,128)(2,1)S(1)}, u32[]{:S(2)}, u32[]{:S(2)}) %collective-permute-start.12) | collective-permute-done | bytes 131104 | tf_op jit(solution)/shard_map/ppermute | solution.py:229
  31.9 0.1 collective-permute-done.13.refs_2_
  31.9 0.8 %shard_map.69 = bf16[8,128,256]{2,1,0:T(8,128)(2,1)} custom-call(bf16[2,128,256]{2,1,0:T(8,128)(2,1)S(1)} %collective-permute-done.11.refs_0_, bf16[2,128,256]{2,1,0:T(8,128)(2,1)S(1)} %collective-permute-done.12.refs_1_, bf16[2,128,256]{2,1,0:T(8,128)(2,1)S(1)} %collective-permute-done.13.refs_2_, bf16[2,128,256]{2,1,0:T(8,128)(2,1)S(1)} %get-tuple-element.38.refs_3_), custom_call_target="tpu_custom_call" | custom-call | tf_op jit(solution)/shard_map/pallas_call | solution.py:218
Async XLA Ops:
  1.7 9.8 %collective-permute-start.5 = (bf16[784,128]{1,0:T(8,128)(2,1)}, bf16[784,128]{1,0:T(8,128)(2,1)S(1)}, u32[]{:S(2)}, u32[]{:S(2)}) collective-permute-start(bf16[784,128]{1,0:T(8,128)(2,1)} %get-tuple-element.31.refs_0_), channel_id=1, source_target_pairs={{0,16},{16,24},{24,8},{8,0},{1,17},{17,25},{25,9},{9,1},{2,18},{18... | collective-permute-start | bytes 602120 | tf_op jit(solution)/shard_map/ppermute | solution.py:254
  5.8 9.0 %copy-start.2 = (s32[16,2]{0,1:T(2,128)S(1)}, s32[16,2]{0,1:T(2,128)}, u32[]{:S(2)}) copy-start(s32[16,2]{0,1:T(2,128)} %param.10) | copy-start | bytes 388
  5.8 10.3 %collective-permute-start = (bf16[1,128,256]{2,1,0:T(8,128)(2,1)}, bf16[1,128,256]{2,1,0:T(8,128)(2,1)S(1)}, u32[]{:S(2)}, u32[]{:S(2)}) collective-permute-start(bf16[1,128,256]{2,1,0:T(8,128)(2,1)} %get-tuple-element.27), channel_id=1, source_target_pairs={{0,2},{2,0},{4,6},{6,4},{1,3},{3,1},{5,7},{7,5},{8,10},{10,8},{12,... | collective-permute-start | bytes 196616 | tf_op jit(solution)/shard_map/ppermute | solution.py:229
  7.3 8.8 %collective-permute-start.1 = (bf16[1,128,256]{2,1,0:T(8,128)(2,1)}, bf16[1,128,256]{2,1,0:T(8,128)(2,1)S(1)}, u32[]{:S(2)}, u32[]{:S(2)}) collective-permute-start(bf16[1,128,256]{2,1,0:T(8,128)(2,1)} %get-tuple-element.27), channel_id=1, source_target_pairs={{0,4},{2,6},{4,0},{6,2},{1,5},{3,7},{5,1},{7,3},{8,12},{10,14},{12... | collective-permute-start | bytes 196616 | tf_op jit(solution)/shard_map/ppermute | solution.py:229
  8.8 7.3 %collective-permute-start.2 = (bf16[1,128,256]{2,1,0:T(8,128)(2,1)}, bf16[1,128,256]{2,1,0:T(8,128)(2,1)S(1)}, u32[]{:S(2)}, u32[]{:S(2)}) collective-permute-start(bf16[1,128,256]{2,1,0:T(8,128)(2,1)} %get-tuple-element.27), channel_id=1, source_target_pairs={{0,6},{2,4},{4,2},{6,0},{1,7},{3,5},{5,3},{7,1},{8,14},{10,12},{12... | collective-permute-start | bytes 196616 | tf_op jit(solution)/shard_map/ppermute | solution.py:229
  9.3 9.0 %collective-permute-start.7 = (bf16[784,128]{1,0:T(8,128)(2,1)}, bf16[784,128]{1,0:T(8,128)(2,1)S(1)}, u32[]{:S(2)}, u32[]{:S(2)}) collective-permute-start(bf16[784,128]{1,0:T(8,128)(2,1)} %get-tuple-element.31.refs_0_), channel_id=1, source_target_pairs={{0,8},{16,0},{24,16},{8,24},{1,9},{17,1},{25,17},{9,25},{2,10},{18... | collective-permute-start | bytes 602120 | tf_op jit(solution)/shard_map/ppermute | solution.py:254
  11.5 9.2 %collective-permute-start.9 = (bf16[784,128]{1,0:T(8,128)(2,1)S(1)}, bf16[784,128]{1,0:T(8,128)(2,1)S(1)}, u32[]{:S(2)}, u32[]{:S(2)}) collective-permute-start(bf16[784,128]{1,0:T(8,128)(2,1)S(1)} %collective-permute-done.5.refs_2_), channel_id=1, source_target_pairs={{0,16},{16,24},{24,8},{8,0},{1,17},{17,25},{25,9},{9,1},{2,18},{18... | collective-permute-start | bytes 602120 | tf_op jit(solution)/shard_map/ppermute | solution.py:254
  14.8 0.7 %copy-start.1 = (s32[1,2,8]{2,1,0:T(2,128)S(1)}, s32[1,2,8]{2,1,0:T(2,128)}, u32[]{:S(2)}) copy-start(s32[1,2,8]{2,1,0:T(2,128)} %param.11) | copy-start | bytes 196
  16.1 1.0 %copy-start = (bf16[784,128]{1,0:T(8,128)(2,1)S(1)}, bf16[784,128]{1,0:T(8,128)(2,1)}, u32[]{:S(2)}) copy-start(bf16[784,128]{1,0:T(8,128)(2,1)} %get-tuple-element.31.refs_0_) | copy-start | bytes 602116
  17.0 3.6 %collective-permute-start.3 = (bf16[4,1,128,256]{3,2,1,0:T(8,128)(2,1)S(1)}, bf16[4,1,128,256]{3,2,1,0:T(8,128)(2,1)S(1)}, u32[]{:S(2)}, u32[]{:S(2)}) collective-permute-start(bf16[4,1,128,256]{3,2,1,0:T(8,128)(2,1)S(1)} %pad_maximum_fusion.slab_ref), channel_id=1, source_target_pairs={{0,1},{1,0},{2,3},{3,2},{4,5},{5,4},{6,7},{7,6},{8,9},{9,8},{10,11... | collective-permute-start | bytes 786440 | tf_op jit(solution)/shard_map/ppermute | solution.py:229
  17.1 3.5 %collective-permute-start.4 = (bf16[784,128]{1,0:T(8,128)(2,1)S(1)}, bf16[784,128]{1,0:T(8,128)(2,1)S(1)}, u32[]{:S(2)}, u32[]{:S(2)}) collective-permute-start(bf16[784,128]{1,0:T(8,128)(2,1)S(1)} %copy-done), channel_id=1, source_target_pairs={{0,1},{1,0},{2,3},{3,2},{4,5},{5,4},{6,7},{7,6},{8,9},{9,8},{10,11... | collective-permute-start | bytes 602120 | tf_op jit(solution)/shard_map/ppermute | solution.py:229
  17.6 3.1 %collective-permute-start.6 = (bf16[784,128]{1,0:T(8,128)(2,1)S(1)}, bf16[784,128]{1,0:T(8,128)(2,1)S(1)}, u32[]{:S(2)}, u32[]{:S(2)}) collective-permute-start(bf16[784,128]{1,0:T(8,128)(2,1)S(1)} %collective-permute-done.5.refs_2_), channel_id=1, source_target_pairs={{0,1},{1,0},{2,3},{3,2},{4,5},{5,4},{6,7},{7,6},{8,9},{9,8},{10,11... | collective-permute-start | bytes 602120 | tf_op jit(solution)/shard_map/ppermute | solution.py:229
  18.3 3.5 %collective-permute-start.8 = (bf16[784,128]{1,0:T(8,128)(2,1)S(1)}, bf16[784,128]{1,0:T(8,128)(2,1)S(1)}, u32[]{:S(2)}, u32[]{:S(2)}) collective-permute-start(bf16[784,128]{1,0:T(8,128)(2,1)S(1)} %collective-permute-done.7.refs_0_), channel_id=1, source_target_pairs={{0,1},{1,0},{2,3},{3,2},{4,5},{5,4},{6,7},{7,6},{8,9},{9,8},{10,11... | collective-permute-start | bytes 602120 | tf_op jit(solution)/shard_map/ppermute | solution.py:229
  20.7 1.4 %collective-permute-start.10 = (bf16[784,128]{1,0:T(8,128)(2,1)S(1)}, bf16[784,128]{1,0:T(8,128)(2,1)S(1)}, u32[]{:S(2)}, u32[]{:S(2)}) collective-permute-start(bf16[784,128]{1,0:T(8,128)(2,1)S(1)} %collective-permute-done.9.refs_2_), channel_id=1, source_target_pairs={{0,1},{1,0},{2,3},{3,2},{4,5},{5,4},{6,7},{7,6},{8,9},{9,8},{10,11... | collective-permute-start | bytes 602120 | tf_op jit(solution)/shard_map/ppermute | solution.py:229
  22.5 6.6 %collective-permute-start.11 = (bf16[2,128,256]{2,1,0:T(8,128)(2,1)S(1)}, bf16[2,128,256]{2,1,0:T(8,128)(2,1)S(1)}, u32[]{:S(2)}, u32[]{:S(2)}) collective-permute-start(bf16[2,128,256]{2,1,0:T(8,128)(2,1)S(1)} %shard_map.67), channel_id=1, source_target_pairs={{0,6},{2,4},{4,2},{6,0},{1,7},{3,5},{5,3},{7,1},{8,14},{10,12},{12... | collective-permute-start | bytes 393224 | tf_op jit(solution)/shard_map/ppermute | solution.py:229
  25.9 6.0 %collective-permute-start.12 = (bf16[2,128,256]{2,1,0:T(8,128)(2,1)S(1)}, bf16[2,128,256]{2,1,0:T(8,128)(2,1)S(1)}, u32[]{:S(2)}, u32[]{:S(2)}) collective-permute-start(bf16[2,128,256]{2,1,0:T(8,128)(2,1)S(1)} %get-tuple-element.36), channel_id=1, source_target_pairs={{0,4},{2,6},{4,0},{6,2},{1,5},{3,7},{5,1},{7,3},{8,12},{10,14},{12... | collective-permute-start | bytes 393224 | tf_op jit(solution)/shard_map/ppermute | solution.py:229
  26.5 5.5 %collective-permute-start.13 = (bf16[2,128,256]{2,1,0:T(8,128)(2,1)S(1)}, bf16[2,128,256]{2,1,0:T(8,128)(2,1)S(1)}, u32[]{:S(2)}, u32[]{:S(2)}) collective-permute-start(bf16[2,128,256]{2,1,0:T(8,128)(2,1)S(1)} %get-tuple-element.37), channel_id=1, source_target_pairs={{0,2},{2,0},{4,6},{6,4},{1,3},{3,1},{5,7},{7,5},{8,10},{10,8},{12,... | collective-permute-start | bytes 393224 | tf_op jit(solution)/shard_map/ppermute | solution.py:229
